TPU v7x, 128 devices: a whole 4x4x4 slice. The times are simulated.
128 devices in a mesh: ra: 8 (over x, core), dec: 16 (over z, y).
Axes of the slice: x: 4, y: 4, z: 4, core: 2. Of those that a mesh axis runs over, the one named last changes fastest.
Arguments:
- model: float32 [6, 2048, 4096], P(None, 'ra', 'dec'), may hold values from -6 to 6
- observed: float32 [4096, 4356], P(('ra', 'dec')), may hold values from -6 to 6
- inv_var: float32 [4096, 4356], P(('ra', 'dec')), may hold values from 0.1 to 10
- psf: float32 [4096, 3969], P(('ra', 'dec')), may hold values from -0.09375 to 0.09375
- target_dec: int32 [4096, 1], P('ra'), may hold values from 0 to 15; in each aligned block of 32 rows (0 to 31, 32 to 63, ...) at most 4 rows name the same one
- band: int32 [4096], P('ra'), may hold values from 0 to 5
- offset_ra: int32 [4096], P('ra'), may hold values from 0 to 252
- offset_dec: int32 [4096], P('ra'), may hold values from 0 to 252
Outputs:
- residual: float32 [4096, 4356], P(('ra', 'dec'))
- gradient: float32 [6, 2048, 4096], P(None, 'ra', 'dec')
Inputs may be any that keep to these rules, and one draw needn't show every extreme that they name: `target_dec`: among the 32 exposures of one visit owner (aligned blocks of 32 rows), no declination index is named more than 4 times, and one is named exactly 4 times.
All inputs are finite; a program needn't handle non-finite values.
Results may differ from a plain program's by a relative error of at most 0.00012.
Values sent between devices are 32-bit elements; how exact they have to be, the bound alone decides.
A program may use at most 128 MiB of HBM per device.

v0:
```python
import math

import jax
import jax.numpy as jnp
from jax import lax
from jax.sharding import PartitionSpec as P

K = 63
C = 66
CAP = 4
P_SIZE = 128
H = 62


def with_halo(block, sides, width):
    for axis, dim in sides:
        count = lax.axis_size(axis)
        forward = [(i, i + 1) for i in range(count - 1)]
        backward = [(target, source) for source, target in forward]
        low = lax.ppermute(
            lax.slice_in_dim(block, block.shape[dim] - width, None, axis=dim), axis, forward
        )
        high = lax.ppermute(lax.slice_in_dim(block, 0, width, axis=dim), axis, backward)
        block = jnp.concatenate([low, block, high], axis=dim)
    return block


def dft_tables(length):
    index = jnp.arange(length, dtype=jnp.int32)
    phase = (index[:, None] * index[None, :] % length).astype(jnp.float32) * (
        2.0 * math.pi / length
    )
    return (jnp.cos(phase), jnp.sin(phase))


def on_left(table, images):
    return jnp.einsum("jk,mkl->mjl", table, images, precision=lax.Precision.HIGHEST)


def on_right(images, table):
    return jnp.einsum("mjk,kl->mjl", images, table, precision=lax.Precision.HIGHEST)


def forward_dft(images, cosine, sine):
    upper_re = on_right(images, cosine)
    upper_im = -on_right(images, sine)
    result_re = on_left(cosine, upper_re) + on_left(sine, upper_im)
    result_im = on_left(cosine, upper_im) - on_left(sine, upper_re)
    return (result_re, result_im)


def inverse_real(spec_re, spec_im, cosine, sine):
    length = cosine.shape[0]
    inner_re = on_right(spec_re, cosine) - on_right(spec_im, sine)
    inner_im = on_right(spec_re, sine) + on_right(spec_im, cosine)
    return (on_left(cosine, inner_re) - on_left(sine, inner_im)) / float(length * length)


def model_and_adjoint(patches, kernels, seen, weights):
    number = patches.shape[0]
    cosine, sine = dft_tables(P_SIZE)
    kernel_pad = jnp.pad(kernels.reshape(number, K, K), ((0, 0), (0, P_SIZE - K), (0, P_SIZE - K)))
    patch_re, patch_im = forward_dft(patches, cosine, sine)
    kern_re, kern_im = forward_dft(kernel_pad, cosine, sine)
    whole = inverse_real(
        patch_re * kern_re - patch_im * kern_im,
        patch_re * kern_im + patch_im * kern_re,
        cosine,
        sine,
    )
    predicted = whole[:, K - 1 :, K - 1 :]
    resid = weights.reshape(number, C, C) * (predicted - seen.reshape(number, C, C))
    resid_pad = jnp.pad(resid, ((0, 0), (K - 1, 0), (K - 1, 0)))
    res_re, res_im = forward_dft(resid_pad, cosine, sine)
    back = inverse_real(
        res_re * kern_re + res_im * kern_im, res_im * kern_re - res_re * kern_im, cosine, sine
    )
    return (resid.reshape(number, C * C), back)


def column_table(first_dec, width):
    columns = jnp.arange(width, dtype=jnp.int32)
    inside = jnp.arange(P_SIZE, dtype=jnp.int32)
    wanted = first_dec[:, None, None] + inside[None, None, :]
    return (columns[None, :, None] == wanted).astype(jnp.float32)


def cut_patches(extended, bands, first_ra, table):
    width = extended.shape[2]

    def single(which, row_start):
        return lax.dynamic_slice(extended, (which, row_start, 0), (1, P_SIZE, width))[0]

    slabs = jax.vmap(single)(bands, first_ra)
    return jnp.einsum("sjc,scl->sjl", slabs, table, precision=lax.Precision.HIGHEST)


def add_patches(gradpad, patches, bands, first_ra, table):
    width = gradpad.shape[2]
    spread = jnp.einsum("sjl,scl->sjc", patches, table, precision=lax.Precision.HIGHEST)

    def accumulate(position, total):
        which = bands[position]
        row_start = first_ra[position]
        current = lax.dynamic_slice(total, (which, row_start, 0), (1, P_SIZE, width))
        return lax.dynamic_update_slice(
            total, current + spread[position][None], (which, row_start, 0)
        )

    return lax.fori_loop(0, patches.shape[0], accumulate, gradpad)


def fold_axis(wide, axis, inner, width):
    center = lax.slice_in_dim(wide, 2 * width, 2 * width + inner, axis=axis)
    lower = lax.slice_in_dim(wide, 0, width, axis=axis)
    upper = lax.slice_in_dim(wide, inner + 3 * width, inner + 4 * width, axis=axis)
    low_widths = [(0, 0)] * wide.ndim
    low_widths[axis] = (0, inner - width)
    high_widths = [(0, 0)] * wide.ndim
    high_widths[axis] = (inner - width, 0)
    return center + jnp.pad(lower, low_widths) + jnp.pad(upper, high_widths)


def slot_tables(targets, n_dec, e_dev):
    same = targets[:, :, None] == targets[:, None, :]
    order = jnp.arange(e_dev, dtype=jnp.int32)
    earlier = order[None, :] < order[:, None]
    ranks = jnp.sum(jnp.logical_and(same, earlier[None]), axis=2)
    tile_ids = jnp.arange(n_dec, dtype=jnp.int32)
    slot_ids = jnp.arange(CAP, dtype=jnp.int32)
    hits = jnp.logical_and(
        targets[:, None, None, :] == tile_ids[None, :, None, None],
        ranks[:, None, None, :] == slot_ids[None, None, :, None],
    )
    source = jnp.sum(hits.astype(jnp.int32) * order, axis=3)
    filled = jnp.any(hits, axis=3)
    return (ranks, source, filled)


def body(model, observed, inv_var, psf, target_dec, band, offset_ra, offset_dec):
    n_dec = lax.axis_size("dec")
    own_dec = lax.axis_index("dec")
    e_dev = observed.shape[0]
    tile_ra = model.shape[1]
    tile_dec = model.shape[2]
    targets = target_dec[:, 0].reshape(n_dec, e_dev)
    ranks, source, filled = slot_tables(targets, n_dec, e_dev)
    own_targets = lax.dynamic_index_in_dim(targets, own_dec, 0, keepdims=False)
    own_ranks = lax.dynamic_index_in_dim(ranks, own_dec, 0, keepdims=False)
    own_source = lax.dynamic_index_in_dim(source, own_dec, 0, keepdims=False).reshape(-1)
    own_filled = lax.dynamic_index_in_dim(filled, own_dec, 0, keepdims=False).reshape(-1)
    own_slot = own_targets * CAP + own_ranks
    in_source = lax.dynamic_index_in_dim(source, own_dec, 1, keepdims=False)
    in_filled = lax.dynamic_index_in_dim(filled, own_dec, 1, keepdims=False).reshape(-1)
    in_rows = (jnp.arange(n_dec, dtype=jnp.int32)[:, None] * e_dev + in_source).reshape(-1)
    in_bands = band[in_rows]
    in_first_ra = offset_ra[in_rows]
    in_first_dec = offset_dec[in_rows]
    in_mask = in_filled.astype(jnp.float32)
    extended = with_halo(model, (("ra", 1), ("dec", 2)), H)
    table = column_table(in_first_dec, extended.shape[2])
    tile_patches = cut_patches(extended, in_bands, in_first_ra, table)
    gradpad = jnp.zeros(extended.shape, jnp.float32)
    outgoing = (tile_patches * in_mask[:, None, None]).reshape(n_dec, CAP, P_SIZE * P_SIZE)
    arrived = lax.all_to_all(outgoing, "dec", split_axis=0, concat_axis=0, tiled=True)
    mine = arrived.reshape(n_dec * CAP, P_SIZE * P_SIZE)[own_slot].reshape(e_dev, P_SIZE, P_SIZE)
    residual, back = model_and_adjoint(mine, psf, observed, inv_var)
    own_mask = own_filled.astype(jnp.float32)
    returning = (back.reshape(e_dev, P_SIZE * P_SIZE)[own_source] * own_mask[:, None]).reshape(
        n_dec, CAP, P_SIZE * P_SIZE
    )
    landed = lax.all_to_all(returning, "dec", split_axis=0, concat_axis=0, tiled=True)
    landed = landed.reshape(n_dec * CAP, P_SIZE, P_SIZE) * in_mask[:, None, None]
    gradpad = add_patches(gradpad, landed, in_bands, in_first_ra, table)
    wide = with_halo(gradpad, (("ra", 1), ("dec", 2)), H)
    folded = fold_axis(wide, 1, tile_ra, H)
    gradient = fold_axis(folded, 2, tile_dec, H)
    return (residual, gradient)


def solution(mesh):
    placed = (
        P(None, "ra", "dec"),
        P(("ra", "dec"), None),
        P(("ra", "dec"), None),
        P(("ra", "dec"), None),
        P("ra", None),
        P("ra"),
        P("ra"),
        P("ra"),
    )
    return jax.shard_map(
        body,
        mesh=mesh,
        in_specs=placed,
        out_specs=(P(("ra", "dec"), None), P(None, "ra", "dec")),
        check_vma=False,
    )
```

profile of v0, /device:TPU:1, one launch (start us, length us, event | category | flops | bytes accessed | tf_op | source)
XLA Modules:
  0.0 996.4 jit_solution(12926061206292473158)
XLA Ops:
  34.8 6.3 collective-permute-done.2
  51.4 5.7 pad_maximum_fusion.1
  57.1 19.2 %gather_fusion.2 = f32[64,128,380]{2,0,1:T(8,128)} fusion(f32[6,380,380]{2,0,1:T(8,128)} %pad_maximum_fusion.1, s32[64]{0:T(128)S(1)} %fusion.198), kind=kCustom, calls=%fused_computation.2 | custom fusion | bytes 24904448 | tf_op jit(solution)/shard_map/vmap()/gather | solution.py:92
  76.2 18.9 %broadcast_multiply_fusion.1 = f32[64,128,128]{2,1,0:T(8,128)} fusion(f32[64]{0:T(128)S(1)} %reshape.241, s32[64,128]{1,0:T(8,128)S(1)} %iota_add_fusion, f32[64,128,380]{2,0,1:T(8,128)} %gather_fusion.2), kind=kOutput, calls=%fused_computation.68 | convolution fusion | flops 4785668096 | bytes 16679168 | tf_op jit(solution)/shard_map/sjc,scl->sjl/dot_general | solution.py:95
  95.1 5.6 reshape.232
  100.8 9.0 all-to-all-start
  132.9 38.2 %all-to-all-done = f32[16,4,16384]{2,1,0:T(4,128)} async-done(((f32[16,4,16384]{2,1,0:T(4,128)}), f32[16,4,16384]{2,1,0:T(4,128)}, u32[]{:S(2)}, u32[]{:S(2)}) %all-to-all-start) | async-done | bytes 4194336 | tf_op jit(solution)/shard_map/all_to_all | solution.py:165
  171.1 5.3 reshape.233
  176.5 5.5 gather_fusion.4
  204.5 5.2 fusion.31
  218.4 5.4 fusion.41
  226.9 7.2 fusion.43
  268.8 5.0 fusion.27
  273.8 5.3 fusion.37
  282.2 6.6 fusion.39
  298.0 5.2 gather.32
  303.2 5.1 broadcast_multiply_fusion
  313.1 59.2 %all-to-all-done.1 = f32[16,4,16384]{2,1,0:T(4,128)} async-done(((f32[16,4,16384]{2,1,0:T(4,128)}), f32[16,4,16384]{2,1,0:T(4,128)}, u32[]{:S(2)}, u32[]{:S(2)}) %all-to-all-start.1) | async-done | bytes 4194336 | tf_op jit(solution)/shard_map/all_to_all | solution.py:172
  372.3 6.1 reshape.240
  378.3 13.0 %fusion.2 = f32[64,128,380]{2,1,0:T(8,128)} fusion(s32[64,128]{1,0:T(8,128)S(1)} %iota_add_fusion, f32[64,128,128]{2,1,0:T(8,128)} %reshape.240, f32[64]{0:T(128)S(1)} %reshape.241), kind=kOutput, calls=%fused_computation.10 | convolution fusion | flops 4785668096 | bytes 16679168 | tf_op jit(solution)/shard_map/sjl,scl->sjc/dot_general | solution.py:100
  391.6 551.7 %while.13 = (s32[]{:T(128)}, f32[6,380,380]{2,1,0:T(8,128)S(1)}, s32[64]{0:T(128)S(1)}, s32[64]{0:T(128)S(1)}, f32[64,128,380]{2,1,0:T(8,128)}, /*index=5*/s32[]{:T(128)}, s32[]{:T(128)}, s32[]{:T(128)}, s32[]{:T(128)}) while((s32[]{:T(128)}, f32[6,380,380]{2,1,0:T(8,128)S(1)}, s32[64]{0:T(128)S(1)}, s32[64]{0:T(128)S(1)}, ...), condition=%wide.region_4.5_spmd, body=%wide.region_3.4_spmd.sunk | while | flops 48648 | bytes 973001 | solution.py:110
  946.4 5.8 collective-permute-start.5
  969.5 12.6 %collective-permute-done.6 = f32[6,504,62]{1,2,0:T(8,128)} collective-permute-done((f32[6,504,62]{1,2,0:T(8,128)}, f32[6,504,62]{1,2,0:T(8,128)}, u32[]{:S(2)}, u32[]{:S(2)}) %collective-permute-start.6) | collective-permute-done | bytes 749984 | tf_op jit(solution)/shard_map/ppermute | solution.py:20
  982.1 5.1 collective-permute-done.7
  (390 shorter events, 484.1 us)
Async XLA Ops:
  0.6 12.8 %copy-start = (s32[512]{0:T(512)S(1)}, s32[512]{0:T(512)}, u32[]{:S(2)}) copy-start(s32[512]{0:T(512)} %param.15) | copy-start | bytes 6148
  0.6 9.5 copy-start.13
  0.7 13.6 %copy-start.2 = (s32[512]{0:T(512)S(1)}, s32[512]{0:T(512)}, u32[]{:S(2)}) copy-start(s32[512]{0:T(512)} %param.16) | copy-start | bytes 6148
  0.7 14.4 %copy-start.3 = (s32[512]{0:T(512)S(1)}, s32[512]{0:T(512)}, u32[]{:S(2)}) copy-start(s32[512]{0:T(512)} %param.17) | copy-start | bytes 6148
  2.1 13.8 %collective-permute-start = (f32[6,62,256]{2,0,1:T(8,128)S(1)}, f32[6,62,256]{2,0,1:T(8,128)}, u32[]{:S(2)}, u32[]{:S(2)}) collective-permute-start(f32[6,62,256]{2,0,1:T(8,128)S(1)} %copy.262), channel_id=1, source_target_pairs={{0,16},{16,32},{32,48},{48,64},{64,80},{80,96},{96,112},{1,17},{17... | collective-permute-start | bytes 1142792 | tf_op jit(solution)/shard_map/ppermute | solution.py:20
  7.7 11.7 %collective-permute-start.1 = (f32[6,62,256]{2,0,1:T(8,128)}, f32[6,62,256]{2,0,1:T(8,128)}, u32[]{:S(2)}, u32[]{:S(2)}) collective-permute-start(f32[6,62,256]{2,0,1:T(8,128)} %copy.263), channel_id=1, source_target_pairs={{16,0},{32,16},{48,32},{64,48},{80,64},{96,80},{112,96},{17,1},{33... | collective-permute-start | bytes 1142792 | tf_op jit(solution)/shard_map/ppermute | solution.py:23
  25.2 16.0 %collective-permute-start.2 = (f32[6,380,62]{1,2,0:T(8,128)}, f32[6,380,62]{1,2,0:T(8,128)}, u32[]{:S(2)}, u32[]{:S(2)}) collective-permute-start(f32[6,380,62]{1,2,0:T(8,128)} %copy.185), channel_id=1, source_target_pairs={{0,1},{1,2},{2,3},{3,4},{4,5},{5,6},{6,7},{7,8},{8,9},{9,10},{10,1... | collective-permute-start | bytes 1696328 | tf_op jit(solution)/shard_map/ppermute | solution.py:20
  31.8 16.9 %collective-permute-start.3 = (f32[6,380,62]{1,2,0:T(8,128)}, f32[6,380,62]{1,2,0:T(8,128)}, u32[]{:S(2)}, u32[]{:S(2)}) collective-permute-start(f32[6,380,62]{1,2,0:T(8,128)} %copy.186), channel_id=1, source_target_pairs={{1,0},{2,1},{3,2},{4,3},{5,4},{6,5},{7,6},{8,7},{9,8},{10,9},{11,1... | collective-permute-start | bytes 1696328 | tf_op jit(solution)/shard_map/ppermute | solution.py:23
  100.8 9.0 copy-start.12
  100.8 10.5 %copy-start.11 = (f32[32,4356]{1,0:T(8,128)S(1)}, f32[32,4356]{1,0:T(8,128)}, u32[]{:S(2)}) copy-start(f32[32,4356]{1,0:T(8,128)} %param.12) | copy-start | bytes 1672708
  100.8 70.3 %all-to-all-start = ((f32[16,4,16384]{2,1,0:T(4,128)}), f32[16,4,16384]{2,1,0:T(4,128)}, u32[]{:S(2)}, u32[]{:S(2)}) async-start(f32[16,4,16384]{2,1,0:T(4,128)} %reshape.232), calls=%async_computation | async-start | bytes 8388608 | tf_op jit(solution)/shard_map/all_to_all | solution.py:165
  192.7 4.2 copy-start.5
  237.1 2.8 copy-start.10
  241.0 4.3 copy-start.9
  249.7 3.9 copy-start.6
  308.4 63.9 %all-to-all-start.1 = ((f32[16,4,16384]{2,1,0:T(4,128)}), f32[16,4,16384]{2,1,0:T(4,128)}, u32[]{:S(2)}, u32[]{:S(2)}) async-start(f32[16,4,16384]{2,1,0:T(4,128)} %broadcast_multiply_fusion), calls=%async_computation.1 | async-start | bytes 8388608 | tf_op jit(solution)/shard_map/all_to_all | solution.py:172
  943.2 3.2 copy-start.4
  944.5 11.1 %collective-permute-start.4 = (f32[6,62,380]{2,1,0:T(8,128)}, f32[6,62,380]{2,1,0:T(8,128)}, u32[]{:S(2)}, u32[]{:S(2)}) collective-permute-start(f32[6,62,380]{2,1,0:T(8,128)} %get-tuple-element.121), channel_id=1, source_target_pairs={{0,16},{16,32},{32,48},{48,64},{64,80},{80,96},{96,112},{1,17},{17... | collective-permute-start | bytes 1696328 | tf_op jit(solution)/shard_map/ppermute | solution.py:20
  946.4 11.7 %collective-permute-start.5 = (f32[6,62,380]{2,1,0:T(8,128)}, f32[6,62,380]{2,1,0:T(8,128)}, u32[]{:S(2)}, u32[]{:S(2)}) collective-permute-start(f32[6,62,380]{2,1,0:T(8,128)} %get-tuple-element.122), channel_id=1, source_target_pairs={{16,0},{32,16},{48,32},{64,48},{80,64},{96,80},{112,96},{17,1},{33... | collective-permute-start | bytes 1696328 | tf_op jit(solution)/shard_map/ppermute | solution.py:23
  963.5 18.5 %collective-permute-start.6 = (f32[6,504,62]{1,2,0:T(8,128)}, f32[6,504,62]{1,2,0:T(8,128)}, u32[]{:S(2)}, u32[]{:S(2)}) collective-permute-start(f32[6,504,62]{1,2,0:T(8,128)} %get-tuple-element.119), channel_id=1, source_target_pairs={{0,1},{1,2},{2,3},{3,4},{4,5},{5,6},{6,7},{7,8},{8,9},{9,10},{10,1... | collective-permute-start | bytes 2249864 | tf_op jit(solution)/shard_map/ppermute | solution.py:20
  965.7 21.4 %collective-permute-start.7 = (f32[6,504,62]{1,2,0:T(8,128)}, f32[6,504,62]{1,2,0:T(8,128)}, u32[]{:S(2)}, u32[]{:S(2)}) collective-permute-start(f32[6,504,62]{1,2,0:T(8,128)} %get-tuple-element.120), channel_id=1, source_target_pairs={{1,0},{2,1},{3,2},{4,3},{5,4},{6,5},{7,6},{8,7},{9,8},{10,9},{11,1... | collective-permute-start | bytes 2249864 | tf_op jit(solution)/shard_map/ppermute | solution.py:23
  969.5 21.8 %copy-start.7 = (f32[6,62,380]{1,2,0:T(8,128)S(1)}, f32[6,62,380]{1,2,0:T(8,128)}, u32[]{:S(2)}) copy-start(f32[6,62,380]{1,2,0:T(8,128)} %copy.226) | copy-start | bytes 1696324
  969.5 21.8 %copy-start.8 = (f32[6,62,380]{1,2,0:T(8,128)S(1)}, f32[6,62,380]{1,2,0:T(8,128)}, u32[]{:S(2)}) copy-start(f32[6,62,380]{1,2,0:T(8,128)} %copy.228) | copy-start | bytes 1696324
  969.5 21.8 %copy-start.14 = (pred[256]{0:T(512)(128)(4,1)S(1)}, pred[256]{0:T(512)(128)(4,1)}, u32[]{:S(2)}) copy-start(pred[256]{0:T(512)(128)(4,1)} %constant.107.clone.1) | copy-start | bytes 772
  (1 other events, 2.0 us)
where the time goes:
time: 1010 us; the launch traced here: 996 us
  local copies, waits for them, and re-layouts  304 us (30%)
  loops' own time  250 us (25%)
  matrix products  142 us (14%)
  other arithmetic  136 us (13%)
  waiting for transfers between devices  126 us (12%)
  starting transfers between devices  36.8 us (4%)
    another operation x1, loops' own time, add_patches(): return lax.fori_loop(0, patches.shape[0], accumulate, gradpad)  250 us
    dynamic_update_slice x64, local copies, waits for them, and re-layouts, accumulate(): lax.dynamic_update_slice(total, current + spread[position][None], (which,...  121 us
    add x64, other arithmetic, accumulate(): current + spread[position][None]  105 us
    dot_general x16, matrix products, on_left(): jnp.einsum('jk,mkl->mjl', table, images, precision=lax.Precision.HIGHEST)  62.1 us
    all_to_all x1, waiting for transfers between devices, body(): lax.all_to_all(returning, 'dec', split_axis=0, concat_axis=0, tiled=True)  59.2 us
    dot_general x14, matrix products, on_right(): jnp.einsum('mjk,kl->mjl', images, table, precision=lax.Precision.HIGHEST)  47.7 us
    all_to_all x1, waiting for transfers between devices, body(): lax.all_to_all(outgoing, 'dec', split_axis=0, concat_axis=0, tiled=True)  38.2 us
    dynamic_slice x64, local copies, waits for them, and re-layouts, accumulate(): which = bands[position]  37.7 us
  transfers between devices with their start and end apart: 10, of which 6 were waited for; matrix products, arithmetic and copies ran while one was open for 5% of the time, Pallas kernels for 0%

commit v1 on v0

v1 whole, which is shorter than its diff:
```python
import functools
import math

import jax
import jax.numpy as jnp
import ml_dtypes
import numpy as np
from jax import lax
from jax.experimental import pallas as pl
from jax.experimental.pallas import tpu as pltpu
from jax.sharding import PartitionSpec as P

K = 63
C = 66
CAP = 4
N = 128
PAIRS = 33
PAD = 40
PSF_ROWS = 32
OBS_AT = 32
VAR_AT = 72
SLOT_ROWS = 112
EDGE = 64
SIDE = 128
LIMIT = 60 * 1024 * 1024
MESH = pl.DeviceIdType.MESH
F32 = jnp.float32
BF16 = jnp.bfloat16


def np_split(table):
    high = table.astype(np.float32).astype(ml_dtypes.bfloat16)
    low = (table - high.astype(np.float64)).astype(np.float32).astype(ml_dtypes.bfloat16)
    return high, low


def make_tables():
    theta = 2.0 * math.pi * (np.arange(64) + 0.5) / N

    def to_freq(columns):
        angle = np.asarray(columns)[:, None] * theta[None, :]
        return np.concatenate([np.cos(angle), -np.sin(angle)], axis=1)

    def rows_cs(out_index, in_index, sign):
        angle = 2.0 * math.pi * ((out_index[:, None] * in_index[None, :]) % N) / N
        return np.cos(angle), sign * np.sin(angle)

    full = np.arange(N)
    zero = np.zeros((N, N))
    zero16 = zero.astype(ml_dtypes.bfloat16)

    def wide(table):
        high, low = np_split(table)
        return np.block([[high, low], [high, zero16]])

    patch_cols = wide(to_freq(full))
    psf_cols = np.zeros((N, 2 * N))
    psf_cols[:K, :N] = to_freq(np.arange(K))
    psf_cols[K : 2 * K, N:] = to_freq(np.arange(K))
    psf_h, psf_l = np_split(psf_cols)
    psf_cols = np.concatenate([psf_h, psf_h, psf_l], axis=0)

    def left(out_index, in_index, sign, keep_in=None, keep_out=None):
        cosine, sine = rows_cs(out_index, in_index, sign)
        table = np.concatenate([cosine, sine], axis=1)
        if keep_in is not None:
            table = table * np.concatenate([keep_in, keep_in])[None, :]
        if keep_out is not None:
            table = table * keep_out[:, None]
        return np.concatenate(np_split(table), axis=0)

    patch_rows = left(full, full, 1.0)
    psf_index = np.concatenate([2 * np.arange(32), 2 * np.arange(32) + 1])
    psf_rows = left(full, psf_index, 1.0, keep_in=(psf_index < K).astype(np.float64))
    within = (np.arange(PAD) < PAIRS).astype(np.float64)
    inner_keep = np.concatenate([within, within])
    inner_index = np.concatenate([K - 1 + 2 * np.arange(PAD), K + 2 * np.arange(PAD)])
    pred_rows = left(inner_index, full, -1.0, keep_out=inner_keep)
    res_rows = left(full, inner_index, 1.0, keep_in=inner_keep)
    back_rows = left(full, full, -1.0)
    scale = 2.0 / (N * N)
    inner_cols = K - 1 + np.arange(C)
    pred_cols = np.zeros((2 * N, 2 * N))
    pred_cols[:N, :C] = scale * to_freq(inner_cols).T
    pred_cols[N:, C : 2 * C] = scale * to_freq(inner_cols).T
    pred_cols = np.concatenate(np_split(pred_cols), axis=0)
    res_cols = np.zeros((2 * N, 2 * N))
    res_cols[:C, :N] = to_freq(inner_cols)
    res_cols[C : 2 * C, N:] = to_freq(inner_cols)
    res_cols = np.concatenate(np_split(res_cols), axis=0)
    back_cols = wide(scale * to_freq(full).T)
    psf_rows = np.concatenate([np.concatenate([psf_rows[:N], psf_rows[:N]], axis=1),
                               np.concatenate([psf_rows[N:], np.zeros_like(psf_rows[N:])], axis=1)], axis=0)
    return (patch_cols, patch_rows, psf_cols, psf_rows, pred_rows, pred_cols, res_cols, res_rows,
            back_rows, back_cols)


def split(x):
    high = x.astype(BF16)
    return high, (x - high.astype(F32)).astype(BF16)


def dot(a, b):
    return jnp.dot(a, b, preferred_element_type=F32)


def right_wide(x, table_ref):
    high, low = split(x)
    both = dot(jnp.concatenate([high, low], axis=1), table_ref[...])
    return both[:, :N] + both[:, N:]


def right_three(x, table_ref):
    high, low = split(x)
    depth = x.shape[1]
    return (dot(high, table_ref[:depth, :]) + dot(low, table_ref[:depth, :])
            + dot(high, table_ref[depth:, :]))


def left_three(table_ref, x):
    rows = table_ref.shape[0] // 2
    high, low = split(x)
    both = dot(table_ref[...], high)
    return both[:rows] + both[rows:] + dot(table_ref[:rows, :], low)


def turned(y, sign):
    return pltpu.roll(y, 64, 1) * sign


def stacked(parts, sign):
    return jnp.concatenate(
        [jnp.concatenate([y, turned(y, sign)], axis=0) for y in parts], axis=1)


def exposure_kernel(first, meta_ref, slots_ref, ext_ref, *refs):
    if first:
        acc_in_ref = None
    else:
        acc_in_ref, refs = refs[0], refs[1:]
    (patch_cols, patch_rows, psf_cols, psf_rows, pred_rows, pred_cols, res_cols, res_rows,
     back_rows, back_cols, resid_ref, acc_ref) = refs
    step = pl.program_id(0)

    @pl.when(step == 0)
    def _():
        if first:
            acc_ref[...] = jnp.zeros_like(acc_ref)
        else:
            acc_ref[...] = acc_in_ref[...]

    lane = lax.broadcasted_iota(jnp.int32, (1, N), 1)
    sign = jnp.where(lane < 64, 1.0, -1.0).astype(F32)
    low_half = lane < 64

    places = []
    patches = []
    for e in range(2):
        code = jnp.maximum(meta_ref[step * 2 + e] - 1, 0)
        which = lax.shift_right_logical(code, 16)
        row = lax.bitwise_and(lax.shift_right_logical(code, 8), 255) + (EDGE - K + 1)
        column = lax.bitwise_and(code, 255) + (SIDE - K + 1)
        row_at = pl.multiple_of(lax.shift_left(lax.shift_right_logical(row, 3), 3), 8)
        col_at = pl.multiple_of(lax.shift_left(lax.shift_right_logical(column, 7), 7), 128)
        down = row - row_at
        over = column - col_at
        places.append((which, row_at, col_at, down, over))
        window = ext_ref[which, pl.ds(row_at, N + 8), pl.ds(col_at, 2 * N)]
        window = pltpu.roll(window, lax.bitwise_and(2 * N - over, 2 * N - 1), 1)[:, :N]
        window = pltpu.roll(window, jnp.where(down == 0, 0, N + 8 - down), 0)[:N]
        patches.append(window)

    y = right_wide(jnp.concatenate(patches, axis=0), patch_cols)
    z = left_three(patch_rows, stacked([y[:N], y[N:]], sign))

    pairs = []
    for e in range(2):
        x = slots_ref[e, :PSF_ROWS, :]
        both = jnp.concatenate([pltpu.roll(x, 1, 0), x], axis=1)
        pairs.append(pltpu.roll(both, N, 1, stride=2, stride_axis=0)[:, :N])
    high, low = split(jnp.concatenate(pairs, axis=0))
    y = dot(jnp.concatenate([high, low], axis=1), psf_cols[: 2 * N, :]) + dot(high, psf_cols[2 * N :, :])
    y = stacked([jnp.concatenate([y[32 * e : 32 * e + 32, :N], y[32 * e : 32 * e + 32, N:]], axis=0)
                 for e in range(2)], sign)
    high, low = split(y)
    khat = (dot(psf_rows[:N, :], jnp.concatenate([high, low], axis=0))
            + dot(psf_rows[N:, :N], high))

    kernels = []
    spec = []
    for e in range(2):
        k = khat[:, e * N : e * N + N]
        rk = pltpu.roll(k, 64, 1)
        k_re = jnp.where(low_half, k, rk)
        k_im = jnp.where(low_half, -rk, k)
        kernels.append((k_re, k_im))
        p = z[:, e * N : e * N + N]
        rp = pltpu.roll(p, 64, 1)
        spec.append(jnp.concatenate(
            [p * k_re + rp * k_im, (rp * k_re - p * k_im) * sign], axis=0))
    u = left_three(pred_rows, jnp.concatenate(spec, axis=1))
    u = jnp.concatenate(
        [jnp.concatenate([u[:PAD, e * N : e * N + N], u[PAD:, e * N : e * N + N]], axis=1)
         for e in range(2)], axis=0)
    predicted = right_three(u, pred_cols)

    number = lax.broadcasted_iota(jnp.int32, (PAD, 1), 0)
    last = number == PAIRS - 1
    turn = lax.bitwise_and(lane + 4 * number, N - 1)
    pairs = []
    for e in range(2):
        image = pltpu.roll(predicted[e * PAD : e * PAD + PAD], 0, 1, stride=4, stride_axis=0)
        front, rear = image[:, :N], image[:, N:]
        flat = (jnp.where(last, 0.0, front) + pltpu.roll(rear, 1, 0)
                + pltpu.roll(jnp.where(last, front, 0.0), 2, 0))
        resid = slots_ref[e, VAR_AT : VAR_AT + PAD, :] * (flat - slots_ref[e, OBS_AT : OBS_AT + PAD, :])
        resid_ref[e] = resid
        front = jnp.take_along_axis(resid, turn, axis=1, mode="promise_in_bounds")
        rear = jnp.take_along_axis(pltpu.roll(resid, PAD - 1, 0), turn, axis=1, mode="promise_in_bounds")
        pairs.append(jnp.concatenate(
            [jnp.where(lane + 4 * number < N, front, rear),
             jnp.where(last, pltpu.roll(resid, PAD - 2, 0), rear)], axis=1))
    v = right_three(jnp.concatenate(pairs, axis=0), res_cols)
    v = [jnp.concatenate([v[e * PAD : e * PAD + PAD, :N], v[e * PAD : e * PAD + PAD, N:]], axis=0)
         for e in range(2)]
    r = left_three(res_rows, stacked(v, sign))
    spec = []
    for e in range(2):
        k_re, k_im = kernels[e]
        p = r[:, e * N : e * N + N]
        rp = pltpu.roll(p, 64, 1)
        spec.append(jnp.concatenate(
            [p * k_re - rp * k_im, (rp * k_re + p * k_im) * sign], axis=0))
    u = left_three(back_rows, jnp.concatenate(spec, axis=1))
    back = right_wide(jnp.concatenate([u[:, :N], u[:, N:]], axis=0), back_cols)
    for e in range(2):
        which, row_at, col_at, down, over = places[e]
        image = jnp.concatenate([back[e * N : e * N + N], jnp.zeros((8, N), F32)], axis=0)
        image = pltpu.roll(image, down, 0)
        image = jnp.concatenate([image, jnp.zeros_like(image)], axis=1)
        image = pltpu.roll(image, over, 1)
        acc_ref[which, pl.ds(row_at, N + 8), pl.ds(col_at, 2 * N)] += image


def whole(shape):
    return pl.BlockSpec(shape, lambda i, meta: (0,) * len(shape), pipeline_mode=pl.Buffered(1))


def run_exposures(meta, slots, ext, acc, tables):
    number = slots.shape[0]
    first = acc is None
    operands = [slots, ext] + ([] if first else [acc]) + list(tables)
    in_specs = [pl.BlockSpec((2, SLOT_ROWS, N), lambda i, meta: (i, 0, 0))]
    in_specs += [whole(o.shape) for o in operands[1:]]
    return pl.pallas_call(
        functools.partial(exposure_kernel, first),
        grid_spec=pltpu.PrefetchScalarGridSpec(
            num_scalar_prefetch=1,
            grid=(number // 2,),
            in_specs=in_specs,
            out_specs=[
                pl.BlockSpec((2, PAD, N), lambda i, meta: (i, 0, 0)),
                whole(ext.shape),
            ],
        ),
        out_shape=[
            jax.ShapeDtypeStruct((number, PAD, N), F32),
            jax.ShapeDtypeStruct(ext.shape, F32),
        ],
        compiler_params=pltpu.CompilerParams(vmem_limit_bytes=LIMIT),
        cost_estimate=pl.CostEstimate(flops=number * 200_000_000, bytes_accessed=12_000_000, transcendentals=0),
    )(meta, *operands)


def three(x):
    high = x.astype(BF16)
    rest = x - high.astype(F32)
    middle = rest.astype(BF16)
    return jnp.concatenate([high, middle, (rest - middle.astype(F32)).astype(BF16)], axis=0)


def prepare_kernel(n_dec, column_ref, row_ref, psf_ref, obs_ref, var_ref, out_ref):
    column, row = column_ref[...], row_ref[...]
    count = row.shape[1]
    slots = CAP * n_dec
    earlier = lax.broadcasted_iota(jnp.int32, (count, count), 0) < lax.broadcasted_iota(
        jnp.int32, (count, count), 1)
    rank = jnp.sum(jnp.where(jnp.logical_and(column == row, earlier), 1, 0), axis=0, keepdims=True)
    place = rank * n_dec + row
    chosen = (lax.broadcasted_iota(jnp.int32, (slots, count), 0) == place).astype(F32).astype(BF16)
    chosen = jnp.concatenate([chosen] * 3, axis=1)
    for ref, base, rows in ((psf_ref, 0, 32), (obs_ref, OBS_AT, PAD), (var_ref, VAR_AT, PAD)):
        width = ref.shape[1]
        for start in range(0, rows, 4):
            end = min((start + 4) * N, width)
            if start * N < width:
                x = ref[:, start * N : end]
                y = dot(chosen, three(x))
                if end < (start + 4) * N:
                    y = jnp.concatenate([y, jnp.zeros((slots, (start + 4) * N - end), F32)], axis=1)
            else:
                y = jnp.zeros((slots, 4 * N), F32)
            for t in range(4):
                out_ref[pl.ds(base + start + t, slots, stride=SLOT_ROWS), :] = y[:, t * N : t * N + N]


def prepare(column, row, psf, obs, var, n_dec):
    return pl.pallas_call(
        functools.partial(prepare_kernel, n_dec),
        out_shape=jax.ShapeDtypeStruct((CAP * n_dec * SLOT_ROWS, N), F32),
        compiler_params=pltpu.CompilerParams(vmem_limit_bytes=LIMIT),
    )(column, row, psf, obs, var)


def finish_kernel(n_dec, column_ref, row_ref, in_ref, out_ref):
    column, row = column_ref[...], row_ref[...]
    count = row.shape[1]
    slots = CAP * n_dec
    earlier = lax.broadcasted_iota(jnp.int32, (count, count), 1) < lax.broadcasted_iota(
        jnp.int32, (count, count), 0)
    rank = jnp.sum(jnp.where(jnp.logical_and(column == row, earlier), 1, 0), axis=1, keepdims=True)
    place = rank * n_dec + column
    chosen = (lax.broadcasted_iota(jnp.int32, (count, slots), 1) == place).astype(F32).astype(BF16)
    chosen = jnp.concatenate([chosen] * 3, axis=1)
    width = out_ref.shape[1]
    for start in range(0, PAD, 4):
        if start * N >= width:
            break
        x = jnp.concatenate(
            [in_ref[pl.ds(start + t, slots, stride=PAD), :] for t in range(4)], axis=1)
        y = dot(chosen, three(x))
        end = min((start + 4) * N, width)
        out_ref[:, start * N : end] = y[:, : end - start * N]


def finish(column, row, landed, n_dec):
    return pl.pallas_call(
        functools.partial(finish_kernel, n_dec),
        out_shape=jax.ShapeDtypeStruct((row.shape[1], C * C), F32),
        compiler_params=pltpu.CompilerParams(vmem_limit_bytes=LIMIT),
    )(column, row, landed)


def neighbours(n_ra, n_dec):
    ra, dec = lax.axis_index("ra"), lax.axis_index("dec")
    up, down = lax.rem(ra + 1, n_ra), lax.rem(ra + n_ra - 1, n_ra)
    right, left = lax.rem(dec + 1, n_dec), lax.rem(dec + n_dec - 1, n_dec)
    return ra, dec, up, down, right, left


def greet(ra, dec, up, down, right, left):
    barrier = pltpu.get_barrier_semaphore()
    for other in ((up, dec), (down, dec), (ra, right), (ra, left),
                  (up, right), (up, left), (down, right), (down, left)):
        pl.semaphore_signal(barrier, inc=1, device_id=other, device_id_type=MESH)
    pl.semaphore_wait(barrier, 8)


def halo_kernel(n_ra, n_dec, model_ref, ext_ref, to_right, to_left, from_left, from_right, corners,
                send, recv):
    ra, dec, up, down, right, left = neighbours(n_ra, n_dec)
    greet(ra, dec, up, down, right, left)
    tra, tdec = model_ref.shape[1], model_ref.shape[2]
    top, side_at = EDGE + tra, SIDE + tdec
    low_half = lax.broadcasted_iota(jnp.int32, (1, 1, N), 2) < 64

    def copy(index, src, dst, other):
        return pltpu.make_async_remote_copy(
            src_ref=src, dst_ref=dst, send_sem=send.at[index], recv_sem=recv.at[index],
            device_id=other, device_id_type=MESH)

    copies = [
        copy(0, model_ref.at[:, tra - EDGE :, :], ext_ref.at[:, :EDGE, SIDE:side_at], (up, dec)),
        copy(1, model_ref.at[:, :EDGE, :], ext_ref.at[:, top:, SIDE:side_at], (down, dec)),
    ]
    for c in copies:
        c.start()
    for q in range(3):
        to_right[q] = jnp.where(
            low_half[0], pltpu.roll(model_ref[2 * q + 1, :, tdec - N :], 64, 1), model_ref[2 * q, :, tdec - N :])
    more = [
        copy(2, to_right, from_left, (ra, right)),
        copy(4, to_right.at[:, tra - EDGE :, :], corners.at[0], (up, right)),
        copy(5, to_right.at[:, :EDGE, :], corners.at[1], (down, right)),
    ]
    for c in more:
        c.start()
    copies += more
    for q in range(3):
        to_left[q] = jnp.where(
            low_half[0], model_ref[2 * q, :, :N], pltpu.roll(model_ref[2 * q + 1, :, :N], 64, 1))
    more = [
        copy(3, to_left, from_right, (ra, left)),
        copy(6, to_left.at[:, tra - EDGE :, :], corners.at[2], (up, left)),
        copy(7, to_left.at[:, :EDGE, :], corners.at[3], (down, left)),
    ]
    for c in more:
        c.start()
    copies += more
    ext_ref[:, EDGE:top, SIDE:side_at] = model_ref[...]
    for c in copies:
        c.wait()
    zero = jnp.zeros((), F32)
    one = jnp.ones((), F32)
    in_left = jnp.where(dec > 0, one, zero)
    in_right = jnp.where(dec < n_dec - 1, one, zero)
    in_low = jnp.where(ra > 0, one, zero)
    in_high = jnp.where(ra < n_ra - 1, one, zero)

    @pl.when(ra == 0)
    def _():
        ext_ref[:, :EDGE, SIDE:side_at] = jnp.zeros((ext_ref.shape[0], EDGE, tdec), F32)

    @pl.when(ra == n_ra - 1)
    def _():
        ext_ref[:, top:, SIDE:side_at] = jnp.zeros((ext_ref.shape[0], EDGE, tdec), F32)

    for q in range(3):
        for src, rows, col, scale in (
            (from_left.at[q], slice(EDGE, top), slice(0, SIDE), in_left),
            (from_right.at[q], slice(EDGE, top), slice(side_at, side_at + SIDE), in_right),
            (corners.at[0, q], slice(0, EDGE), slice(0, SIDE), in_low * in_left),
            (corners.at[1, q], slice(top, top + EDGE), slice(0, SIDE), in_high * in_left),
            (corners.at[2, q], slice(0, EDGE), slice(side_at, side_at + SIDE), in_low * in_right),
            (corners.at[3, q], slice(top, top + EDGE), slice(side_at, side_at + SIDE), in_high * in_right),
        ):
            value = src[...] * scale
            ext_ref[2 * q, rows, col] = value
            ext_ref[2 * q + 1, rows, col] = pltpu.roll(value, 64, 1)


def halo(model, n_ra, n_dec):
    bands, tra, tdec = model.shape
    strip = pltpu.VMEM((3, tra, N), F32)
    return pl.pallas_call(
        functools.partial(halo_kernel, n_ra, n_dec),
        out_shape=jax.ShapeDtypeStruct((bands, tra + 2 * EDGE, tdec + 2 * SIDE), F32),
        in_specs=[pl.BlockSpec(memory_space=pltpu.VMEM)],
        out_specs=pl.BlockSpec(memory_space=pltpu.VMEM),
        scratch_shapes=[strip, strip, strip, strip, pltpu.VMEM((4, 3, EDGE, N), F32),
                        pltpu.SemaphoreType.DMA((8,)), pltpu.SemaphoreType.DMA((8,))],
        compiler_params=pltpu.CompilerParams(
            collective_id=0, has_side_effects=True, vmem_limit_bytes=LIMIT),
        cost_estimate=pl.CostEstimate(flops=0, bytes_accessed=40_000_000, transcendentals=0),
    )(model)


def fold_kernel(n_ra, n_dec, acc_ref, out_ref, to_right, to_left, from_left, from_right, out_corners,
                corners, from_up, from_down, send, recv):
    ra, dec, up, down, right, left = neighbours(n_ra, n_dec)
    greet(ra, dec, up, down, right, left)
    tra, tdec = out_ref.shape[1], out_ref.shape[2]
    top, side_at = EDGE + tra, SIDE + tdec
    low_half = lax.broadcasted_iota(jnp.int32, (1, N), 1) < 64

    def copy(index, src, dst, other):
        return pltpu.make_async_remote_copy(
            src_ref=src, dst_ref=dst, send_sem=send.at[index], recv_sem=recv.at[index],
            device_id=other, device_id_type=MESH)

    copies = [
        copy(0, acc_ref.at[:, :EDGE, SIDE:side_at], from_up, (down, dec)),
        copy(1, acc_ref.at[:, top:, SIDE:side_at], from_down, (up, dec)),
    ]
    for c in copies:
        c.start()

    def pack_left(q, rows):
        return jnp.where(low_half, pltpu.roll(acc_ref[2 * q + 1, rows, :SIDE], 64, 1), acc_ref[2 * q, rows, :SIDE])

    def pack_right(q, rows):
        return jnp.where(low_half, acc_ref[2 * q, rows, side_at:], pltpu.roll(acc_ref[2 * q + 1, rows, side_at:], 64, 1))

    middle, lower, upper = slice(EDGE, top), slice(0, EDGE), slice(top, top + EDGE)
    for q in range(3):
        to_left[q] = pack_left(q, middle)
    more = [copy(2, to_left, from_right, (ra, left))]
    more[0].start()
    copies += more
    for q in range(3):
        to_right[q] = pack_right(q, middle)
    more = [copy(3, to_right, from_left, (ra, right))]
    more[0].start()
    copies += more
    for q in range(3):
        out_corners[0, q] = pack_left(q, lower)
        out_corners[1, q] = pack_left(q, upper)
        out_corners[2, q] = pack_right(q, lower)
        out_corners[3, q] = pack_right(q, upper)
    more = [
        copy(4, out_corners.at[0], corners.at[0], (down, left)),
        copy(5, out_corners.at[1], corners.at[1], (up, left)),
        copy(6, out_corners.at[2], corners.at[2], (down, right)),
        copy(7, out_corners.at[3], corners.at[3], (up, right)),
    ]
    for c in more:
        c.start()
    copies += more
    out_ref[...] = acc_ref[:, EDGE:top, SIDE:side_at]
    for c in copies:
        c.wait()
    zero = jnp.zeros((), F32)
    one = jnp.ones((), F32)
    in_left = jnp.where(dec > 0, one, zero)
    in_right = jnp.where(dec < n_dec - 1, one, zero)
    in_low = jnp.where(ra > 0, one, zero)
    in_high = jnp.where(ra < n_ra - 1, one, zero)
    out_ref[:, tra - EDGE :, :] += from_up[...] * in_high
    out_ref[:, :EDGE, :] += from_down[...] * in_low
    every, low_rows, high_rows = slice(0, tra), slice(0, EDGE), slice(tra - EDGE, tra)
    for q in range(3):
        for src, rows, scale, at_right in (
            (from_right.at[q], every, in_right, True),
            (from_left.at[q], every, in_left, False),
            (corners.at[0, q], high_rows, in_high * in_right, True),
            (corners.at[1, q], low_rows, in_low * in_right, True),
            (corners.at[2, q], high_rows, in_high * in_left, False),
            (corners.at[3, q], low_rows, in_low * in_left, False),
        ):
            value = src[...] * scale
            other = pltpu.roll(value, 64, 1)
            if at_right:
                cols, keep = slice(tdec - N, tdec), jnp.logical_not(low_half)
            else:
                cols, keep = slice(0, N), low_half
            out_ref[2 * q, rows, cols] += jnp.where(keep, value, 0.0)
            out_ref[2 * q + 1, rows, cols] += jnp.where(keep, other, 0.0)


def fold(acc, n_ra, n_dec):
    bands, tra, tdec = acc.shape[0], acc.shape[1] - 2 * EDGE, acc.shape[2] - 2 * SIDE
    strip = pltpu.VMEM((3, tra, N), F32)
    corner = pltpu.VMEM((4, 3, EDGE, N), F32)
    band = pltpu.VMEM((bands, EDGE, tdec), F32)
    return pl.pallas_call(
        functools.partial(fold_kernel, n_ra, n_dec),
        out_shape=jax.ShapeDtypeStruct((bands, tra, tdec), F32),
        in_specs=[pl.BlockSpec(memory_space=pltpu.VMEM)],
        out_specs=pl.BlockSpec(memory_space=pltpu.VMEM),
        scratch_shapes=[strip, strip, strip, strip, corner, corner, band, band,
                        pltpu.SemaphoreType.DMA((8,)), pltpu.SemaphoreType.DMA((8,))],
        compiler_params=pltpu.CompilerParams(
            collective_id=1, has_side_effects=True, vmem_limit_bytes=LIMIT),
        cost_estimate=pl.CostEstimate(flops=0, bytes_accessed=40_000_000, transcendentals=0),
    )(acc)


def body(model, observed, inv_var, psf, target_dec, band, offset_ra, offset_dec):
    n_ra, n_dec = lax.axis_size("ra"), lax.axis_size("dec")
    own = lax.axis_index("dec")
    e_dev = observed.shape[0]
    targets = target_dec[:, 0].reshape(n_dec, e_dev)
    row = lax.dynamic_slice_in_dim(targets, own, 1, 0)
    column = lax.dynamic_slice_in_dim(target_dec, own * e_dev, e_dev, 0)
    slots = prepare(column, row, psf, observed, inv_var, n_dec)
    slots = slots.reshape(CAP, n_dec, SLOT_ROWS, N)
    here = targets == own
    order = jnp.arange(e_dev, dtype=jnp.int32)
    rank = jnp.sum(jnp.where(here[:, None, :] & (order[None, :] < order[:, None])[None], 1, 0), axis=2)
    code = ((band * 256 + offset_ra) * 256 + offset_dec + 1).reshape(n_dec, e_dev)
    meta = jnp.sum(
        jnp.where(here[None] & (rank[None] == jnp.arange(CAP, dtype=jnp.int32)[:, None, None]), code[None], 0),
        axis=2)
    arrived = [lax.all_to_all(slots[s], "dec", 0, 0, tiled=True) for s in range(CAP)]
    ext = halo(model, n_ra, n_dec)
    tables = [jnp.asarray(t) for t in make_tables()]
    acc = None
    landed = []
    for s in range(CAP):
        resid, acc = run_exposures(meta[s], arrived[s], ext, acc, tables)
        landed.append(lax.all_to_all(resid, "dec", 0, 0, tiled=True))
    gradient = fold(acc, n_ra, n_dec)
    landed = jnp.concatenate(landed, axis=0).reshape(CAP * n_dec * PAD, N)
    residual = finish(column, row, landed, n_dec)
    return residual, gradient


def solution(mesh):
    placed = (
        P(None, "ra", "dec"),
        P(("ra", "dec"), None),
        P(("ra", "dec"), None),
        P(("ra", "dec"), None),
        P("ra", None),
        P("ra"),
        P("ra"),
        P("ra"),
    )
    return jax.shard_map(
        body,
        mesh=mesh,
        in_specs=placed,
        out_specs=(P(("ra", "dec"), None), P(None, "ra", "dec")),
        check_vma=False,
    )
```

time: 1010 us -> 263 us (0.26); the launches traced: 996 us -> 262 us
  local copies, waits for them, and re-layouts: 304 us -> 7.92 us
  loops' own time: 250 us -> 0 us
  Pallas kernels: 0 us -> 171 us
  matrix products: 142 us -> 0 us
  other arithmetic: 136 us -> 3.01 us
  waiting for transfers between devices: 126 us -> 0.01 us
  blocking collectives: 0 us -> 55.7 us
  starting transfers between devices: 36.8 us -> 24.1 us
    another operation x1 -> x0, loops' own time: 250 us -> none  [add_patches(): return lax.fori_loop(0, patches.shape[0], accumulate, gradpad)]
    pallas_call x0 -> x8, Pallas kernels: none -> 171 us  [the longest x4 105 us: run_exposures(): pl.pallas_call(functools.partial(exposure_kernel, first), grid_spec=pltpu...]
    dot_general x32 -> x0, matrix products: 142 us -> none  [the longest x16 62.1 us: on_left(): jnp.einsum('jk,mkl->mjl', table, images, precision=lax.Precision.HIGHEST)]
    dynamic_update_slice x64 -> x0, local copies, waits for them, and re-layouts: 121 us -> none  [accumulate(): lax.dynamic_update_slice(total, current + spread[position][None], (which,...]
    add x67 -> x1, other arithmetic: 108 us -> 0.01 us  [body(): (band * 256 + offset_ra) * 256 + offset_dec + 1]
    all_to_all x2 -> x5, waiting for transfers between devices: 97.4 us -> 0.01 us  [the longest x3 0.01 us: body(): landed.append(lax.all_to_all(resid, 'dec', 0, 0, tiled=True))]
    dynamic_slice x131 -> x2, local copies, waits for them, and re-layouts: 75.7 us -> 1.33 us  [the longest x1 0.73 us: body(): column = lax.dynamic_slice_in_dim(target_dec, own * e_dev, e_dev, 0)]
    all_to_all x0 -> x3, blocking collectives: none -> 55.7 us  [the longest x2 41 us: body(): lax.all_to_all(slots[s], 'dec', 0, 0, tiled=True)]
  transfers between devices with their start and end apart: 10 -> 5, of which waited for: 6 -> 0; matrix products, arithmetic and copies ran while one was open for 5% -> 0% of each run, Pallas kernels for 0% -> 62%
where the time goes in v1:
time: 263 us; the launch traced here: 262 us
  Pallas kernels  171 us (65%)
  blocking collectives  55.7 us (21%)
  starting transfers between devices  24.1 us (9%)
  local copies, waits for them, and re-layouts  7.92 us (3%)
  other arithmetic  3.01 us (1%)
    pallas_call x4, Pallas kernels, run_exposures(): pl.pallas_call(functools.partial(exposure_kernel, first), grid_spec=pltpu...  105 us
    all_to_all x2, blocking collectives, body(): lax.all_to_all(slots[s], 'dec', 0, 0, tiled=True)  41 us
    pallas_call x1, Pallas kernels, halo(): pl.pallas_call(functools.partial(halo_kernel, n_ra, n_dec), out_shape=jax...  30.9 us
    pallas_call x1, Pallas kernels, fold(): pl.pallas_call(functools.partial(fold_kernel, n_ra, n_dec), out_shape=jax...  26.9 us
    all_to_all x3, starting transfers between devices, body(): landed.append(lax.all_to_all(resid, 'dec', 0, 0, tiled=True))  16.8 us
    all_to_all x1, blocking collectives, body(): landed.append(lax.all_to_all(resid, 'dec', 0, 0, tiled=True))  14.7 us
    all_to_all x2, starting transfers between devices, body(): lax.all_to_all(slots[s], 'dec', 0, 0, tiled=True)  7.28 us
  transfers between devices with their start and end apart: 5, of which 0 were waited for; matrix products, arithmetic and copies ran while one was open for 0% of the time, Pallas kernels for 62%

profile of v1, /device:TPU:1, one launch (start us, length us, event | category | flops | bytes accessed | tf_op | source)
XLA Modules:
  0.0 262.3 jit_solution(559584583898032715)
XLA Ops:
  0.6 0.7 constant_dynamic-slice_fusion.1
  1.9 1.3 reduce.3
  3.3 0.7 copy.22.column_ref
  4.0 0.6 constant_dynamic-slice_fusion.row_ref
  4.6 4.8 %shard_map.185 = f32[7168,128]{1,0:T(8,128)} custom-call(s32[32,1]{1,0:T(8,128)} %copy.22.column_ref, s32[1,32]{1,0:T(1,128)} %constant_dynamic-slice_fusion.row_ref, f32[32,3969]{1,0:T(8,128)} %psf_ref.1, f32[32,4356]{1,0:T(8,128)} %obs_ref.1, f32[32,4356]{1,0:T(8,128)} %var_ref.1), custom_call_target="tpu_custom_call" | custom-call | tf_op jit(solution)/shard_map/pallas_call | solution.py:308
  9.4 3.5 %fusion.1 = (f32[1792,128]{1,0:T(8,128)S(1)}, f32[1792,128]{1,0:T(8,128)S(1)}, f32[1792,128]{1,0:T(8,128)}, f32[1792,128]{1,0:T(8,128)}) fusion(f32[7168,128]{1,0:T(8,128)} %shard_map.185), kind=kLoop, calls=%fused_computation.14 | loop fusion | bytes 7340032 | tf_op jit(solution)/shard_map/slice | solution.py:564
  12.8 23.4 %all_to_all.40.slots_ref = f32[16,112,128]{2,1,0:T(8,128)} all-to-all(f32[16,112,128]{2,1,0:T(8,128)S(1)} %bitcast.16), channel_id=1, replica_groups=mesh['ra'=8,'dec'=16] {'dec'}, dimensions={0} | all-to-all | bytes 1835008 | tf_op jit(solution)/shard_map/all_to_all | solution.py:564
  36.2 17.6 %all_to_all.41.slots_ref = f32[16,112,128]{2,1,0:T(8,128)} all-to-all(f32[16,112,128]{2,1,0:T(8,128)S(1)} %bitcast.15), channel_id=1, replica_groups=mesh['ra'=8,'dec'=16] {'dec'}, dimensions={0} | all-to-all | bytes 1835008 | tf_op jit(solution)/shard_map/all_to_all | solution.py:564
  53.8 3.6 %all-to-all-start.4 = ((f32[16,112,128]{2,1,0:T(8,128)}), f32[16,112,128]{2,1,0:T(8,128)S(1)}, u32[]{:S(2)}, u32[]{:S(2)}) async-start(f32[16,112,128]{2,1,0:T(8,128)} %bitcast.5), calls=%async_computation.4 | async-start | bytes 1835008 | tf_op jit(solution)/shard_map/all_to_all | solution.py:564
  57.6 30.9 %shard_map.186.ext_ref = f32[6,384,512]{2,1,0:T(8,128)} custom-call(f32[6,256,256]{2,1,0:T(8,128)} %model_ref.1), custom_call_target="tpu_custom_call" | custom-call | bytes 40000000 | tf_op jit(solution)/shard_map/pallas_call | solution.py:435
  88.5 3.6 %all-to-all-start.2 = ((f32[16,112,128]{2,1,0:T(8,128)}), f32[16,112,128]{2,1,0:T(8,128)S(1)}, u32[]{:S(2)}, u32[]{:S(2)}) async-start(f32[16,112,128]{2,1,0:T(8,128)} %bitcast.3), calls=%async_computation.2 | async-start | bytes 1835008 | tf_op jit(solution)/shard_map/all_to_all | solution.py:564
  92.7 0.6 slice_bitcast_fusion.3
  93.3 25.3 %shard_map.187 = (f32[16,40,128]{2,1,0:T(8,128)}, f32[6,384,512]{2,1,0:T(8,128)}) custom-call(s32[16]{0:T(128)} %get-tuple-element.22.meta_ref, f32[16,112,128]{2,1,0:T(8,128)} %all_to_all.41.slots_ref, f32[6,384,512]{2,1,0:T(8,128)} %shard_map.186.ext_ref, bf16[256,256]{1,0:T(8,128)(2,1)} %constant.16.clone.refs_0_.refs_1_, ...), custom_call_target="tpu_custom_call" | custom-call | flops 3200000000 | bytes 12000000 | tf_op jit(solution)/shard_map/pallas_call | solution.py:255
  118.6 6.6 %all-to-all-start.1 = ((f32[16,40,128]{2,1,0:T(8,128)}), f32[16,40,128]{2,1,0:T(8,128)S(1)}, u32[]{:S(2)}, u32[]{:S(2)}) async-start(f32[16,40,128]{2,1,0:T(8,128)} %get-tuple-element.10), calls=%async_computation.1 | async-start | bytes 655360 | tf_op jit(solution)/shard_map/all_to_all | solution.py:571
  125.2 26.6 %shard_map.188 = (f32[16,40,128]{2,1,0:T(8,128)}, f32[6,384,512]{2,1,0:T(8,128)}) custom-call(s32[16]{0:T(128)} %get-tuple-element.25.meta_ref, f32[16,112,128]{2,1,0:T(8,128)} %copy-done.2, f32[6,384,512]{2,1,0:T(8,128)} %shard_map.186.ext_ref, f32[6,384,512]{2,1,0:T(8,128)} %get-tuple-element.11.refs_0_, bf16[256,256]{1,0:T(8,128)(2,1)} %constant.16.clone.refs_0_.refs_1_, ...), custom_call_target="tpu_custom_call" | custom-call | flops 3200000000 | bytes 12000000 | tf_op jit(solution)/shard_map/pallas_call | solution.py:255
  151.9 6.7 %all-to-all-start.3 = ((f32[16,40,128]{2,1,0:T(8,128)}), f32[16,40,128]{2,1,0:T(8,128)S(1)}, u32[]{:S(2)}, u32[]{:S(2)}) async-start(f32[16,40,128]{2,1,0:T(8,128)} %get-tuple-element.12), calls=%async_computation.3 | async-start | bytes 655360 | tf_op jit(solution)/shard_map/all_to_all | solution.py:571
  158.5 26.6 %shard_map.189 = (f32[16,40,128]{2,1,0:T(8,128)}, f32[6,384,512]{2,1,0:T(8,128)}) custom-call(s32[16]{0:T(128)} %get-tuple-element.24.meta_ref, f32[16,112,128]{2,1,0:T(8,128)} %copy-done.1, f32[6,384,512]{2,1,0:T(8,128)} %shard_map.186.ext_ref, f32[6,384,512]{2,1,0:T(8,128)} %get-tuple-element.13.refs_0_, bf16[256,256]{1,0:T(8,128)(2,1)} %constant.16.clone.refs_0_.refs_1_, ...), custom_call_target="tpu_custom_call" | custom-call | flops 3200000000 | bytes 12000000 | tf_op jit(solution)/shard_map/pallas_call | solution.py:255
  185.1 26.6 %shard_map.190 = (f32[16,40,128]{2,1,0:T(8,128)}, f32[6,384,512]{2,1,0:T(8,128)}) custom-call(s32[16]{0:T(128)} %get-tuple-element.23.meta_ref, f32[16,112,128]{2,1,0:T(8,128)} %all_to_all.40.slots_ref, f32[6,384,512]{2,1,0:T(8,128)} %shard_map.186.ext_ref, f32[6,384,512]{2,1,0:T(8,128)} %get-tuple-element.15.refs_0_, ...), custom_call_target="tpu_custom_call" | custom-call | flops 3200000000 | bytes 12000000 | tf_op jit(solution)/shard_map/pallas_call | solution.py:255
  211.8 14.7 %all_to_all.42 = f32[16,40,128]{2,1,0:T(8,128)S(1)} all-to-all(f32[16,40,128]{2,1,0:T(8,128)} %get-tuple-element.16), channel_id=1, replica_groups=mesh['ra'=8,'dec'=16] {'dec'}, dimensions={0} | all-to-all | bytes 655360 | tf_op jit(solution)/shard_map/all_to_all | solution.py:571
  226.5 3.5 %all-to-all-start.5 = ((f32[16,40,128]{2,1,0:T(8,128)}), f32[16,40,128]{2,1,0:T(8,128)S(1)}, u32[]{:S(2)}, u32[]{:S(2)}) async-start(f32[16,40,128]{2,1,0:T(8,128)} %get-tuple-element.14), calls=%async_computation.5 | async-start | bytes 655360 | tf_op jit(solution)/shard_map/all_to_all | solution.py:571
  230.0 26.9 %shard_map.192 = f32[6,256,256]{2,1,0:T(8,128)} custom-call(f32[6,384,512]{2,1,0:T(8,128)} %get-tuple-element.17.acc_ref), custom_call_target="tpu_custom_call" | custom-call | bytes 40000000 | tf_op jit(solution)/shard_map/pallas_call | solution.py:535
  256.9 1.1 pad_maximum_fusion
  258.1 3.0 %shard_map.191 = f32[32,4356]{1,0:T(8,128)} custom-call(s32[32,1]{1,0:T(8,128)} %copy.22.column_ref, s32[1,32]{1,0:T(1,128)} %constant_dynamic-slice_fusion.row_ref, f32[2560,128]{1,0:T(8,128)} %bitcast.14), custom_call_target="tpu_custom_call" | custom-call | tf_op jit(solution)/shard_map/pallas_call | solution.py:337
  261.1 1.1 copy.24
  (25 shorter events, 1.2 us)
Async XLA Ops:
  36.2 21.3 %copy-start.3 = (s32[512]{0:T(512)S(1)}, s32[512]{0:T(512)}, u32[]{:S(2)}) copy-start(s32[512]{0:T(512)} %param.25) | copy-start | bytes 6148
  36.2 21.3 %copy-start.4 = (s32[512]{0:T(512)S(1)}, s32[512]{0:T(512)}, u32[]{:S(2)}) copy-start(s32[512]{0:T(512)} %param.24) | copy-start | bytes 6148
  36.2 21.3 %copy-start.5 = (s32[512]{0:T(512)S(1)}, s32[512]{0:T(512)}, u32[]{:S(2)}) copy-start(s32[512]{0:T(512)} %param.23) | copy-start | bytes 6148
  53.8 34.6 %all-to-all-start.4 = ((f32[16,112,128]{2,1,0:T(8,128)}), f32[16,112,128]{2,1,0:T(8,128)S(1)}, u32[]{:S(2)}, u32[]{:S(2)}) async-start(f32[16,112,128]{2,1,0:T(8,128)} %bitcast.5), calls=%async_computation.4 | async-start | bytes 1835008 | tf_op jit(solution)/shard_map/all_to_all | solution.py:564
  88.5 30.1 %copy-start.1 = (f32[16,112,128]{2,1,0:T(8,128)}, f32[16,112,128]{2,1,0:T(8,128)S(1)}, u32[]{:S(2)}) copy-start(f32[16,112,128]{2,1,0:T(8,128)S(1)} %all-to-all-done.4.slots_ref) | copy-start | bytes 2752516
  88.5 30.1 %all-to-all-start.2 = ((f32[16,112,128]{2,1,0:T(8,128)}), f32[16,112,128]{2,1,0:T(8,128)S(1)}, u32[]{:S(2)}, u32[]{:S(2)}) async-start(f32[16,112,128]{2,1,0:T(8,128)} %bitcast.3), calls=%async_computation.2 | async-start | bytes 1835008 | tf_op jit(solution)/shard_map/all_to_all | solution.py:564
  118.6 6.6 %copy-start.2 = (f32[16,112,128]{2,1,0:T(8,128)}, f32[16,112,128]{2,1,0:T(8,128)S(1)}, u32[]{:S(2)}) copy-start(f32[16,112,128]{2,1,0:T(8,128)S(1)} %all-to-all-done.2.slots_ref) | copy-start | bytes 2752516
  118.6 33.3 %all-to-all-start.1 = ((f32[16,40,128]{2,1,0:T(8,128)}), f32[16,40,128]{2,1,0:T(8,128)S(1)}, u32[]{:S(2)}, u32[]{:S(2)}) async-start(f32[16,40,128]{2,1,0:T(8,128)} %get-tuple-element.10), calls=%async_computation.1 | async-start | bytes 655360 | tf_op jit(solution)/shard_map/all_to_all | solution.py:571
  151.9 59.9 %all-to-all-start.3 = ((f32[16,40,128]{2,1,0:T(8,128)}), f32[16,40,128]{2,1,0:T(8,128)S(1)}, u32[]{:S(2)}, u32[]{:S(2)}) async-start(f32[16,40,128]{2,1,0:T(8,128)} %get-tuple-element.12), calls=%async_computation.3 | async-start | bytes 655360 | tf_op jit(solution)/shard_map/all_to_all | solution.py:571
  226.5 30.5 %all-to-all-start.5 = ((f32[16,40,128]{2,1,0:T(8,128)}), f32[16,40,128]{2,1,0:T(8,128)S(1)}, u32[]{:S(2)}, u32[]{:S(2)}) async-start(f32[16,40,128]{2,1,0:T(8,128)} %get-tuple-element.14), calls=%async_computation.5 | async-start | bytes 655360 | tf_op jit(solution)/shard_map/all_to_all | solution.py:571
  258.1 3.0 %copy-start = (f32[6,256,256]{2,1,0:T(8,128)S(1)}, f32[6,256,256]{2,1,0:T(8,128)}, u32[]{:S(2)}) copy-start(f32[6,256,256]{2,1,0:T(8,128)} %shard_map.192) | copy-start | bytes 4718596

commit v2 on v1

--- a/solution.py
+++ b/solution.py
@@ -13,6 +13,7 @@
 K = 63
 C = 66
 CAP = 4
+GROUP = 8
 N = 128
 PAIRS = 33
 PAD = 40
@@ -155,8 +156,8 @@
 
     places = []
     patches = []
-    for e in range(2):
-        code = jnp.maximum(meta_ref[step * 2 + e] - 1, 0)
+    for e in range(GROUP):
+        code = jnp.maximum(meta_ref[step * GROUP + e] - 1, 0)
         which = lax.shift_right_logical(code, 16)
         row = lax.bitwise_and(lax.shift_right_logical(code, 8), 255) + (EDGE - K + 1)
         column = lax.bitwise_and(code, 255) + (SIDE - K + 1)
@@ -171,24 +172,24 @@
         patches.append(window)
 
     y = right_wide(jnp.concatenate(patches, axis=0), patch_cols)
-    z = left_three(patch_rows, stacked([y[:N], y[N:]], sign))
+    z = left_three(patch_rows, stacked([y[e * N : e * N + N] for e in range(GROUP)], sign))
 
     pairs = []
-    for e in range(2):
+    for e in range(GROUP):
         x = slots_ref[e, :PSF_ROWS, :]
         both = jnp.concatenate([pltpu.roll(x, 1, 0), x], axis=1)
         pairs.append(pltpu.roll(both, N, 1, stride=2, stride_axis=0)[:, :N])
     high, low = split(jnp.concatenate(pairs, axis=0))
     y = dot(jnp.concatenate([high, low], axis=1), psf_cols[: 2 * N, :]) + dot(high, psf_cols[2 * N :, :])
     y = stacked([jnp.concatenate([y[32 * e : 32 * e + 32, :N], y[32 * e : 32 * e + 32, N:]], axis=0)
-                 for e in range(2)], sign)
+                 for e in range(GROUP)], sign)
     high, low = split(y)
     khat = (dot(psf_rows[:N, :], jnp.concatenate([high, low], axis=0))
             + dot(psf_rows[N:, :N], high))
 
     kernels = []
     spec = []
-    for e in range(2):
+    for e in range(GROUP):
         k = khat[:, e * N : e * N + N]
         rk = pltpu.roll(k, 64, 1)
         k_re = jnp.where(low_half, k, rk)
@@ -201,14 +202,14 @@
     u = left_three(pred_rows, jnp.concatenate(spec, axis=1))
     u = jnp.concatenate(
         [jnp.concatenate([u[:PAD, e * N : e * N + N], u[PAD:, e * N : e * N + N]], axis=1)
-         for e in range(2)], axis=0)
+         for e in range(GROUP)], axis=0)
     predicted = right_three(u, pred_cols)
 
     number = lax.broadcasted_iota(jnp.int32, (PAD, 1), 0)
     last = number == PAIRS - 1
     turn = lax.bitwise_and(lane + 4 * number, N - 1)
     pairs = []
-    for e in range(2):
+    for e in range(GROUP):
         image = pltpu.roll(predicted[e * PAD : e * PAD + PAD], 0, 1, stride=4, stride_axis=0)
         front, rear = image[:, :N], image[:, N:]
         flat = (jnp.where(last, 0.0, front) + pltpu.roll(rear, 1, 0)
@@ -222,18 +223,18 @@
              jnp.where(last, pltpu.roll(resid, PAD - 2, 0), rear)], axis=1))
     v = right_three(jnp.concatenate(pairs, axis=0), res_cols)
     v = [jnp.concatenate([v[e * PAD : e * PAD + PAD, :N], v[e * PAD : e * PAD + PAD, N:]], axis=0)
-         for e in range(2)]
+         for e in range(GROUP)]
     r = left_three(res_rows, stacked(v, sign))
     spec = []
-    for e in range(2):
+    for e in range(GROUP):
         k_re, k_im = kernels[e]
         p = r[:, e * N : e * N + N]
         rp = pltpu.roll(p, 64, 1)
         spec.append(jnp.concatenate(
             [p * k_re - rp * k_im, (rp * k_re + p * k_im) * sign], axis=0))
     u = left_three(back_rows, jnp.concatenate(spec, axis=1))
-    back = right_wide(jnp.concatenate([u[:, :N], u[:, N:]], axis=0), back_cols)
-    for e in range(2):
+    back = right_wide(jnp.concatenate([u[:, e * N : e * N + N] for e in range(GROUP)], axis=0), back_cols)
+    for e in range(GROUP):
         which, row_at, col_at, down, over = places[e]
         image = jnp.concatenate([back[e * N : e * N + N], jnp.zeros((8, N), F32)], axis=0)
         image = pltpu.roll(image, down, 0)
@@ -250,16 +251,16 @@
     number = slots.shape[0]
     first = acc is None
     operands = [slots, ext] + ([] if first else [acc]) + list(tables)
-    in_specs = [pl.BlockSpec((2, SLOT_ROWS, N), lambda i, meta: (i, 0, 0))]
+    in_specs = [pl.BlockSpec((GROUP, SLOT_ROWS, N), lambda i, meta: (i, 0, 0))]
     in_specs += [whole(o.shape) for o in operands[1:]]
     return pl.pallas_call(
         functools.partial(exposure_kernel, first),
         grid_spec=pltpu.PrefetchScalarGridSpec(
             num_scalar_prefetch=1,
-            grid=(number // 2,),
+            grid=(number // GROUP,),
             in_specs=in_specs,
             out_specs=[
-                pl.BlockSpec((2, PAD, N), lambda i, meta: (i, 0, 0)),
+                pl.BlockSpec((GROUP, PAD, N), lambda i, meta: (i, 0, 0)),
                 whole(ext.shape),
             ],
         ),
@@ -279,66 +280,27 @@
     return jnp.concatenate([high, middle, (rest - middle.astype(F32)).astype(BF16)], axis=0)
 
 
-def prepare_kernel(n_dec, column_ref, row_ref, psf_ref, obs_ref, var_ref, out_ref):
-    column, row = column_ref[...], row_ref[...]
+def own_places(packed_ref, own):
+    row = lax.shift_right_logical(packed_ref[pl.ds(own, 1), :], 19)
     count = row.shape[1]
-    slots = CAP * n_dec
-    earlier = lax.broadcasted_iota(jnp.int32, (count, count), 0) < lax.broadcasted_iota(
-        jnp.int32, (count, count), 1)
-    rank = jnp.sum(jnp.where(jnp.logical_and(column == row, earlier), 1, 0), axis=0, keepdims=True)
-    place = rank * n_dec + row
-    chosen = (lax.broadcasted_iota(jnp.int32, (slots, count), 0) == place).astype(F32).astype(BF16)
-    chosen = jnp.concatenate([chosen] * 3, axis=1)
-    for ref, base, rows in ((psf_ref, 0, 32), (obs_ref, OBS_AT, PAD), (var_ref, VAR_AT, PAD)):
-        width = ref.shape[1]
-        for start in range(0, rows, 4):
-            end = min((start + 4) * N, width)
-            if start * N < width:
-                x = ref[:, start * N : end]
-                y = dot(chosen, three(x))
-                if end < (start + 4) * N:
-                    y = jnp.concatenate([y, jnp.zeros((slots, (start + 4) * N - end), F32)], axis=1)
-            else:
-                y = jnp.zeros((slots, 4 * N), F32)
-            for t in range(4):
-                out_ref[pl.ds(base + start + t, slots, stride=SLOT_ROWS), :] = y[:, t * N : t * N + N]
-
-
-def prepare(column, row, psf, obs, var, n_dec):
-    return pl.pallas_call(
-        functools.partial(prepare_kernel, n_dec),
-        out_shape=jax.ShapeDtypeStruct((CAP * n_dec * SLOT_ROWS, N), F32),
-        compiler_params=pltpu.CompilerParams(vmem_limit_bytes=LIMIT),
-    )(column, row, psf, obs, var)
-
-
-def finish_kernel(n_dec, column_ref, row_ref, in_ref, out_ref):
-    column, row = column_ref[...], row_ref[...]
-    count = row.shape[1]
-    slots = CAP * n_dec
-    earlier = lax.broadcasted_iota(jnp.int32, (count, count), 1) < lax.broadcasted_iota(
-        jnp.int32, (count, count), 0)
-    rank = jnp.sum(jnp.where(jnp.logical_and(column == row, earlier), 1, 0), axis=1, keepdims=True)
-    place = rank * n_dec + column
-    chosen = (lax.broadcasted_iota(jnp.int32, (count, slots), 1) == place).astype(F32).astype(BF16)
-    chosen = jnp.concatenate([chosen] * 3, axis=1)
-    width = out_ref.shape[1]
-    for start in range(0, PAD, 4):
-        if start * N >= width:
-            break
-        x = jnp.concatenate(
-            [in_ref[pl.ds(start + t, slots, stride=PAD), :] for t in range(4)], axis=1)
-        y = dot(chosen, three(x))
-        end = min((start + 4) * N, width)
-        out_ref[:, start * N : end] = y[:, : end - start * N]
-
-
-def finish(column, row, landed, n_dec):
-    return pl.pallas_call(
-        functools.partial(finish_kernel, n_dec),
-        out_shape=jax.ShapeDtypeStruct((row.shape[1], C * C), F32),
-        compiler_params=pltpu.CompilerParams(vmem_limit_bytes=LIMIT),
-    )(column, row, landed)
+    first = lax.broadcasted_iota(jnp.int32, (count, count), 0)
+    second = lax.broadcasted_iota(jnp.int32, (count, count), 1)
+    column = jnp.sum(jnp.where(first == second, row, 0), axis=1, keepdims=True)
+    return row, column, first, second
+
+
+def places_of_tile(packed_ref, own):
+    packed = packed_ref[...]
+    count = packed.shape[1]
+    here = lax.shift_right_logical(packed, 19) == own
+    code = lax.bitwise_and(packed, (1 << 19) - 1) + 1
+    first = lax.broadcasted_iota(jnp.int32, (count, count), 0)
+    second = lax.broadcasted_iota(jnp.int32, (count, count), 1)
+    earlier = (first < second).astype(F32).astype(BF16)
+    rank = dot(here.astype(F32).astype(BF16), earlier)
+    return jnp.concatenate(
+        [jnp.sum(jnp.where(jnp.logical_and(here, rank == float(s)), code, 0), axis=1, keepdims=True)
+         for s in range(CAP)], axis=1)
 
 
 def neighbours(n_ra, n_dec):
@@ -348,27 +310,42 @@
     return ra, dec, up, down, right, left
 
 
-def greet(ra, dec, up, down, right, left):
+def greet(n_dec, ra, dec, up, down, right, left):
     barrier = pltpu.get_barrier_semaphore()
-    for other in ((up, dec), (down, dec), (ra, right), (ra, left),
-                  (up, right), (up, left), (down, right), (down, left)):
+    for other in ((up, dec), (down, dec), (up, right), (up, left), (down, right), (down, left)):
         pl.semaphore_signal(barrier, inc=1, device_id=other, device_id_type=MESH)
-    pl.semaphore_wait(barrier, 8)
-
-
-def halo_kernel(n_ra, n_dec, model_ref, ext_ref, to_right, to_left, from_left, from_right, corners,
-                send, recv):
-    ra, dec, up, down, right, left = neighbours(n_ra, n_dec)
-    greet(ra, dec, up, down, right, left)
-    tra, tdec = model_ref.shape[1], model_ref.shape[2]
-    top, side_at = EDGE + tra, SIDE + tdec
-    low_half = lax.broadcasted_iota(jnp.int32, (1, 1, N), 2) < 64
-
+    for d in range(1, n_dec):
+        pl.semaphore_signal(barrier, inc=1, device_id=(ra, lax.rem(dec + d, n_dec)), device_id_type=MESH)
+    pl.semaphore_wait(barrier, n_dec + 5)
+
+
+def edges(n_ra, n_dec, ra, dec):
+    zero, one = jnp.zeros((), F32), jnp.ones((), F32)
+    return (jnp.where(ra > 0, one, zero), jnp.where(ra < n_ra - 1, one, zero),
+            jnp.where(dec > 0, one, zero), jnp.where(dec < n_dec - 1, one, zero))
+
+
+def sender(send, recv):
     def copy(index, src, dst, other):
         return pltpu.make_async_remote_copy(
             src_ref=src, dst_ref=dst, send_sem=send.at[index], recv_sem=recv.at[index],
             device_id=other, device_id_type=MESH)
-
+    return copy
+
+
+def far_first(n_dec):
+    return sorted(range(1, n_dec), key=lambda d: -(min(d // 4, 4 - d // 4) + min(d % 4, 4 - d % 4)))
+
+
+def exchange_kernel(n_ra, n_dec, packed_ref, psf_ref, obs_ref, var_ref, model_ref,
+                    meta_ref, slots_ref, ext_ref,
+                    leaving, to_right, to_left, from_left, from_right, corners, send, recv, send_slot, recv_slot):
+    ra, dec, up, down, right, left = neighbours(n_ra, n_dec)
+    greet(n_dec, ra, dec, up, down, right, left)
+    tra, tdec = model_ref.shape[1], model_ref.shape[2]
+    top, side_at = EDGE + tra, SIDE + tdec
+    low_half = lax.broadcasted_iota(jnp.int32, (1, N), 1) < 64
+    copy = sender(send, recv)
     copies = [
         copy(0, model_ref.at[:, tra - EDGE :, :], ext_ref.at[:, :EDGE, SIDE:side_at], (up, dec)),
         copy(1, model_ref.at[:, :EDGE, :], ext_ref.at[:, top:, SIDE:side_at], (down, dec)),
@@ -377,7 +354,7 @@
         c.start()
     for q in range(3):
         to_right[q] = jnp.where(
-            low_half[0], pltpu.roll(model_ref[2 * q + 1, :, tdec - N :], 64, 1), model_ref[2 * q, :, tdec - N :])
+            low_half, pltpu.roll(model_ref[2 * q + 1, :, tdec - N :], 64, 1), model_ref[2 * q, :, tdec - N :])
     more = [
         copy(2, to_right, from_left, (ra, right)),
         copy(4, to_right.at[:, tra - EDGE :, :], corners.at[0], (up, right)),
@@ -388,7 +365,7 @@
     copies += more
     for q in range(3):
         to_left[q] = jnp.where(
-            low_half[0], model_ref[2 * q, :, :N], pltpu.roll(model_ref[2 * q + 1, :, :N], 64, 1))
+            low_half, model_ref[2 * q, :, :N], pltpu.roll(model_ref[2 * q + 1, :, :N], 64, 1))
     more = [
         copy(3, to_left, from_right, (ra, left)),
         copy(6, to_left.at[:, tra - EDGE :, :], corners.at[2], (up, left)),
@@ -397,15 +374,42 @@
     for c in more:
         c.start()
     copies += more
+
+    row, column, first, second = own_places(packed_ref, dec)
+    count = row.shape[1]
+    slots = CAP * n_dec
+    rank = jnp.sum(jnp.where(jnp.logical_and(column == row, first < second), 1, 0), axis=0, keepdims=True)
+    place = row * CAP + rank
+    chosen = (lax.broadcasted_iota(jnp.int32, (slots, count), 0) == place).astype(F32).astype(BF16)
+    chosen = jnp.concatenate([chosen] * 3, axis=1)
+    for ref, base, rows in ((psf_ref, 0, PSF_ROWS), (obs_ref, OBS_AT, PAD), (var_ref, VAR_AT, PAD)):
+        width = ref.shape[1]
+        for start in range(0, rows, 4):
+            end = min((start + 4) * N, width)
+            if start * N < width:
+                y = dot(chosen, three(ref[:, start * N : end]))
+                if end < (start + 4) * N:
+                    y = jnp.concatenate([y, jnp.zeros((slots, (start + 4) * N - end), F32)], axis=1)
+            else:
+                y = jnp.zeros((slots, 4 * N), F32)
+            for t in range(4):
+                leaving[pl.ds(base + start + t, slots, stride=SLOT_ROWS), :] = y[:, t * N : t * N + N]
+    size = CAP * SLOT_ROWS
+    slot_copy = sender(send_slot, recv_slot)
+    moves = []
+    for d in far_first(n_dec):
+        other = lax.rem(dec + d, n_dec)
+        moves.append(slot_copy(
+            d, leaving.at[pl.ds(pl.multiple_of(other * size, 8), size), :],
+            slots_ref.at[pl.ds(pl.multiple_of(dec * size, 8), size), :], (ra, other)))
+        moves[-1].start()
+    here = pl.ds(pl.multiple_of(dec * size, 8), size)
+    slots_ref[here, :] = leaving[here, :]
     ext_ref[:, EDGE:top, SIDE:side_at] = model_ref[...]
+    meta_ref[...] = places_of_tile(packed_ref, dec)
     for c in copies:
         c.wait()
-    zero = jnp.zeros((), F32)
-    one = jnp.ones((), F32)
-    in_left = jnp.where(dec > 0, one, zero)
-    in_right = jnp.where(dec < n_dec - 1, one, zero)
-    in_low = jnp.where(ra > 0, one, zero)
-    in_high = jnp.where(ra < n_ra - 1, one, zero)
+    in_low, in_high, in_left, in_right = edges(n_ra, n_dec, ra, dec)
 
     @pl.when(ra == 0)
     def _():
@@ -427,37 +431,44 @@
             value = src[...] * scale
             ext_ref[2 * q, rows, col] = value
             ext_ref[2 * q + 1, rows, col] = pltpu.roll(value, 64, 1)
-
-
-def halo(model, n_ra, n_dec):
+    for c in moves:
+        c.wait()
+
+
+def vmem(count):
+    return [pl.BlockSpec(memory_space=pltpu.VMEM)] * count
+
+
+def exchange(packed, psf, obs, var, model, n_ra, n_dec):
     bands, tra, tdec = model.shape
     strip = pltpu.VMEM((3, tra, N), F32)
+    size = n_dec * CAP * SLOT_ROWS
     return pl.pallas_call(
-        functools.partial(halo_kernel, n_ra, n_dec),
-        out_shape=jax.ShapeDtypeStruct((bands, tra + 2 * EDGE, tdec + 2 * SIDE), F32),
-        in_specs=[pl.BlockSpec(memory_space=pltpu.VMEM)],
-        out_specs=pl.BlockSpec(memory_space=pltpu.VMEM),
-        scratch_shapes=[strip, strip, strip, strip, pltpu.VMEM((4, 3, EDGE, N), F32),
-                        pltpu.SemaphoreType.DMA((8,)), pltpu.SemaphoreType.DMA((8,))],
+        functools.partial(exchange_kernel, n_ra, n_dec),
+        out_shape=[
+            jax.ShapeDtypeStruct((n_dec, CAP), jnp.int32),
+            jax.ShapeDtypeStruct((size, N), F32),
+            jax.ShapeDtypeStruct((bands, tra + 2 * EDGE, tdec + 2 * SIDE), F32),
+        ],
+        in_specs=vmem(5),
+        out_specs=vmem(3),
+        scratch_shapes=[pltpu.VMEM((size, N), F32), strip, strip, strip, strip, pltpu.VMEM((4, 3, EDGE, N), F32),
+                        pltpu.SemaphoreType.DMA((8,)), pltpu.SemaphoreType.DMA((8,)),
+                        pltpu.SemaphoreType.DMA((n_dec,)), pltpu.SemaphoreType.DMA((n_dec,))],
         compiler_params=pltpu.CompilerParams(
             collective_id=0, has_side_effects=True, vmem_limit_bytes=LIMIT),
         cost_estimate=pl.CostEstimate(flops=0, bytes_accessed=40_000_000, transcendentals=0),
-    )(model)
-
-
-def fold_kernel(n_ra, n_dec, acc_ref, out_ref, to_right, to_left, from_left, from_right, out_corners,
-                corners, from_up, from_down, send, recv):
+    )(packed, psf, obs, var, model)
+
+
+def return_kernel(n_ra, n_dec, packed_ref, resid_ref, acc_ref, residual_ref, out_ref, landed, to_right, to_left,
+                  from_left, from_right, out_corners, corners, from_up, from_down, send, recv, send_slot, recv_slot):
     ra, dec, up, down, right, left = neighbours(n_ra, n_dec)
-    greet(ra, dec, up, down, right, left)
+    greet(n_dec, ra, dec, up, down, right, left)
     tra, tdec = out_ref.shape[1], out_ref.shape[2]
     top, side_at = EDGE + tra, SIDE + tdec
     low_half = lax.broadcasted_iota(jnp.int32, (1, N), 1) < 64
-
-    def copy(index, src, dst, other):
-        return pltpu.make_async_remote_copy(
-            src_ref=src, dst_ref=dst, send_sem=send.at[index], recv_sem=recv.at[index],
-            device_id=other, device_id_type=MESH)
-
+    copy = sender(send, recv)
     copies = [
         copy(0, acc_ref.at[:, :EDGE, SIDE:side_at], from_up, (down, dec)),
         copy(1, acc_ref.at[:, top:, SIDE:side_at], from_down, (up, dec)),
@@ -496,15 +507,20 @@
     for c in more:
         c.start()
     copies += more
+    size = CAP * PAD
+    slot_copy = sender(send_slot, recv_slot)
+    moves = []
+    here = pl.ds(pl.multiple_of(dec * size, 8), size)
+    for d in far_first(n_dec):
+        other = lax.rem(dec + d, n_dec)
+        moves.append(slot_copy(
+            d, resid_ref.at[pl.ds(pl.multiple_of(other * size, 8), size), :], landed.at[here, :], (ra, other)))
+        moves[-1].start()
+    landed[here, :] = resid_ref[here, :]
     out_ref[...] = acc_ref[:, EDGE:top, SIDE:side_at]
     for c in copies:
         c.wait()
-    zero = jnp.zeros((), F32)
-    one = jnp.ones((), F32)
-    in_left = jnp.where(dec > 0, one, zero)
-    in_right = jnp.where(dec < n_dec - 1, one, zero)
-    in_low = jnp.where(ra > 0, one, zero)
-    in_high = jnp.where(ra < n_ra - 1, one, zero)
+    in_low, in_high, in_left, in_right = edges(n_ra, n_dec, ra, dec)
     out_ref[:, tra - EDGE :, :] += from_up[...] * in_high
     out_ref[:, :EDGE, :] += from_down[...] * in_low
     every, low_rows, high_rows = slice(0, tra), slice(0, EDGE), slice(tra - EDGE, tra)
@@ -525,53 +541,55 @@
                 cols, keep = slice(0, N), low_half
             out_ref[2 * q, rows, cols] += jnp.where(keep, value, 0.0)
             out_ref[2 * q + 1, rows, cols] += jnp.where(keep, other, 0.0)
-
-
-def fold(acc, n_ra, n_dec):
+    for c in moves:
+        c.wait()
+    row, column, first, second = own_places(packed_ref, dec)
+    count = row.shape[1]
+    slots = CAP * n_dec
+    rank = jnp.sum(jnp.where(jnp.logical_and(column == row, second < first), 1, 0), axis=1, keepdims=True)
+    place = column * CAP + rank
+    chosen = (lax.broadcasted_iota(jnp.int32, (count, slots), 1) == place).astype(F32).astype(BF16)
+    chosen = jnp.concatenate([chosen] * 3, axis=1)
+    width = residual_ref.shape[1]
+    for start in range(0, PAD, 4):
+        if start * N >= width:
+            break
+        x = jnp.concatenate(
+            [landed[pl.ds(start + t, slots, stride=PAD), :] for t in range(4)], axis=1)
+        y = dot(chosen, three(x))
+        end = min((start + 4) * N, width)
+        residual_ref[:, start * N : end] = y[:, : end - start * N]
+
+
+def give_back(packed, resid, acc, n_ra, n_dec):
     bands, tra, tdec = acc.shape[0], acc.shape[1] - 2 * EDGE, acc.shape[2] - 2 * SIDE
     strip = pltpu.VMEM((3, tra, N), F32)
     corner = pltpu.VMEM((4, 3, EDGE, N), F32)
     band = pltpu.VMEM((bands, EDGE, tdec), F32)
+    size = n_dec * CAP * PAD
     return pl.pallas_call(
-        functools.partial(fold_kernel, n_ra, n_dec),
-        out_shape=jax.ShapeDtypeStruct((bands, tra, tdec), F32),
-        in_specs=[pl.BlockSpec(memory_space=pltpu.VMEM)],
-        out_specs=pl.BlockSpec(memory_space=pltpu.VMEM),
-        scratch_shapes=[strip, strip, strip, strip, corner, corner, band, band,
-                        pltpu.SemaphoreType.DMA((8,)), pltpu.SemaphoreType.DMA((8,))],
+        functools.partial(return_kernel, n_ra, n_dec),
+        out_shape=[jax.ShapeDtypeStruct((packed.shape[1], C * C), F32),
+                   jax.ShapeDtypeStruct((bands, tra, tdec), F32)],
+        in_specs=vmem(3),
+        out_specs=vmem(2),
+        scratch_shapes=[pltpu.VMEM((size, N), F32), strip, strip, strip, strip, corner, corner, band, band,
+                        pltpu.SemaphoreType.DMA((8,)), pltpu.SemaphoreType.DMA((8,)),
+                        pltpu.SemaphoreType.DMA((n_dec,)), pltpu.SemaphoreType.DMA((n_dec,))],
         compiler_params=pltpu.CompilerParams(
             collective_id=1, has_side_effects=True, vmem_limit_bytes=LIMIT),
         cost_estimate=pl.CostEstimate(flops=0, bytes_accessed=40_000_000, transcendentals=0),
-    )(acc)
+    )(packed, resid, acc)
 
 
 def body(model, observed, inv_var, psf, target_dec, band, offset_ra, offset_dec):
     n_ra, n_dec = lax.axis_size("ra"), lax.axis_size("dec")
-    own = lax.axis_index("dec")
     e_dev = observed.shape[0]
-    targets = target_dec[:, 0].reshape(n_dec, e_dev)
-    row = lax.dynamic_slice_in_dim(targets, own, 1, 0)
-    column = lax.dynamic_slice_in_dim(target_dec, own * e_dev, e_dev, 0)
-    slots = prepare(column, row, psf, observed, inv_var, n_dec)
-    slots = slots.reshape(CAP, n_dec, SLOT_ROWS, N)
-    here = targets == own
-    order = jnp.arange(e_dev, dtype=jnp.int32)
-    rank = jnp.sum(jnp.where(here[:, None, :] & (order[None, :] < order[:, None])[None], 1, 0), axis=2)
-    code = ((band * 256 + offset_ra) * 256 + offset_dec + 1).reshape(n_dec, e_dev)
-    meta = jnp.sum(
-        jnp.where(here[None] & (rank[None] == jnp.arange(CAP, dtype=jnp.int32)[:, None, None]), code[None], 0),
-        axis=2)
-    arrived = [lax.all_to_all(slots[s], "dec", 0, 0, tiled=True) for s in range(CAP)]
-    ext = halo(model, n_ra, n_dec)
+    packed = (((target_dec[:, 0] * 8 + band) * 256 + offset_ra) * 256 + offset_dec).reshape(n_dec, e_dev)
+    meta, slots, ext = exchange(packed, psf, observed, inv_var, model, n_ra, n_dec)
     tables = [jnp.asarray(t) for t in make_tables()]
-    acc = None
-    landed = []
-    for s in range(CAP):
-        resid, acc = run_exposures(meta[s], arrived[s], ext, acc, tables)
-        landed.append(lax.all_to_all(resid, "dec", 0, 0, tiled=True))
-    gradient = fold(acc, n_ra, n_dec)
-    landed = jnp.concatenate(landed, axis=0).reshape(CAP * n_dec * PAD, N)
-    residual = finish(column, row, landed, n_dec)
+    resid, acc = run_exposures(meta.reshape(-1), slots.reshape(n_dec * CAP, SLOT_ROWS, N), ext, None, tables)
+    residual, gradient = give_back(packed, resid.reshape(n_dec * CAP * PAD, N), acc, n_ra, n_dec)
     return residual, gradient
 
 

time: 263 us -> 160 us (0.61)
  blocking collectives: 55.7 us -> 0 us
  starting transfers between devices: 24.1 us -> 0 us
  Pallas kernels: 171 us -> 151 us
    pallas_call x4 -> x1, Pallas kernels: 105 us -> 36.9 us  [run_exposures(): pl.pallas_call(functools.partial(exposure_kernel, first), grid_spec=pltpu...]
    all_to_all x3 -> x0, blocking collectives: 55.7 us -> none  [the longest x2 41 us: body(): lax.all_to_all(slots[s], 'dec', 0, 0, tiled=True)]
    pallas_call x4 -> x2, Pallas kernels: 65.6 us -> 114 us  [the longest x1 73.4 us: exchange(): pl.pallas_call(functools.partial(exchange_kernel, n_ra, n_dec), out_shape...]
    all_to_all x5 -> x0, starting transfers between devices: 24.1 us -> none  [the longest x3 16.8 us: body(): landed.append(lax.all_to_all(resid, 'dec', 0, 0, tiled=True))]
    slice x1 -> x0, local copies, waits for them, and re-layouts: 3.47 us -> none  [body(): slots[s]]
  transfers between devices with their start and end apart: 5 -> 0, of which waited for: 0 -> 0; matrix products, arithmetic and copies ran while one was open for 0% -> 0% of each run, Pallas kernels for 62% -> 0%
where the time goes in v2:
time: 160 us
  Pallas kernels  151 us (94%)
  local copies, waits for them, and re-layouts  6.67 us (4%)
    pallas_call x1, Pallas kernels, exchange(): pl.pallas_call(functools.partial(exchange_kernel, n_ra, n_dec), out_shape...  73.4 us
    pallas_call x1, Pallas kernels, give_back(): pl.pallas_call(functools.partial(return_kernel, n_ra, n_dec), out_shape=[...  41 us
    pallas_call x1, Pallas kernels, run_exposures(): pl.pallas_call(functools.partial(exposure_kernel, first), grid_spec=pltpu...  36.9 us
    unnamed x2, local copies, waits for them, and re-layouts  4.64 us

profile of v2, /device:TPU:1, one launch (start us, length us, event | category | flops | bytes accessed | tf_op | source)
XLA Modules:
  0.0 160.1 jit_solution(15999238873465173118)
XLA Ops:
  0.6 0.7 broadcast_multiply_fusion
  1.3 0.7 multiply_add_fusion
  2.0 0.7 reshape.18.packed_ref
  2.7 73.4 %shard_map.185 = (s32[16,4]{1,0:T(8,128)}, f32[7168,128]{1,0:T(8,128)}, f32[6,384,512]{2,1,0:T(8,128)}) custom-call(s32[16,32]{1,0:T(8,128)} %reshape.18.packed_ref, f32[32,3969]{1,0:T(8,128)} %psf_ref.1, f32[32,4356]{1,0:T(8,128)} %obs_ref.1, f32[32,4356]{1,0:T(8,128)} %var_ref.1, f32[6,256,256]{2,1,0:T(8,128)} %model_ref.1), custom_call_target="tpu_custom_call" | custom-call | bytes 40000000 | tf_op jit(solution)/shard_map/pallas_call | solution.py:446
  76.2 1.4 reshape.19.meta_ref
  77.5 36.9 %shard_map.186 = (f32[64,40,128]{2,1,0:T(8,128)}, f32[6,384,512]{2,1,0:T(8,128)}) custom-call(s32[64]{0:T(128)} %reshape.19.meta_ref, f32[64,112,128]{2,1,0:T(8,128)} %bitcast.5, f32[6,384,512]{2,1,0:T(8,128)} %get-tuple-element.9.ext_ref, bf16[256,256]{1,0:T(8,128)(2,1)} %constant.24.clone.refs_0_, bf16[256,256]{1,0:T(8,128)(2,1)} %constant.25.clone.refs_1_, ...), custom_call_target="tpu_custom_call" | custom-call | flops 12800000000 | bytes 12000000 | tf_op jit(solution)/shard_map/pallas_call | solution.py:256
  114.4 41.0 %shard_map.187 = (f32[32,4356]{1,0:T(8,128)}, f32[6,256,256]{2,1,0:T(8,128)}) custom-call(s32[16,32]{1,0:T(8,128)} %reshape.18.packed_ref, f32[2560,128]{1,0:T(8,128)} %bitcast.3, f32[6,384,512]{2,1,0:T(8,128)} %get-tuple-element.11.acc_ref), custom_call_target="tpu_custom_call" | custom-call | bytes 40000000 | tf_op jit(solution)/shard_map/pallas_call | solution.py:570
  155.5 1.9 %copy.22 = f32[32,4356]{1,0:T(8,128)} copy(f32[32,4356]{1,0:T(8,128)} %get-tuple-element.14) | data formatting | bytes 1115136
  157.4 2.7 %copy.23 = f32[6,256,256]{2,1,0:T(8,128)} copy(f32[6,256,256]{2,1,0:T(8,128)} %get-tuple-element.15) | data formatting | bytes 3145728

commit v3 on v2

v3 whole, which is shorter than its diff:
```python
import functools
import math

import jax
import jax.numpy as jnp
import ml_dtypes
import numpy as np
from jax import lax
from jax.experimental import pallas as pl
from jax.experimental.pallas import tpu as pltpu
from jax.sharding import PartitionSpec as P

K = 63
C = 66
CAP = 4
GROUP = 8
N = 128
PAIRS = 33
PAD = 40
PSF_ROWS = 32
EDGE = 64
SIDE = 128
LIMIT = 60 * 1024 * 1024
MESH = pl.DeviceIdType.MESH
F32 = jnp.float32
BF16 = jnp.bfloat16


def np_split(table):
    high = table.astype(np.float32).astype(ml_dtypes.bfloat16)
    low = (table - high.astype(np.float64)).astype(np.float32).astype(ml_dtypes.bfloat16)
    return high, low


def make_tables():
    theta = 2.0 * math.pi * (np.arange(64) + 0.5) / N

    def to_freq(columns):
        angle = np.asarray(columns)[:, None] * theta[None, :]
        return np.concatenate([np.cos(angle), -np.sin(angle)], axis=1)

    def rows_cs(out_index, in_index, sign):
        angle = 2.0 * math.pi * ((out_index[:, None] * in_index[None, :]) % N) / N
        return np.cos(angle), sign * np.sin(angle)

    full = np.arange(N)
    zero = np.zeros((N, N))
    zero16 = zero.astype(ml_dtypes.bfloat16)

    def wide(table):
        high, low = np_split(table)
        return np.block([[high, low], [high, zero16]])

    patch_cols = wide(to_freq(full))
    psf_cols = np.zeros((N, 2 * N))
    psf_cols[:K, :N] = to_freq(np.arange(K))
    psf_cols[K : 2 * K, N:] = to_freq(np.arange(K))
    psf_h, psf_l = np_split(psf_cols)
    psf_cols = np.concatenate([psf_h, psf_h, psf_l], axis=0)

    def left(out_index, in_index, sign, keep_in=None, keep_out=None):
        cosine, sine = rows_cs(out_index, in_index, sign)
        table = np.concatenate([cosine, sine], axis=1)
        if keep_in is not None:
            table = table * np.concatenate([keep_in, keep_in])[None, :]
        if keep_out is not None:
            table = table * keep_out[:, None]
        return np.concatenate(np_split(table), axis=0)

    patch_rows = left(full, full, 1.0)
    psf_index = np.concatenate([2 * np.arange(32), 2 * np.arange(32) + 1])
    psf_rows = left(full, psf_index, 1.0, keep_in=(psf_index < K).astype(np.float64))
    within = (np.arange(PAD) < PAIRS).astype(np.float64)
    inner_keep = np.concatenate([within, within])
    inner_index = np.concatenate([K - 1 + 2 * np.arange(PAD), K + 2 * np.arange(PAD)])
    pred_rows = left(inner_index, full, -1.0, keep_out=inner_keep)
    res_rows = left(full, inner_index, 1.0, keep_in=inner_keep)
    back_rows = left(full, full, -1.0)
    scale = 2.0 / (N * N)
    inner_cols = K - 1 + np.arange(C)
    pred_cols = np.zeros((2 * N, 2 * N))
    pred_cols[:N, :C] = scale * to_freq(inner_cols).T
    pred_cols[N:, C : 2 * C] = scale * to_freq(inner_cols).T
    pred_cols = np.concatenate(np_split(pred_cols), axis=0)
    res_cols = np.zeros((2 * N, 2 * N))
    res_cols[:C, :N] = to_freq(inner_cols)
    res_cols[C : 2 * C, N:] = to_freq(inner_cols)
    res_cols = np.concatenate(np_split(res_cols), axis=0)
    back_cols = wide(scale * to_freq(full).T)
    psf_rows = np.concatenate([np.concatenate([psf_rows[:N], psf_rows[:N]], axis=1),
                               np.concatenate([psf_rows[N:], np.zeros_like(psf_rows[N:])], axis=1)], axis=0)
    return (patch_cols, patch_rows, psf_cols, psf_rows, pred_rows, pred_cols, res_cols, res_rows,
            back_rows, back_cols)


def split(x):
    high = x.astype(BF16)
    return high, (x - high.astype(F32)).astype(BF16)


def dot(a, b):
    return jnp.dot(a, b, preferred_element_type=F32)


def right_wide(x, table_ref):
    high, low = split(x)
    both = dot(jnp.concatenate([high, low], axis=1), table_ref[...])
    return both[:, :N] + both[:, N:]


def right_three(x, table_ref):
    high, low = split(x)
    depth = x.shape[1]
    return (dot(high, table_ref[:depth, :]) + dot(low, table_ref[:depth, :])
            + dot(high, table_ref[depth:, :]))


def left_three(table_ref, x):
    rows = table_ref.shape[0] // 2
    high, low = split(x)
    both = dot(table_ref[...], high)
    return both[:rows] + both[rows:] + dot(table_ref[:rows, :], low)


def turned(y, sign):
    return pltpu.roll(y, 64, 1) * sign


def stacked(parts, sign):
    return jnp.concatenate(
        [jnp.concatenate([y, turned(y, sign)], axis=0) for y in parts], axis=1)


def lanes():
    lane = lax.broadcasted_iota(jnp.int32, (1, N), 1)
    return lane, jnp.where(lane < 64, 1.0, -1.0).astype(F32), lane < 64


def place_of(code):
    code = jnp.maximum(code - 1, 0)
    which = lax.shift_right_logical(code, 16)
    row = lax.bitwise_and(lax.shift_right_logical(code, 8), 255) + (EDGE - K + 1)
    column = lax.bitwise_and(code, 255) + (SIDE - K + 1)
    row_at = pl.multiple_of(lax.shift_left(lax.shift_right_logical(row, 3), 3), 8)
    col_at = pl.multiple_of(lax.shift_left(lax.shift_right_logical(column, 7), 7), 128)
    return which, row_at, col_at, row - row_at, column - col_at


def halves(k, low_half):
    rk = pltpu.roll(k, 64, 1)
    return jnp.where(low_half, k, rk), jnp.where(low_half, -rk, k)


def predict(patches, psfs, tables):
    patch_cols, patch_rows, psf_cols, psf_rows, pred_rows, pred_cols = tables
    count = len(patches)
    lane, sign, low_half = lanes()
    y = right_wide(jnp.concatenate(patches, axis=0), patch_cols)
    z = left_three(patch_rows, stacked([y[e * N : e * N + N] for e in range(count)], sign))
    pairs = []
    for x in psfs:
        both = jnp.concatenate([pltpu.roll(x, 1, 0), x], axis=1)
        pairs.append(pltpu.roll(both, N, 1, stride=2, stride_axis=0)[:, :N])
    high, low = split(jnp.concatenate(pairs, axis=0))
    y = dot(jnp.concatenate([high, low], axis=1), psf_cols[: 2 * N, :]) + dot(high, psf_cols[2 * N :, :])
    y = stacked([jnp.concatenate([y[32 * e : 32 * e + 32, :N], y[32 * e : 32 * e + 32, N:]], axis=0)
                 for e in range(count)], sign)
    high, low = split(y)
    khat = (dot(psf_rows[:N, :], jnp.concatenate([high, low], axis=0))
            + dot(psf_rows[N:, :N], high))
    khat = [khat[:, e * N : e * N + N] for e in range(count)]
    spec = []
    for e in range(count):
        k_re, k_im = halves(khat[e], low_half)
        p = z[:, e * N : e * N + N]
        rp = pltpu.roll(p, 64, 1)
        spec.append(jnp.concatenate(
            [p * k_re + rp * k_im, (rp * k_re - p * k_im) * sign], axis=0))
    u = left_three(pred_rows, jnp.concatenate(spec, axis=1))
    u = jnp.concatenate(
        [jnp.concatenate([u[:PAD, e * N : e * N + N], u[PAD:, e * N : e * N + N]], axis=1)
         for e in range(count)], axis=0)
    predicted = right_three(u, pred_cols)
    last = lax.broadcasted_iota(jnp.int32, (PAD, 1), 0) == PAIRS - 1
    flat = []
    for e in range(count):
        image = pltpu.roll(predicted[e * PAD : e * PAD + PAD], 0, 1, stride=4, stride_axis=0)
        front, rear = image[:, :N], image[:, N:]
        flat.append(jnp.where(last, 0.0, front) + pltpu.roll(rear, 1, 0)
                    + pltpu.roll(jnp.where(last, front, 0.0), 2, 0))
    return khat, flat


def adjoint(resids, khat, tables):
    res_cols, res_rows, back_rows, back_cols = tables
    count = len(resids)
    lane, sign, low_half = lanes()
    number = lax.broadcasted_iota(jnp.int32, (PAD, 1), 0)
    last = number == PAIRS - 1
    turn = lax.bitwise_and(lane + 4 * number, N - 1)
    pairs = []
    for resid in resids:
        front = jnp.take_along_axis(resid, turn, axis=1, mode="promise_in_bounds")
        rear = jnp.take_along_axis(pltpu.roll(resid, PAD - 1, 0), turn, axis=1, mode="promise_in_bounds")
        pairs.append(jnp.concatenate(
            [jnp.where(lane + 4 * number < N, front, rear),
             jnp.where(last, pltpu.roll(resid, PAD - 2, 0), rear)], axis=1))
    v = right_three(jnp.concatenate(pairs, axis=0), res_cols)
    v = [jnp.concatenate([v[e * PAD : e * PAD + PAD, :N], v[e * PAD : e * PAD + PAD, N:]], axis=0)
         for e in range(count)]
    r = left_three(res_rows, stacked(v, sign))
    spec = []
    for e in range(count):
        k_re, k_im = halves(khat[e], low_half)
        p = r[:, e * N : e * N + N]
        rp = pltpu.roll(p, 64, 1)
        spec.append(jnp.concatenate(
            [p * k_re - rp * k_im, (rp * k_re + p * k_im) * sign], axis=0))
    u = left_three(back_rows, jnp.concatenate(spec, axis=1))
    back = right_wide(jnp.concatenate([u[:, e * N : e * N + N] for e in range(count)], axis=0), back_cols)
    return [back[e * N : e * N + N] for e in range(count)]


def three(x):
    high = x.astype(BF16)
    rest = x - high.astype(F32)
    middle = rest.astype(BF16)
    return jnp.concatenate([high, middle, (rest - middle.astype(F32)).astype(BF16)], axis=0)


def own_places(packed_ref, own):
    row = lax.shift_right_logical(packed_ref[pl.ds(own, 1), :], 19)
    count = row.shape[1]
    first = lax.broadcasted_iota(jnp.int32, (count, count), 0)
    second = lax.broadcasted_iota(jnp.int32, (count, count), 1)
    column = jnp.sum(jnp.where(first == second, row, 0), axis=1, keepdims=True)
    return row, column, first, second


def places_of_tile(packed_ref, own):
    packed = packed_ref[...]
    count = packed.shape[1]
    here = lax.shift_right_logical(packed, 19) == own
    code = lax.bitwise_and(packed, (1 << 19) - 1) + 1
    first = lax.broadcasted_iota(jnp.int32, (count, count), 0)
    second = lax.broadcasted_iota(jnp.int32, (count, count), 1)
    earlier = (first < second).astype(F32).astype(BF16)
    rank = dot(here.astype(F32).astype(BF16), earlier)
    return jnp.concatenate(
        [jnp.sum(jnp.where(jnp.logical_and(here, rank == float(s)), code, 0), axis=1, keepdims=True)
         for s in range(CAP)], axis=1)


def neighbours(n_ra, n_dec):
    ra, dec = lax.axis_index("ra"), lax.axis_index("dec")
    up, down = lax.rem(ra + 1, n_ra), lax.rem(ra + n_ra - 1, n_ra)
    right, left = lax.rem(dec + 1, n_dec), lax.rem(dec + n_dec - 1, n_dec)
    return ra, dec, up, down, right, left


def greet(n_dec, ra, dec, up, down, right, left):
    barrier = pltpu.get_barrier_semaphore()
    for other in ((up, dec), (down, dec), (up, right), (up, left), (down, right), (down, left)):
        pl.semaphore_signal(barrier, inc=1, device_id=other, device_id_type=MESH)
    for d in range(1, n_dec):
        pl.semaphore_signal(barrier, inc=1, device_id=(ra, lax.rem(dec + d, n_dec)), device_id_type=MESH)
    pl.semaphore_wait(barrier, n_dec + 5)


def greet_near(ra, dec, up, down, right, left):
    barrier = pltpu.get_barrier_semaphore()
    for other in ((up, dec), (down, dec), (ra, right), (ra, left),
                  (up, right), (up, left), (down, right), (down, left)):
        pl.semaphore_signal(barrier, inc=1, device_id=other, device_id_type=MESH)
    pl.semaphore_wait(barrier, 8)


def edges(n_ra, n_dec, ra, dec):
    zero, one = jnp.zeros((), F32), jnp.ones((), F32)
    return (jnp.where(ra > 0, one, zero), jnp.where(ra < n_ra - 1, one, zero),
            jnp.where(dec > 0, one, zero), jnp.where(dec < n_dec - 1, one, zero))


def sender(send, recv):
    def copy(index, src, dst, other):
        return pltpu.make_async_remote_copy(
            src_ref=src, dst_ref=dst, send_sem=send.at[index], recv_sem=recv.at[index],
            device_id=other, device_id_type=MESH)
    return copy


def rows_of(index, size):
    return pl.ds(pl.multiple_of(index * size, 8), size)


def slot_chooser(packed_ref, dec, n_dec):
    row, column, first, second = own_places(packed_ref, dec)
    count = row.shape[1]
    slots = CAP * n_dec
    rank = jnp.sum(jnp.where(jnp.logical_and(column == row, first < second), 1, 0), axis=0, keepdims=True)
    place = row * CAP + rank
    chosen = (lax.broadcasted_iota(jnp.int32, (slots, count), 0) == place).astype(F32).astype(BF16)
    return jnp.concatenate([chosen] * 3, axis=1)


def to_slots(chosen, ref, out_ref, rows):
    width, slots = ref.shape[1], chosen.shape[0]
    for start in range(0, rows, 4):
        end = min((start + 4) * N, width)
        if start * N < width:
            y = dot(chosen, three(ref[:, start * N : end]))
            if end < (start + 4) * N:
                y = jnp.concatenate([y, jnp.zeros((slots, (start + 4) * N - end), F32)], axis=1)
        else:
            y = jnp.zeros((slots, 4 * N), F32)
        for t in range(4):
            out_ref[pl.ds(start + t, slots, stride=rows), :] = y[:, t * N : t * N + N]


def exchange_kernel(n_ra, n_dec, packed_ref, psf_ref, model_ref, psf_in, ext_ref,
                    to_right, to_left, from_left, from_right, corners, psf_out, send, recv, send_psf, recv_psf):
    ra, dec, up, down, right, left = neighbours(n_ra, n_dec)
    greet(n_dec, ra, dec, up, down, right, left)
    tra, tdec = model_ref.shape[1], model_ref.shape[2]
    top = EDGE + tra
    low_half = lax.broadcasted_iota(jnp.int32, (1, N), 1) < 64
    copy = sender(send, recv)
    copies = [
        copy(8 * t, model_ref.at[:, tra - EDGE :, t * N : t * N + N], ext_ref.at[:, 1 + t, :EDGE, :], (up, dec))
        for t in range(2)
    ] + [
        copy(1 + 8 * t, model_ref.at[:, :EDGE, t * N : t * N + N], ext_ref.at[:, 1 + t, top:, :], (down, dec))
        for t in range(2)
    ]
    for c in copies:
        c.start()
    for q in range(3):
        to_right[q] = jnp.where(
            low_half, pltpu.roll(model_ref[2 * q + 1, :, tdec - N :], 64, 1), model_ref[2 * q, :, tdec - N :])
    more = [
        copy(2, to_right, from_left, (ra, right)),
        copy(4, to_right.at[:, tra - EDGE :, :], corners.at[0], (up, right)),
        copy(5, to_right.at[:, :EDGE, :], corners.at[1], (down, right)),
    ]
    for c in more:
        c.start()
    copies += more
    for q in range(3):
        to_left[q] = jnp.where(
            low_half, model_ref[2 * q, :, :N], pltpu.roll(model_ref[2 * q + 1, :, :N], 64, 1))
    more = [
        copy(3, to_left, from_right, (ra, left)),
        copy(6, to_left.at[:, tra - EDGE :, :], corners.at[2], (up, left)),
        copy(7, to_left.at[:, :EDGE, :], corners.at[3], (down, left)),
    ]
    for c in more:
        c.start()
    copies += more

    def psf_move(d):
        tile = lax.rem(dec + d, n_dec)
        return sender(send_psf, recv_psf)(
            d, psf_out.at[rows_of(tile, CAP * PSF_ROWS), :], psf_in.at[rows_of(dec, CAP * PSF_ROWS), :], (ra, tile))

    to_slots(slot_chooser(packed_ref, dec, n_dec), psf_ref, psf_out, PSF_ROWS)

    def start_psf(d, carry):
        psf_move(d).start()
        return carry

    lax.fori_loop(1, n_dec, start_psf, 0)
    psf_in[rows_of(dec, CAP * PSF_ROWS), :] = psf_out[rows_of(dec, CAP * PSF_ROWS), :]
    for t in range(2):
        ext_ref[:, 1 + t, EDGE:top, :] = model_ref[:, :, t * N : t * N + N]
    for c in copies:
        c.wait()
    in_low, in_high, in_left, in_right = edges(n_ra, n_dec, ra, dec)

    @pl.when(ra == 0)
    def _():
        ext_ref[:, 1:3, :EDGE, :] = jnp.zeros((ext_ref.shape[0], 2, EDGE, N), F32)

    @pl.when(ra == n_ra - 1)
    def _():
        ext_ref[:, 1:3, top:, :] = jnp.zeros((ext_ref.shape[0], 2, EDGE, N), F32)

    for q in range(3):
        for src, rows, col, scale in (
            (from_left.at[q], slice(EDGE, top), 0, in_left),
            (from_right.at[q], slice(EDGE, top), 3, in_right),
            (corners.at[0, q], slice(0, EDGE), 0, in_low * in_left),
            (corners.at[1, q], slice(top, top + EDGE), 0, in_high * in_left),
            (corners.at[2, q], slice(0, EDGE), 3, in_low * in_right),
            (corners.at[3, q], slice(top, top + EDGE), 3, in_high * in_right),
        ):
            value = src[...] * scale
            ext_ref[2 * q, col, rows, :] = value
            ext_ref[2 * q + 1, col, rows, :] = pltpu.roll(value, 64, 1)

    def end_psf(d, carry):
        psf_move(d).wait()
        return carry

    lax.fori_loop(1, n_dec, end_psf, 0)


def photometry_kernel(n_ra, n_dec, packed_ref, obs_ref, var_ref, psf_in, patch_ref, *refs):
    tables, refs = refs[:10], refs[10:]
    (back_ref, residual_ref, obs_slots, var_slots, pred_out, pred_in, resid_in, khat_ref,
     send_pred, recv_pred, send_res, recv_res) = refs
    ra, dec = lax.axis_index("ra"), lax.axis_index("dec")
    barrier = pltpu.get_barrier_semaphore()
    for d in range(1, n_dec):
        pl.semaphore_signal(barrier, inc=1, device_id=(ra, lax.rem(dec + d, n_dec)), device_id_type=MESH)
    chosen = slot_chooser(packed_ref, dec, n_dec)
    to_slots(chosen, obs_ref, obs_slots, PAD)
    to_slots(chosen, var_ref, var_slots, PAD)
    pl.semaphore_wait(barrier, n_dec - 1)

    def pred_move(d):
        owner = lax.rem(dec + n_dec - d, n_dec)
        return sender(send_pred, recv_pred)(
            d, pred_out.at[rows_of(owner, CAP * PAD), :], pred_in.at[rows_of(dec, CAP * PAD), :], (ra, owner))

    def res_move(d):
        tile = lax.rem(dec + d, n_dec)
        return sender(send_res, recv_res)(
            d, residual_ref.at[rows_of(tile, CAP * PAD), :], resid_in.at[rows_of(dec, CAP * PAD), :], (ra, tile))

    per = GROUP // CAP
    steps = n_dec // per

    def each(j, move, what):
        for i in range(per):
            d = j * per + i
            if i == 0:
                @pl.when(j > 0)
                def _():
                    what(move(d))
            else:
                what(move(d))

    def owned(j):
        return [(lax.rem(dec + 2 * n_dec - (j * per + e // CAP), n_dec), e % CAP) for e in range(GROUP)]

    def step(j, carry):
        @pl.when(j < steps)
        def _():
            which = owned(j)
            khat, flat = predict(
                [patch_ref[o * CAP + s] for o, s in which],
                [psf_in[rows_of(o * CAP + s, PSF_ROWS), :] for o, s in which],
                tables[:6])
            for (o, s), k, f in zip(which, khat, flat):
                khat_ref[o * CAP + s] = k
                pred_out[rows_of(o * CAP + s, PAD), :] = f
            each(j, pred_move, lambda c: c.start())

        @pl.when(jnp.logical_and(j > 0, j <= steps))
        def _():
            each(j - 1, pred_move, lambda c: c.wait_recv())

            @pl.when(j == 1)
            def _():
                pred_in[rows_of(dec, CAP * PAD), :] = pred_out[rows_of(dec, CAP * PAD), :]

            for i in range(per):
                tile = rows_of(lax.rem(dec + (j - 1) * per + i, n_dec), CAP * PAD)
                residual_ref[tile, :] = var_slots[tile, :] * (pred_in[tile, :] - obs_slots[tile, :])
            each(j - 1, res_move, lambda c: c.start())

            @pl.when(j == 1)
            def _():
                resid_in[rows_of(dec, CAP * PAD), :] = residual_ref[rows_of(dec, CAP * PAD), :]

        @pl.when(j > 1)
        def _():
            each(j - 2, res_move, lambda c: c.wait_recv())
            which = owned(j - 2)
            back = adjoint(
                [resid_in[rows_of(o * CAP + s, PAD), :] for o, s in which],
                [khat_ref[o * CAP + s] for o, s in which], tables[6:])
            for (o, s), image in zip(which, back):
                back_ref[o * CAP + s] = image

        return carry

    lax.fori_loop(0, steps + 2, step, 0)

    def end(d, carry):
        pred_move(d).wait_send()
        res_move(d).wait_send()
        return carry

    lax.fori_loop(1, n_dec, end, 0)


def vmem(count):
    return [pl.BlockSpec(memory_space=pltpu.VMEM)] * count


def exchange(packed, psf, model, n_ra, n_dec):
    bands, tra, tdec = model.shape
    strip = pltpu.VMEM((3, tra, N), F32)
    size = n_dec * CAP * PSF_ROWS
    several, many = pltpu.SemaphoreType.DMA((10,)), pltpu.SemaphoreType.DMA((n_dec,))
    return pl.pallas_call(
        functools.partial(exchange_kernel, n_ra, n_dec),
        out_shape=[
            jax.ShapeDtypeStruct((size, N), F32),
            jax.ShapeDtypeStruct((bands, (tdec + 2 * SIDE) // N, tra + 2 * EDGE, N), F32),
        ],
        in_specs=vmem(3),
        out_specs=vmem(2),
        scratch_shapes=[strip, strip, strip, strip, pltpu.VMEM((4, 3, EDGE, N), F32), pltpu.VMEM((size, N), F32),
                        several, several, many, many],
        compiler_params=pltpu.CompilerParams(
            collective_id=2, has_side_effects=True, vmem_limit_bytes=LIMIT),
        cost_estimate=pl.CostEstimate(flops=0, bytes_accessed=40_000_000, transcendentals=0),
    )(packed, psf, model)


def cut_kernel(meta_ref, ext_ref, patch_ref):
    step = pl.program_id(0)
    for e in range(GROUP):
        which, row_at, col_at, down, over = place_of(meta_ref[step * (GROUP // CAP) + e // CAP, e % CAP])
        at = lax.shift_right_logical(col_at, 7)
        rows = pl.ds(row_at + down, N)
        window = jnp.concatenate([ext_ref[which, at, rows, :], ext_ref[which, at + 1, rows, :]], axis=1)
        patch_ref[e] = pltpu.roll(window, lax.bitwise_and(2 * N - over, 2 * N - 1), 1)[:, :N]


def cut(meta, ext):
    slots = meta.shape[0] * CAP
    return pl.pallas_call(
        cut_kernel,
        grid_spec=pltpu.PrefetchScalarGridSpec(
            num_scalar_prefetch=1,
            grid=(slots // GROUP,),
            in_specs=[pl.BlockSpec(ext.shape, lambda i, meta: (0, 0, 0, 0), pipeline_mode=pl.Buffered(1))],
            out_specs=pl.BlockSpec((GROUP, N, N), lambda i, meta: (i, 0, 0)),
        ),
        out_shape=jax.ShapeDtypeStruct((slots, N, N), F32),
        compiler_params=pltpu.CompilerParams(vmem_limit_bytes=LIMIT),
    )(meta, ext)


def photometry(packed, obs, var, psfs, patches, n_ra, n_dec):
    slots = n_dec * CAP
    image = pltpu.VMEM((slots * PAD, N), F32)
    many = pltpu.SemaphoreType.DMA((n_dec,))
    tables = [jnp.asarray(t) for t in make_tables()]
    return pl.pallas_call(
        functools.partial(photometry_kernel, n_ra, n_dec),
        out_shape=[
            jax.ShapeDtypeStruct((slots, N, N), F32),
            jax.ShapeDtypeStruct((slots * PAD, N), F32),
        ],
        in_specs=vmem(5 + len(tables)),
        out_specs=vmem(2),
        scratch_shapes=[image, image, image, image, image, pltpu.VMEM((slots, N, N), F32), many, many, many, many],
        compiler_params=pltpu.CompilerParams(
            collective_id=0, has_side_effects=True, vmem_limit_bytes=LIMIT),
        cost_estimate=pl.CostEstimate(flops=0, bytes_accessed=40_000_000, transcendentals=0),
    )(packed, obs, var, psfs, patches, *tables)


def meta_kernel(packed_ref, meta_ref):
    meta_ref[...] = places_of_tile(packed_ref, lax.axis_index("dec"))


def tile_meta(packed):
    return pl.pallas_call(
        meta_kernel, out_shape=jax.ShapeDtypeStruct((packed.shape[0], CAP), jnp.int32))(packed)


def scatter_kernel(n_dec, meta_ref, packed_ref, slots_ref, back_ref, residual_ref, acc_ref):
    step = pl.program_id(0)

    @pl.when(step == 0)
    def _():
        acc_ref[...] = jnp.zeros_like(acc_ref)
        row, column, first, second = own_places(packed_ref, lax.axis_index("dec"))
        count = row.shape[1]
        slots = CAP * n_dec
        rank = jnp.sum(jnp.where(jnp.logical_and(column == row, second < first), 1, 0), axis=1, keepdims=True)
        place = column * CAP + rank
        chosen = (lax.broadcasted_iota(jnp.int32, (count, slots), 1) == place).astype(F32).astype(BF16)
        chosen = jnp.concatenate([chosen] * 3, axis=1)
        width = residual_ref.shape[1]
        for start in range(0, PAD, 4):
            if start * N >= width:
                break
            x = jnp.concatenate(
                [slots_ref[pl.ds(start + t, slots, stride=PAD), :] for t in range(4)], axis=1)
            y = dot(chosen, three(x))
            end = min((start + 4) * N, width)
            residual_ref[:, start * N : end] = y[:, : end - start * N]

    for e in range(GROUP):
        which, row_at, col_at, down, over = place_of(meta_ref[step * (GROUP // CAP) + e // CAP, e % CAP])
        image = jnp.concatenate([back_ref[e], jnp.zeros((8, N), F32)], axis=0)
        image = pltpu.roll(image, down, 0)
        image = jnp.concatenate([image, jnp.zeros_like(image)], axis=1)
        image = pltpu.roll(image, over, 1)
        acc_ref[which, pl.ds(row_at, N + 8), pl.ds(col_at, 2 * N)] += image


def scatter(meta, packed, residual, back, shape, n_dec):
    def whole(block):
        return pl.BlockSpec(block, lambda i, meta: (0,) * len(block), pipeline_mode=pl.Buffered(1))

    bands, tra, tdec = shape
    wide = (bands, tra + 2 * EDGE, tdec + 2 * SIDE)
    out = (packed.shape[1], C * C)
    return pl.pallas_call(
        functools.partial(scatter_kernel, n_dec),
        grid_spec=pltpu.PrefetchScalarGridSpec(
            num_scalar_prefetch=1,
            grid=(back.shape[0] // GROUP,),
            in_specs=[whole(packed.shape), whole(residual.shape), pl.BlockSpec((GROUP, N, N), lambda i, meta: (i, 0, 0))],
            out_specs=[whole(out), whole(wide)],
        ),
        out_shape=[jax.ShapeDtypeStruct(out, F32), jax.ShapeDtypeStruct(wide, F32)],
        compiler_params=pltpu.CompilerParams(vmem_limit_bytes=LIMIT),
    )(meta, packed, residual, back)


def fold_kernel(n_ra, n_dec, acc_ref, out_ref, to_right, to_left, from_left, from_right, out_corners, corners,
                from_up, from_down, send, recv):
    ra, dec, up, down, right, left = neighbours(n_ra, n_dec)
    greet_near(ra, dec, up, down, right, left)
    tra, tdec = out_ref.shape[1], out_ref.shape[2]
    top, side_at = EDGE + tra, SIDE + tdec
    low_half = lax.broadcasted_iota(jnp.int32, (1, N), 1) < 64
    copy = sender(send, recv)
    copies = [
        copy(0, acc_ref.at[:, :EDGE, SIDE:side_at], from_up, (down, dec)),
        copy(1, acc_ref.at[:, top:, SIDE:side_at], from_down, (up, dec)),
    ]
    for c in copies:
        c.start()

    def pack_left(q, rows):
        return jnp.where(low_half, pltpu.roll(acc_ref[2 * q + 1, rows, :SIDE], 64, 1), acc_ref[2 * q, rows, :SIDE])

    def pack_right(q, rows):
        return jnp.where(low_half, acc_ref[2 * q, rows, side_at:], pltpu.roll(acc_ref[2 * q + 1, rows, side_at:], 64, 1))

    middle, lower, upper = slice(EDGE, top), slice(0, EDGE), slice(top, top + EDGE)
    for q in range(3):
        to_left[q] = pack_left(q, middle)
    more = [copy(2, to_left, from_right, (ra, left))]
    more[0].start()
    copies += more
    for q in range(3):
        to_right[q] = pack_right(q, middle)
    more = [copy(3, to_right, from_left, (ra, right))]
    more[0].start()
    copies += more
    for q in range(3):
        out_corners[0, q] = pack_left(q, lower)
        out_corners[1, q] = pack_left(q, upper)
        out_corners[2, q] = pack_right(q, lower)
        out_corners[3, q] = pack_right(q, upper)
    more = [
        copy(4, out_corners.at[0], corners.at[0], (down, left)),
        copy(5, out_corners.at[1], corners.at[1], (up, left)),
        copy(6, out_corners.at[2], corners.at[2], (down, right)),
        copy(7, out_corners.at[3], corners.at[3], (up, right)),
    ]
    for c in more:
        c.start()
    copies += more
    out_ref[...] = acc_ref[:, EDGE:top, SIDE:side_at]
    for c in copies:
        c.wait()
    in_low, in_high, in_left, in_right = edges(n_ra, n_dec, ra, dec)
    out_ref[:, tra - EDGE :, :] += from_up[...] * in_high
    out_ref[:, :EDGE, :] += from_down[...] * in_low
    every, low_rows, high_rows = slice(0, tra), slice(0, EDGE), slice(tra - EDGE, tra)
    for q in range(3):
        for src, rows, scale, at_right in (
            (from_right.at[q], every, in_right, True),
            (from_left.at[q], every, in_left, False),
            (corners.at[0, q], high_rows, in_high * in_right, True),
            (corners.at[1, q], low_rows, in_low * in_right, True),
            (corners.at[2, q], high_rows, in_high * in_left, False),
            (corners.at[3, q], low_rows, in_low * in_left, False),
        ):
            value = src[...] * scale
            other = pltpu.roll(value, 64, 1)
            if at_right:
                cols, keep = slice(tdec - N, tdec), jnp.logical_not(low_half)
            else:
                cols, keep = slice(0, N), low_half
            out_ref[2 * q, rows, cols] += jnp.where(keep, value, 0.0)
            out_ref[2 * q + 1, rows, cols] += jnp.where(keep, other, 0.0)


def fold(acc, n_ra, n_dec):
    bands, tra, tdec = acc.shape[0], acc.shape[1] - 2 * EDGE, acc.shape[2] - 2 * SIDE
    strip = pltpu.VMEM((3, tra, N), F32)
    corner = pltpu.VMEM((4, 3, EDGE, N), F32)
    band = pltpu.VMEM((bands, EDGE, tdec), F32)
    return pl.pallas_call(
        functools.partial(fold_kernel, n_ra, n_dec),
        out_shape=jax.ShapeDtypeStruct((bands, tra, tdec), F32),
        in_specs=vmem(1),
        out_specs=pl.BlockSpec(memory_space=pltpu.VMEM),
        scratch_shapes=[strip, strip, strip, strip, corner, corner, band, band,
                        pltpu.SemaphoreType.DMA((8,)), pltpu.SemaphoreType.DMA((8,))],
        compiler_params=pltpu.CompilerParams(
            collective_id=1, has_side_effects=True, vmem_limit_bytes=LIMIT),
        cost_estimate=pl.CostEstimate(flops=0, bytes_accessed=40_000_000, transcendentals=0),
    )(acc)


def body(model, observed, inv_var, psf, target_dec, band, offset_ra, offset_dec):
    n_ra, n_dec = lax.axis_size("ra"), lax.axis_size("dec")
    e_dev = observed.shape[0]
    packed = (((target_dec[:, 0] * 8 + band) * 256 + offset_ra) * 256 + offset_dec).reshape(n_dec, e_dev)
    meta = tile_meta(packed)
    psfs, ext = exchange(packed, psf, model, n_ra, n_dec)
    patches = cut(meta, ext)
    back, slots = photometry(packed, observed, inv_var, psfs, patches, n_ra, n_dec)
    residual, acc = scatter(meta, packed, slots, back, model.shape, n_dec)
    return residual, fold(acc, n_ra, n_dec)


def solution(mesh):
    placed = (
        P(None, "ra", "dec"),
        P(("ra", "dec"), None),
        P(("ra", "dec"), None),
        P(("ra", "dec"), None),
        P("ra", None),
        P("ra"),
        P("ra"),
        P("ra"),
    )
    return jax.shard_map(
        body,
        mesh=mesh,
        in_specs=placed,
        out_specs=(P(("ra", "dec"), None), P(None, "ra", "dec")),
        check_vma=False,
    )
```

time: 160 us -> 159 us (level)
  local copies, waits for them, and re-layouts: 6.67 us -> 3.41 us
  Pallas kernels: 151 us -> 153 us
    pallas_call x2 -> x5, Pallas kernels: 77.9 us -> 114 us  [the longest x1 62.7 us: photometry(): pl.pallas_call(functools.partial(photometry_kernel, n_ra, n_dec), out_sha...]
    pallas_call x1, Pallas kernels: 73.4 us -> 39.1 us  [exchange(): pl.pallas_call(functools.partial(exchange_kernel, n_ra, n_dec), out_shape...]
    unnamed x2 -> x1, local copies, waits for them, and re-layouts: 4.64 us -> 2.74 us
where the time goes in v3:
time: 159 us; the launch traced here: 158 us
  Pallas kernels  153 us (96%)
  local copies, waits for them, and re-layouts  3.41 us (2%)
    pallas_call x1, Pallas kernels, photometry(): pl.pallas_call(functools.partial(photometry_kernel, n_ra, n_dec), out_sha...  62.7 us
    pallas_call x1, Pallas kernels, exchange(): pl.pallas_call(functools.partial(exchange_kernel, n_ra, n_dec), out_shape...  39.1 us
    pallas_call x1, Pallas kernels, fold(): pl.pallas_call(functools.partial(fold_kernel, n_ra, n_dec), out_shape=jax...  30.9 us
    pallas_call x1, Pallas kernels, scatter(): pl.pallas_call(functools.partial(scatter_kernel, n_dec), grid_spec=pltpu....  10.3 us
    pallas_call x1, Pallas kernels, cut(): pl.pallas_call(cut_kernel, grid_spec=pltpu.PrefetchScalarGridSpec(num_sca...  8.14 us

profile of v3, /device:TPU:1, one launch (start us, length us, event | category | flops | bytes accessed | tf_op | source)
XLA Modules:
  0.0 158.1 jit_solution(2282822227465302291)
XLA Ops:
  0.6 0.7 broadcast_multiply_fusion
  1.3 0.7 multiply_add_fusion
  2.0 0.7 reshape.9.packed_ref
  2.7 1.5 shard_map.185.meta_ref
  4.2 39.1 %shard_map.186 = (f32[2048,128]{1,0:T(8,128)}, f32[6,4,384,128]{3,2,1,0:T(8,128)}) custom-call(s32[16,32]{1,0:T(8,128)} %reshape.9.packed_ref, f32[32,3969]{1,0:T(8,128)} %psf_ref.1, f32[6,256,256]{2,1,0:T(8,128)} %model_ref.1), custom_call_target="tpu_custom_call" | custom-call | bytes 40000000 | tf_op jit(solution)/shard_map/pallas_call | solution.py:507
  43.3 8.1 %shard_map.187.patch_ref = f32[64,128,128]{2,1,0:T(8,128)} custom-call(s32[16,4]{1,0:T(8,128)} %shard_map.185.meta_ref, f32[6,4,384,128]{3,2,1,0:T(8,128)} %get-tuple-element.9.ext_ref), custom_call_target="tpu_custom_call" | custom-call | tf_op jit(solution)/shard_map/pallas_call | solution.py:535
  51.5 62.7 %shard_map.188 = (f32[64,128,128]{2,1,0:T(8,128)}, f32[2560,128]{1,0:T(8,128)}) custom-call(s32[16,32]{1,0:T(8,128)} %reshape.9.packed_ref, f32[32,4356]{1,0:T(8,128)} %obs_ref.1, f32[32,4356]{1,0:T(8,128)} %var_ref.1, f32[2048,128]{1,0:T(8,128)} %get-tuple-element.8.psf_in, f32[64,128,128]{2,1,0:T(8,128)} %shard_map.187.patch_ref, ...), custom_call_target="tpu_custom_call" | custom-call | bytes 40000000 | tf_op jit(solution)/shard_map/pallas_call | solution.py:553
  114.1 10.3 %shard_map.189 = (f32[32,4356]{1,0:T(8,128)}, f32[6,384,512]{2,1,0:T(8,128)}) custom-call(s32[16,4]{1,0:T(8,128)} %shard_map.185.meta_ref, s32[16,32]{1,0:T(8,128)} %reshape.9.packed_ref, f32[2560,128]{1,0:T(8,128)} %get-tuple-element.10.slots_ref, f32[64,128,128]{2,1,0:T(8,128)} %get-tuple-element.11.back_ref), custom_call_target="tpu_custom_call" | custom-call | tf_op jit(solution)/shard_map/pallas_call | solution.py:616
  124.5 30.9 %shard_map.190 = f32[6,256,256]{2,1,0:T(8,128)} custom-call(f32[6,384,512]{2,1,0:T(8,128)} %get-tuple-element.13.acc_ref), custom_call_target="tpu_custom_call" | custom-call | bytes 40000000 | tf_op jit(solution)/shard_map/pallas_call | solution.py:706
  155.4 2.7 %copy.21 = f32[6,256,256]{2,1,0:T(8,128)} copy(f32[6,256,256]{2,1,0:T(8,128)} %shard_map.190) | data formatting | bytes 3145728

commit v4 on v3

--- a/solution.py
+++ b/solution.py
@@ -13,7 +13,14 @@
 K = 63
 C = 66
 CAP = 4
-GROUP = 8
+GROUP = 16
+RING = 4
+PEERS = (
+    ((2, 1), (2, 3), (1, 2), (3, 2)),
+    ((1, 1), (3, 3), (1, 3), (3, 1)),
+    ((2, 0), (0, 2), (2, 2), (0, 0)),
+    ((1, 0), (3, 0), (0, 1), (0, 3)),
+)
 N = 128
 PAIRS = 33
 PAD = 40
@@ -258,21 +265,25 @@
     return ra, dec, up, down, right, left
 
 
-def greet(n_dec, ra, dec, up, down, right, left):
-    barrier = pltpu.get_barrier_semaphore()
-    for other in ((up, dec), (down, dec), (up, right), (up, left), (down, right), (down, left)):
-        pl.semaphore_signal(barrier, inc=1, device_id=other, device_id_type=MESH)
-    for d in range(1, n_dec):
-        pl.semaphore_signal(barrier, inc=1, device_id=(ra, lax.rem(dec + d, n_dec)), device_id_type=MESH)
-    pl.semaphore_wait(barrier, n_dec + 5)
-
-
-def greet_near(ra, dec, up, down, right, left):
-    barrier = pltpu.get_barrier_semaphore()
-    for other in ((up, dec), (down, dec), (ra, right), (ra, left),
-                  (up, right), (up, left), (down, right), (down, left)):
-        pl.semaphore_signal(barrier, inc=1, device_id=other, device_id_type=MESH)
-    pl.semaphore_wait(barrier, 8)
+def signal_all(devices):
+    for device in devices:
+        pl.semaphore_signal(pltpu.get_barrier_semaphore(), inc=1, device_id=device, device_id_type=MESH)
+
+
+def wait_all(devices):
+    pl.semaphore_wait(pltpu.get_barrier_semaphore(), len(devices))
+
+
+def moved(dec, shift, n_dec, sign):
+    rings = n_dec // RING
+    outer = lax.rem(dec // RING + rings + sign * shift[0], rings)
+    inner = lax.rem(lax.rem(dec, RING) + RING + sign * shift[1], RING)
+    return outer * RING + inner
+
+
+def shifts():
+    return [(j * len(PEERS[j]) + i, shift) for j in range(len(PEERS)) for i, shift in enumerate(PEERS[j])
+            if shift != (0, 0)]
 
 
 def edges(n_ra, n_dec, ra, dec):
@@ -320,61 +331,62 @@
 def exchange_kernel(n_ra, n_dec, packed_ref, psf_ref, model_ref, psf_in, ext_ref,
                     to_right, to_left, from_left, from_right, corners, psf_out, send, recv, send_psf, recv_psf):
     ra, dec, up, down, right, left = neighbours(n_ra, n_dec)
-    greet(n_dec, ra, dec, up, down, right, left)
+    peers = [(ra, moved(dec, shift, n_dec, 1)) for _, shift in shifts()] + [(up, dec), (down, dec)]
+    signal_all(peers)
     tra, tdec = model_ref.shape[1], model_ref.shape[2]
     top = EDGE + tra
     low_half = lax.broadcasted_iota(jnp.int32, (1, N), 1) < 64
     copy = sender(send, recv)
-    copies = [
-        copy(8 * t, model_ref.at[:, tra - EDGE :, t * N : t * N + N], ext_ref.at[:, 1 + t, :EDGE, :], (up, dec))
-        for t in range(2)
-    ] + [
-        copy(1 + 8 * t, model_ref.at[:, :EDGE, t * N : t * N + N], ext_ref.at[:, 1 + t, top:, :], (down, dec))
-        for t in range(2)
-    ]
-    for c in copies:
-        c.start()
     for q in range(3):
         to_right[q] = jnp.where(
             low_half, pltpu.roll(model_ref[2 * q + 1, :, tdec - N :], 64, 1), model_ref[2 * q, :, tdec - N :])
+        to_left[q] = jnp.where(
+            low_half, model_ref[2 * q, :, :N], pltpu.roll(model_ref[2 * q + 1, :, :N], 64, 1))
+    wait_all(peers)
+    sides = [copy(0, to_right, from_left, (ra, right)), copy(1, to_left, from_right, (ra, left))]
+    for c in sides:
+        c.start()
+    copies = []
+    for t in range(2):
+        cols = slice(t * N, t * N + N)
+        copies += [copy(2 + t, model_ref.at[:, tra - EDGE :, cols], ext_ref.at[:, 1 + t, :EDGE, :], (up, dec)),
+                   copy(4 + t, model_ref.at[:, :EDGE, cols], ext_ref.at[:, 1 + t, top:, :], (down, dec))]
+    for c in copies:
+        c.start()
+    to_slots(slot_chooser(packed_ref, dec, n_dec), psf_ref, psf_out, PSF_ROWS)
+    moves = []
+    here = rows_of(dec, CAP * PSF_ROWS)
+    for d, shift in shifts():
+        tile = moved(dec, shift, n_dec, 1)
+        moves.append(sender(send_psf, recv_psf)(
+            d, psf_out.at[rows_of(tile, CAP * PSF_ROWS), :], psf_in.at[here, :], (ra, tile)))
+        moves[-1].start()
+    psf_in[here, :] = psf_out[here, :]
+    for t in range(2):
+        ext_ref[:, 1 + t, EDGE:top, :] = model_ref[:, :, t * N : t * N + N]
+    for c in sides:
+        c.wait_recv()
     more = [
-        copy(2, to_right, from_left, (ra, right)),
-        copy(4, to_right.at[:, tra - EDGE :, :], corners.at[0], (up, right)),
-        copy(5, to_right.at[:, :EDGE, :], corners.at[1], (down, right)),
+        copy(6, from_left.at[:, tra - EDGE :, :], corners.at[0], (up, dec)),
+        copy(7, from_left.at[:, :EDGE, :], corners.at[1], (down, dec)),
+        copy(8, from_right.at[:, tra - EDGE :, :], corners.at[2], (up, dec)),
+        copy(9, from_right.at[:, :EDGE, :], corners.at[3], (down, dec)),
     ]
     for c in more:
         c.start()
-    copies += more
-    for q in range(3):
-        to_left[q] = jnp.where(
-            low_half, model_ref[2 * q, :, :N], pltpu.roll(model_ref[2 * q + 1, :, :N], 64, 1))
-    more = [
-        copy(3, to_left, from_right, (ra, left)),
-        copy(6, to_left.at[:, tra - EDGE :, :], corners.at[2], (up, left)),
-        copy(7, to_left.at[:, :EDGE, :], corners.at[3], (down, left)),
-    ]
-    for c in more:
-        c.start()
-    copies += more
-
-    def psf_move(d):
-        tile = lax.rem(dec + d, n_dec)
-        return sender(send_psf, recv_psf)(
-            d, psf_out.at[rows_of(tile, CAP * PSF_ROWS), :], psf_in.at[rows_of(dec, CAP * PSF_ROWS), :], (ra, tile))
-
-    to_slots(slot_chooser(packed_ref, dec, n_dec), psf_ref, psf_out, PSF_ROWS)
-
-    def start_psf(d, carry):
-        psf_move(d).start()
-        return carry
-
-    lax.fori_loop(1, n_dec, start_psf, 0)
-    psf_in[rows_of(dec, CAP * PSF_ROWS), :] = psf_out[rows_of(dec, CAP * PSF_ROWS), :]
-    for t in range(2):
-        ext_ref[:, 1 + t, EDGE:top, :] = model_ref[:, :, t * N : t * N + N]
-    for c in copies:
+    in_low, in_high, in_left, in_right = edges(n_ra, n_dec, ra, dec)
+
+    def place(pieces):
+        for src, q, col, rows, scale in pieces:
+            value = src[...] * scale
+            ext_ref[2 * q, col, rows, :] = value
+            ext_ref[2 * q + 1, col, rows, :] = pltpu.roll(value, 64, 1)
+
+    middle, low, high = slice(EDGE, top), slice(0, EDGE), slice(top, top + EDGE)
+    place([(from_left.at[q], q, 0, middle, in_left) for q in range(3)]
+          + [(from_right.at[q], q, 3, middle, in_right) for q in range(3)])
+    for c in copies + more:
         c.wait()
-    in_low, in_high, in_left, in_right = edges(n_ra, n_dec, ra, dec)
 
     @pl.when(ra == 0)
     def _():
@@ -385,23 +397,12 @@
         ext_ref[:, 1:3, top:, :] = jnp.zeros((ext_ref.shape[0], 2, EDGE, N), F32)
 
     for q in range(3):
-        for src, rows, col, scale in (
-            (from_left.at[q], slice(EDGE, top), 0, in_left),
-            (from_right.at[q], slice(EDGE, top), 3, in_right),
-            (corners.at[0, q], slice(0, EDGE), 0, in_low * in_left),
-            (corners.at[1, q], slice(top, top + EDGE), 0, in_high * in_left),
-            (corners.at[2, q], slice(0, EDGE), 3, in_low * in_right),
-            (corners.at[3, q], slice(top, top + EDGE), 3, in_high * in_right),
-        ):
-            value = src[...] * scale
-            ext_ref[2 * q, col, rows, :] = value
-            ext_ref[2 * q + 1, col, rows, :] = pltpu.roll(value, 64, 1)
-
-    def end_psf(d, carry):
-        psf_move(d).wait()
-        return carry
-
-    lax.fori_loop(1, n_dec, end_psf, 0)
+        place([(corners.at[0, q], q, 0, low, in_low * in_left), (corners.at[1, q], q, 0, high, in_high * in_left),
+               (corners.at[2, q], q, 3, low, in_low * in_right), (corners.at[3, q], q, 3, high, in_high * in_right)])
+    for c in sides:
+        c.wait_send()
+    for c in moves:
+        c.wait()
 
 
 def photometry_kernel(n_ra, n_dec, packed_ref, obs_ref, var_ref, psf_in, patch_ref, *refs):
@@ -409,43 +410,23 @@
     (back_ref, residual_ref, obs_slots, var_slots, pred_out, pred_in, resid_in, khat_ref,
      send_pred, recv_pred, send_res, recv_res) = refs
     ra, dec = lax.axis_index("ra"), lax.axis_index("dec")
-    barrier = pltpu.get_barrier_semaphore()
-    for d in range(1, n_dec):
-        pl.semaphore_signal(barrier, inc=1, device_id=(ra, lax.rem(dec + d, n_dec)), device_id_type=MESH)
-    chosen = slot_chooser(packed_ref, dec, n_dec)
-    to_slots(chosen, obs_ref, obs_slots, PAD)
-    to_slots(chosen, var_ref, var_slots, PAD)
-    pl.semaphore_wait(barrier, n_dec - 1)
-
-    def pred_move(d):
-        owner = lax.rem(dec + n_dec - d, n_dec)
-        return sender(send_pred, recv_pred)(
-            d, pred_out.at[rows_of(owner, CAP * PAD), :], pred_in.at[rows_of(dec, CAP * PAD), :], (ra, owner))
-
-    def res_move(d):
-        tile = lax.rem(dec + d, n_dec)
-        return sender(send_res, recv_res)(
-            d, residual_ref.at[rows_of(tile, CAP * PAD), :], resid_in.at[rows_of(dec, CAP * PAD), :], (ra, tile))
-
-    per = GROUP // CAP
-    steps = n_dec // per
-
-    def each(j, move, what):
-        for i in range(per):
-            d = j * per + i
-            if i == 0:
-                @pl.when(j > 0)
-                def _():
-                    what(move(d))
-            else:
-                what(move(d))
+    peers = [(ra, moved(dec, shift, n_dec, 1)) for _, shift in shifts()]
+    signal_all(peers)
+    own = rows_of(dec, CAP * PAD)
+    steps = len(PEERS)
+    pred_moves, res_moves = {}, {}
+    for d, shift in shifts():
+        owner, tile = moved(dec, shift, n_dec, -1), moved(dec, shift, n_dec, 1)
+        pred_moves[shift] = sender(send_pred, recv_pred)(
+            d, pred_out.at[rows_of(owner, CAP * PAD), :], pred_in.at[own, :], (ra, owner))
+        res_moves[shift] = sender(send_res, recv_res)(
+            d, residual_ref.at[rows_of(tile, CAP * PAD), :], resid_in.at[own, :], (ra, tile))
 
     def owned(j):
-        return [(lax.rem(dec + 2 * n_dec - (j * per + e // CAP), n_dec), e % CAP) for e in range(GROUP)]
-
-    def step(j, carry):
-        @pl.when(j < steps)
-        def _():
+        return [(moved(dec, PEERS[j][e // CAP], n_dec, -1), e % CAP) for e in range(GROUP)]
+
+    for j in range(steps + 2):
+        if j < steps:
             which = owned(j)
             khat, flat = predict(
                 [patch_ref[o * CAP + s] for o, s in which],
@@ -454,45 +435,39 @@
             for (o, s), k, f in zip(which, khat, flat):
                 khat_ref[o * CAP + s] = k
                 pred_out[rows_of(o * CAP + s, PAD), :] = f
-            each(j, pred_move, lambda c: c.start())
-
-        @pl.when(jnp.logical_and(j > 0, j <= steps))
-        def _():
-            each(j - 1, pred_move, lambda c: c.wait_recv())
-
-            @pl.when(j == 1)
-            def _():
-                pred_in[rows_of(dec, CAP * PAD), :] = pred_out[rows_of(dec, CAP * PAD), :]
-
-            for i in range(per):
-                tile = rows_of(lax.rem(dec + (j - 1) * per + i, n_dec), CAP * PAD)
-                residual_ref[tile, :] = var_slots[tile, :] * (pred_in[tile, :] - obs_slots[tile, :])
-            each(j - 1, res_move, lambda c: c.start())
-
-            @pl.when(j == 1)
-            def _():
-                resid_in[rows_of(dec, CAP * PAD), :] = residual_ref[rows_of(dec, CAP * PAD), :]
-
-        @pl.when(j > 1)
-        def _():
-            each(j - 2, res_move, lambda c: c.wait_recv())
+            if j == 0:
+                wait_all(peers)
+            for shift in PEERS[j]:
+                if shift in pred_moves:
+                    pred_moves[shift].start()
+            if j == 0:
+                chosen = slot_chooser(packed_ref, dec, n_dec)
+                to_slots(chosen, obs_ref, obs_slots, PAD)
+                to_slots(chosen, var_ref, var_slots, PAD)
+        if 1 <= j <= steps:
+            for shift in PEERS[j - 1]:
+                tile = rows_of(moved(dec, shift, n_dec, 1), CAP * PAD)
+                if shift in pred_moves:
+                    pred_moves[shift].wait_recv()
+                    residual_ref[tile, :] = var_slots[tile, :] * (pred_in[tile, :] - obs_slots[tile, :])
+                    res_moves[shift].start()
+                else:
+                    resid = var_slots[own, :] * (pred_out[own, :] - obs_slots[own, :])
+                    residual_ref[own, :] = resid
+                    resid_in[own, :] = resid
+        if j >= 2:
+            for shift in PEERS[j - 2]:
+                if shift in res_moves:
+                    res_moves[shift].wait_recv()
             which = owned(j - 2)
             back = adjoint(
                 [resid_in[rows_of(o * CAP + s, PAD), :] for o, s in which],
                 [khat_ref[o * CAP + s] for o, s in which], tables[6:])
             for (o, s), image in zip(which, back):
                 back_ref[o * CAP + s] = image
-
-        return carry
-
-    lax.fori_loop(0, steps + 2, step, 0)
-
-    def end(d, carry):
-        pred_move(d).wait_send()
-        res_move(d).wait_send()
-        return carry
-
-    lax.fori_loop(1, n_dec, end, 0)
+    for shift in pred_moves:
+        pred_moves[shift].wait_send()
+        res_moves[shift].wait_send()
 
 
 def vmem(count):
@@ -629,17 +604,12 @@
 def fold_kernel(n_ra, n_dec, acc_ref, out_ref, to_right, to_left, from_left, from_right, out_corners, corners,
                 from_up, from_down, send, recv):
     ra, dec, up, down, right, left = neighbours(n_ra, n_dec)
-    greet_near(ra, dec, up, down, right, left)
+    peers = [(up, dec), (down, dec), (ra, right), (ra, left)]
+    signal_all(peers)
     tra, tdec = out_ref.shape[1], out_ref.shape[2]
     top, side_at = EDGE + tra, SIDE + tdec
     low_half = lax.broadcasted_iota(jnp.int32, (1, N), 1) < 64
     copy = sender(send, recv)
-    copies = [
-        copy(0, acc_ref.at[:, :EDGE, SIDE:side_at], from_up, (down, dec)),
-        copy(1, acc_ref.at[:, top:, SIDE:side_at], from_down, (up, dec)),
-    ]
-    for c in copies:
-        c.start()
 
     def pack_left(q, rows):
         return jnp.where(low_half, pltpu.roll(acc_ref[2 * q + 1, rows, :SIDE], 64, 1), acc_ref[2 * q, rows, :SIDE])
@@ -648,54 +618,62 @@
         return jnp.where(low_half, acc_ref[2 * q, rows, side_at:], pltpu.roll(acc_ref[2 * q + 1, rows, side_at:], 64, 1))
 
     middle, lower, upper = slice(EDGE, top), slice(0, EDGE), slice(top, top + EDGE)
-    for q in range(3):
-        to_left[q] = pack_left(q, middle)
-    more = [copy(2, to_left, from_right, (ra, left))]
-    more[0].start()
-    copies += more
-    for q in range(3):
-        to_right[q] = pack_right(q, middle)
-    more = [copy(3, to_right, from_left, (ra, right))]
-    more[0].start()
-    copies += more
     for q in range(3):
         out_corners[0, q] = pack_left(q, lower)
         out_corners[1, q] = pack_left(q, upper)
         out_corners[2, q] = pack_right(q, lower)
         out_corners[3, q] = pack_right(q, upper)
+        to_left[q] = pack_left(q, middle)
+        to_right[q] = pack_right(q, middle)
+    wait_all(peers)
+    inner, low_rows, high_rows = slice(EDGE, tra - EDGE), slice(0, EDGE), slice(tra - EDGE, tra)
+    turns = [copy(i, out_corners.at[i], corners.at[i], (down if i % 2 == 0 else up, dec)) for i in range(4)]
+    copies = [
+        copy(4, to_left.at[:, inner, :], from_right.at[:, inner, :], (ra, left)),
+        copy(5, to_right.at[:, inner, :], from_left.at[:, inner, :], (ra, right)),
+        copy(6, acc_ref.at[:, lower, SIDE:side_at], from_up, (down, dec)),
+        copy(7, acc_ref.at[:, upper, SIDE:side_at], from_down, (up, dec)),
+    ]
+    for c in turns + copies:
+        c.start()
+    in_low, in_high, in_left, in_right = edges(n_ra, n_dec, ra, dec)
+    for c in turns:
+        c.wait_recv()
+    to_left[:, high_rows, :] += corners[0] * in_high
+    to_right[:, high_rows, :] += corners[2] * in_high
     more = [
-        copy(4, out_corners.at[0], corners.at[0], (down, left)),
-        copy(5, out_corners.at[1], corners.at[1], (up, left)),
-        copy(6, out_corners.at[2], corners.at[2], (down, right)),
-        copy(7, out_corners.at[3], corners.at[3], (up, right)),
+        copy(8, to_left.at[:, high_rows, :], from_right.at[:, high_rows, :], (ra, left)),
+        copy(9, to_right.at[:, high_rows, :], from_left.at[:, high_rows, :], (ra, right)),
     ]
     for c in more:
         c.start()
-    copies += more
-    out_ref[...] = acc_ref[:, EDGE:top, SIDE:side_at]
-    for c in copies:
+    to_left[:, low_rows, :] += corners[1] * in_low
+    to_right[:, low_rows, :] += corners[3] * in_low
+    more += [
+        copy(10, to_left.at[:, low_rows, :], from_right.at[:, low_rows, :], (ra, left)),
+        copy(11, to_right.at[:, low_rows, :], from_left.at[:, low_rows, :], (ra, right)),
+    ]
+    for c in more[2:]:
+        c.start()
+    out_ref[...] = acc_ref[:, middle, SIDE:side_at]
+    for c in turns:
+        c.wait_send()
+    for c in copies[2:]:
         c.wait()
-    in_low, in_high, in_left, in_right = edges(n_ra, n_dec, ra, dec)
-    out_ref[:, tra - EDGE :, :] += from_up[...] * in_high
-    out_ref[:, :EDGE, :] += from_down[...] * in_low
-    every, low_rows, high_rows = slice(0, tra), slice(0, EDGE), slice(tra - EDGE, tra)
+    out_ref[:, high_rows, :] += from_up[...] * in_high
+    out_ref[:, low_rows, :] += from_down[...] * in_low
+    for c in copies[:2] + more:
+        c.wait()
     for q in range(3):
-        for src, rows, scale, at_right in (
-            (from_right.at[q], every, in_right, True),
-            (from_left.at[q], every, in_left, False),
-            (corners.at[0, q], high_rows, in_high * in_right, True),
-            (corners.at[1, q], low_rows, in_low * in_right, True),
-            (corners.at[2, q], high_rows, in_high * in_left, False),
-            (corners.at[3, q], low_rows, in_low * in_left, False),
-        ):
+        for src, scale, at_right in ((from_right.at[q], in_right, True), (from_left.at[q], in_left, False)):
             value = src[...] * scale
             other = pltpu.roll(value, 64, 1)
             if at_right:
                 cols, keep = slice(tdec - N, tdec), jnp.logical_not(low_half)
             else:
                 cols, keep = slice(0, N), low_half
-            out_ref[2 * q, rows, cols] += jnp.where(keep, value, 0.0)
-            out_ref[2 * q + 1, rows, cols] += jnp.where(keep, other, 0.0)
+            out_ref[2 * q, :, cols] += jnp.where(keep, value, 0.0)
+            out_ref[2 * q + 1, :, cols] += jnp.where(keep, other, 0.0)
 
 
 def fold(acc, n_ra, n_dec):
@@ -709,7 +687,7 @@
         in_specs=vmem(1),
         out_specs=pl.BlockSpec(memory_space=pltpu.VMEM),
         scratch_shapes=[strip, strip, strip, strip, corner, corner, band, band,
-                        pltpu.SemaphoreType.DMA((8,)), pltpu.SemaphoreType.DMA((8,))],
+                        pltpu.SemaphoreType.DMA((12,)), pltpu.SemaphoreType.DMA((12,))],
         compiler_params=pltpu.CompilerParams(
             collective_id=1, has_side_effects=True, vmem_limit_bytes=LIMIT),
         cost_estimate=pl.CostEstimate(flops=0, bytes_accessed=40_000_000, transcendentals=0),

time: 159 us -> 125 us (0.79)
  Pallas kernels: 153 us -> 119 us
    pallas_call x1, Pallas kernels: 62.7 us -> 46.8 us  [photometry(): pl.pallas_call(functools.partial(photometry_kernel, n_ra, n_dec), out_sha...]
    pallas_call x1, Pallas kernels: 30.9 us -> 21.8 us  [fold(): pl.pallas_call(functools.partial(fold_kernel, n_ra, n_dec), out_shape=jax...]
    pallas_call x1, Pallas kernels: 39.1 us -> 32.8 us  [exchange(): pl.pallas_call(functools.partial(exchange_kernel, n_ra, n_dec), out_shape...]
where the time goes in v4:
time: 125 us; the launch traced here: 124 us
  Pallas kernels  119 us (95%)
  local copies, waits for them, and re-layouts  3.41 us (3%)
  other arithmetic  1.41 us (1%)
    pallas_call x1, Pallas kernels, photometry(): pl.pallas_call(functools.partial(photometry_kernel, n_ra, n_dec), out_sha...  46.8 us
    pallas_call x1, Pallas kernels, exchange(): pl.pallas_call(functools.partial(exchange_kernel, n_ra, n_dec), out_shape...  32.8 us
    pallas_call x1, Pallas kernels, fold(): pl.pallas_call(functools.partial(fold_kernel, n_ra, n_dec), out_shape=jax...  21.8 us
    pallas_call x1, Pallas kernels, scatter(): pl.pallas_call(functools.partial(scatter_kernel, n_dec), grid_spec=pltpu....  8.77 us
    pallas_call x1, Pallas kernels, cut(): pl.pallas_call(cut_kernel, grid_spec=pltpu.PrefetchScalarGridSpec(num_sca...  7.06 us
    unnamed x1, local copies, waits for them, and re-layouts  2.74 us

profile of v4, /device:TPU:1, one launch (start us, length us, event | category | flops | bytes accessed | tf_op | source)
XLA Modules:
  0.0 124.2 jit_solution(8530705309725500083)
XLA Ops:
  0.6 0.7 broadcast_multiply_fusion
  1.3 0.7 multiply_add_fusion
  2.0 0.7 reshape.9.packed_ref
  2.7 1.5 %shard_map.185.meta_ref = s32[16,4]{1,0:T(8,128)} custom-call(s32[16,32]{1,0:T(8,128)} %reshape.9.packed_ref), custom_call_target="tpu_custom_call" | custom-call | tf_op jit(solution)/shard_map/pallas_call | solution.py:548
  4.2 32.8 %shard_map.186 = (f32[2048,128]{1,0:T(8,128)}, f32[6,4,384,128]{3,2,1,0:T(8,128)}) custom-call(s32[16,32]{1,0:T(8,128)} %reshape.9.packed_ref, f32[32,3969]{1,0:T(8,128)} %psf_ref.1, f32[6,256,256]{2,1,0:T(8,128)} %model_ref.1), custom_call_target="tpu_custom_call" | custom-call | bytes 40000000 | tf_op jit(solution)/shard_map/pallas_call | solution.py:482
  37.0 7.1 %shard_map.187.patch_ref = f32[64,128,128]{2,1,0:T(8,128)} custom-call(s32[16,4]{1,0:T(8,128)} %shard_map.185.meta_ref, f32[6,4,384,128]{3,2,1,0:T(8,128)} %get-tuple-element.9.ext_ref), custom_call_target="tpu_custom_call" | custom-call | tf_op jit(solution)/shard_map/pallas_call | solution.py:510
  44.1 46.8 %shard_map.188 = (f32[64,128,128]{2,1,0:T(8,128)}, f32[2560,128]{1,0:T(8,128)}) custom-call(s32[16,32]{1,0:T(8,128)} %reshape.9.packed_ref, f32[32,4356]{1,0:T(8,128)} %obs_ref.1, f32[32,4356]{1,0:T(8,128)} %var_ref.1, f32[2048,128]{1,0:T(8,128)} %get-tuple-element.8.psf_in, f32[64,128,128]{2,1,0:T(8,128)} %shard_map.187.patch_ref, ...), custom_call_target="tpu_custom_call" | custom-call | bytes 40000000 | tf_op jit(solution)/shard_map/pallas_call | solution.py:528
  90.9 8.8 %shard_map.189 = (f32[32,4356]{1,0:T(8,128)}, f32[6,384,512]{2,1,0:T(8,128)}) custom-call(s32[16,4]{1,0:T(8,128)} %shard_map.185.meta_ref, s32[16,32]{1,0:T(8,128)} %reshape.9.packed_ref, f32[2560,128]{1,0:T(8,128)} %get-tuple-element.10.slots_ref, f32[64,128,128]{2,1,0:T(8,128)} %get-tuple-element.11.back_ref), custom_call_target="tpu_custom_call" | custom-call | tf_op jit(solution)/shard_map/pallas_call | solution.py:591
  99.6 21.8 %shard_map.190 = f32[6,256,256]{2,1,0:T(8,128)} custom-call(f32[6,384,512]{2,1,0:T(8,128)} %get-tuple-element.13.acc_ref), custom_call_target="tpu_custom_call" | custom-call | bytes 40000000 | tf_op jit(solution)/shard_map/pallas_call | solution.py:684
  121.4 2.7 %copy.21 = f32[6,256,256]{2,1,0:T(8,128)} copy(f32[6,256,256]{2,1,0:T(8,128)} %shard_map.190) | data formatting | bytes 3145728

commit v5 on v4

--- a/solution.py
+++ b/solution.py
@@ -148,9 +148,14 @@
     which = lax.shift_right_logical(code, 16)
     row = lax.bitwise_and(lax.shift_right_logical(code, 8), 255) + (EDGE - K + 1)
     column = lax.bitwise_and(code, 255) + (SIDE - K + 1)
-    row_at = pl.multiple_of(lax.shift_left(lax.shift_right_logical(row, 3), 3), 8)
-    col_at = pl.multiple_of(lax.shift_left(lax.shift_right_logical(column, 7), 7), 128)
-    return which, row_at, col_at, row - row_at, column - col_at
+    return which, lax.shift_right_logical(column, 7), row, lax.bitwise_and(column, N - 1)
+
+
+def cut(code, ext_ref):
+    which, at, row, over = place_of(code)
+    rows = pl.ds(row, N)
+    window = jnp.concatenate([ext_ref[which, at, rows, :], ext_ref[which, at + 1, rows, :]], axis=1)
+    return pltpu.roll(window, lax.bitwise_and(2 * N - over, 2 * N - 1), 1)[:, :N]
 
 
 def halves(k, low_half):
@@ -328,8 +333,11 @@
             out_ref[pl.ds(start + t, slots, stride=rows), :] = y[:, t * N : t * N + N]
 
 
-def exchange_kernel(n_ra, n_dec, packed_ref, psf_ref, model_ref, psf_in, ext_ref,
-                    to_right, to_left, from_left, from_right, corners, psf_out, send, recv, send_psf, recv_psf):
+def photometry_kernel(n_ra, n_dec, meta_ref, packed_ref, psf_ref, obs_ref, var_ref, model_ref, *refs):
+    tables, refs = refs[:10], refs[10:]
+    (back_ref, residual_ref, ext_ref, to_right, to_left, from_left, from_right, corners, psf_out, psf_in,
+     obs_slots, var_slots, pred_out, pred_in, resid_in, khat_ref, send, recv, send_psf, recv_psf,
+     send_pred, recv_pred, send_res, recv_res) = refs
     ra, dec, up, down, right, left = neighbours(n_ra, n_dec)
     peers = [(ra, moved(dec, shift, n_dec, 1)) for _, shift in shifts()] + [(up, dec), (down, dec)]
     signal_all(peers)
@@ -353,15 +361,18 @@
                    copy(4 + t, model_ref.at[:, :EDGE, cols], ext_ref.at[:, 1 + t, top:, :], (down, dec))]
     for c in copies:
         c.start()
-    to_slots(slot_chooser(packed_ref, dec, n_dec), psf_ref, psf_out, PSF_ROWS)
-    moves = []
+    chosen = slot_chooser(packed_ref, dec, n_dec)
+    to_slots(chosen, psf_ref, psf_out, PSF_ROWS)
+    moves = {}
     here = rows_of(dec, CAP * PSF_ROWS)
     for d, shift in shifts():
         tile = moved(dec, shift, n_dec, 1)
-        moves.append(sender(send_psf, recv_psf)(
-            d, psf_out.at[rows_of(tile, CAP * PSF_ROWS), :], psf_in.at[here, :], (ra, tile)))
-        moves[-1].start()
+        moves[shift] = sender(send_psf, recv_psf)(
+            d, psf_out.at[rows_of(tile, CAP * PSF_ROWS), :], psf_in.at[here, :], (ra, tile))
+        moves[shift].start()
     psf_in[here, :] = psf_out[here, :]
+    to_slots(chosen, obs_ref, obs_slots, PAD)
+    to_slots(chosen, var_ref, var_slots, PAD)
     for t in range(2):
         ext_ref[:, 1 + t, EDGE:top, :] = model_ref[:, :, t * N : t * N + N]
     for c in sides:
@@ -401,17 +412,7 @@
                (corners.at[2, q], q, 3, low, in_low * in_right), (corners.at[3, q], q, 3, high, in_high * in_right)])
     for c in sides:
         c.wait_send()
-    for c in moves:
-        c.wait()
-
-
-def photometry_kernel(n_ra, n_dec, packed_ref, obs_ref, var_ref, psf_in, patch_ref, *refs):
-    tables, refs = refs[:10], refs[10:]
-    (back_ref, residual_ref, obs_slots, var_slots, pred_out, pred_in, resid_in, khat_ref,
-     send_pred, recv_pred, send_res, recv_res) = refs
-    ra, dec = lax.axis_index("ra"), lax.axis_index("dec")
-    peers = [(ra, moved(dec, shift, n_dec, 1)) for _, shift in shifts()]
-    signal_all(peers)
+
     own = rows_of(dec, CAP * PAD)
     steps = len(PEERS)
     pred_moves, res_moves = {}, {}
@@ -427,23 +428,20 @@
 
     for j in range(steps + 2):
         if j < steps:
+            for shift in PEERS[j]:
+                if shift in moves:
+                    moves[shift].wait_recv()
             which = owned(j)
             khat, flat = predict(
-                [patch_ref[o * CAP + s] for o, s in which],
+                [cut(meta_ref[o, s], ext_ref) for o, s in which],
                 [psf_in[rows_of(o * CAP + s, PSF_ROWS), :] for o, s in which],
                 tables[:6])
             for (o, s), k, f in zip(which, khat, flat):
                 khat_ref[o * CAP + s] = k
                 pred_out[rows_of(o * CAP + s, PAD), :] = f
-            if j == 0:
-                wait_all(peers)
             for shift in PEERS[j]:
                 if shift in pred_moves:
                     pred_moves[shift].start()
-            if j == 0:
-                chosen = slot_chooser(packed_ref, dec, n_dec)
-                to_slots(chosen, obs_ref, obs_slots, PAD)
-                to_slots(chosen, var_ref, var_slots, PAD)
         if 1 <= j <= steps:
             for shift in PEERS[j - 1]:
                 tile = rows_of(moved(dec, shift, n_dec, 1), CAP * PAD)
@@ -466,6 +464,7 @@
             for (o, s), image in zip(which, back):
                 back_ref[o * CAP + s] = image
     for shift in pred_moves:
+        moves[shift].wait_send()
         pred_moves[shift].wait_send()
         res_moves[shift].wait_send()
 
@@ -474,56 +473,12 @@
     return [pl.BlockSpec(memory_space=pltpu.VMEM)] * count
 
 
-def exchange(packed, psf, model, n_ra, n_dec):
+def photometry(meta, packed, psf, obs, var, model, n_ra, n_dec):
     bands, tra, tdec = model.shape
     strip = pltpu.VMEM((3, tra, N), F32)
-    size = n_dec * CAP * PSF_ROWS
+    slots = n_dec * CAP
+    image, small = pltpu.VMEM((slots * PAD, N), F32), pltpu.VMEM((slots * PSF_ROWS, N), F32)
     several, many = pltpu.SemaphoreType.DMA((10,)), pltpu.SemaphoreType.DMA((n_dec,))
-    return pl.pallas_call(
-        functools.partial(exchange_kernel, n_ra, n_dec),
-        out_shape=[
-            jax.ShapeDtypeStruct((size, N), F32),
-            jax.ShapeDtypeStruct((bands, (tdec + 2 * SIDE) // N, tra + 2 * EDGE, N), F32),
-        ],
-        in_specs=vmem(3),
-        out_specs=vmem(2),
-        scratch_shapes=[strip, strip, strip, strip, pltpu.VMEM((4, 3, EDGE, N), F32), pltpu.VMEM((size, N), F32),
-                        several, several, many, many],
-        compiler_params=pltpu.CompilerParams(
-            collective_id=2, has_side_effects=True, vmem_limit_bytes=LIMIT),
-        cost_estimate=pl.CostEstimate(flops=0, bytes_accessed=40_000_000, transcendentals=0),
-    )(packed, psf, model)
-
-
-def cut_kernel(meta_ref, ext_ref, patch_ref):
-    step = pl.program_id(0)
-    for e in range(GROUP):
-        which, row_at, col_at, down, over = place_of(meta_ref[step * (GROUP // CAP) + e // CAP, e % CAP])
-        at = lax.shift_right_logical(col_at, 7)
-        rows = pl.ds(row_at + down, N)
-        window = jnp.concatenate([ext_ref[which, at, rows, :], ext_ref[which, at + 1, rows, :]], axis=1)
-        patch_ref[e] = pltpu.roll(window, lax.bitwise_and(2 * N - over, 2 * N - 1), 1)[:, :N]
-
-
-def cut(meta, ext):
-    slots = meta.shape[0] * CAP
-    return pl.pallas_call(
-        cut_kernel,
-        grid_spec=pltpu.PrefetchScalarGridSpec(
-            num_scalar_prefetch=1,
-            grid=(slots // GROUP,),
-            in_specs=[pl.BlockSpec(ext.shape, lambda i, meta: (0, 0, 0, 0), pipeline_mode=pl.Buffered(1))],
-            out_specs=pl.BlockSpec((GROUP, N, N), lambda i, meta: (i, 0, 0)),
-        ),
-        out_shape=jax.ShapeDtypeStruct((slots, N, N), F32),
-        compiler_params=pltpu.CompilerParams(vmem_limit_bytes=LIMIT),
-    )(meta, ext)
-
-
-def photometry(packed, obs, var, psfs, patches, n_ra, n_dec):
-    slots = n_dec * CAP
-    image = pltpu.VMEM((slots * PAD, N), F32)
-    many = pltpu.SemaphoreType.DMA((n_dec,))
     tables = [jnp.asarray(t) for t in make_tables()]
     return pl.pallas_call(
         functools.partial(photometry_kernel, n_ra, n_dec),
@@ -531,13 +486,16 @@
             jax.ShapeDtypeStruct((slots, N, N), F32),
             jax.ShapeDtypeStruct((slots * PAD, N), F32),
         ],
-        in_specs=vmem(5 + len(tables)),
+        in_specs=[pl.BlockSpec(memory_space=pltpu.SMEM)] + vmem(5 + len(tables)),
         out_specs=vmem(2),
-        scratch_shapes=[image, image, image, image, image, pltpu.VMEM((slots, N, N), F32), many, many, many, many],
+        scratch_shapes=[pltpu.VMEM((bands, (tdec + 2 * SIDE) // N, tra + 2 * EDGE, N), F32),
+                        strip, strip, strip, strip, pltpu.VMEM((4, 3, EDGE, N), F32), small, small,
+                        image, image, image, image, image, pltpu.VMEM((slots, N, N), F32),
+                        several, several, many, many, many, many, many, many],
         compiler_params=pltpu.CompilerParams(
             collective_id=0, has_side_effects=True, vmem_limit_bytes=LIMIT),
         cost_estimate=pl.CostEstimate(flops=0, bytes_accessed=40_000_000, transcendentals=0),
-    )(packed, obs, var, psfs, patches, *tables)
+    )(meta, packed, psf, obs, var, model, *tables)
 
 
 def meta_kernel(packed_ref, meta_ref):
@@ -573,12 +531,12 @@
             residual_ref[:, start * N : end] = y[:, : end - start * N]
 
     for e in range(GROUP):
-        which, row_at, col_at, down, over = place_of(meta_ref[step * (GROUP // CAP) + e // CAP, e % CAP])
-        image = jnp.concatenate([back_ref[e], jnp.zeros((8, N), F32)], axis=0)
-        image = pltpu.roll(image, down, 0)
-        image = jnp.concatenate([image, jnp.zeros_like(image)], axis=1)
-        image = pltpu.roll(image, over, 1)
-        acc_ref[which, pl.ds(row_at, N + 8), pl.ds(col_at, 2 * N)] += image
+        which, at, row, over = place_of(meta_ref[step * (GROUP // CAP) + e // CAP, e % CAP])
+        image = back_ref[e]
+        image = pltpu.roll(jnp.concatenate([image, jnp.zeros_like(image)], axis=1), over, 1)
+        rows = pl.ds(row, N)
+        acc_ref[which, at, rows, :] += image[:, :N]
+        acc_ref[which, at + 1, rows, :] += image[:, N:]
 
 
 def scatter(meta, packed, residual, back, shape, n_dec):
@@ -586,7 +544,7 @@
         return pl.BlockSpec(block, lambda i, meta: (0,) * len(block), pipeline_mode=pl.Buffered(1))
 
     bands, tra, tdec = shape
-    wide = (bands, tra + 2 * EDGE, tdec + 2 * SIDE)
+    wide = (bands, (tdec + 2 * SIDE) // N, tra + 2 * EDGE, N)
     out = (packed.shape[1], C * C)
     return pl.pallas_call(
         functools.partial(scatter_kernel, n_dec),
@@ -607,15 +565,15 @@
     peers = [(up, dec), (down, dec), (ra, right), (ra, left)]
     signal_all(peers)
     tra, tdec = out_ref.shape[1], out_ref.shape[2]
-    top, side_at = EDGE + tra, SIDE + tdec
+    top = EDGE + tra
     low_half = lax.broadcasted_iota(jnp.int32, (1, N), 1) < 64
     copy = sender(send, recv)
 
     def pack_left(q, rows):
-        return jnp.where(low_half, pltpu.roll(acc_ref[2 * q + 1, rows, :SIDE], 64, 1), acc_ref[2 * q, rows, :SIDE])
+        return jnp.where(low_half, pltpu.roll(acc_ref[2 * q + 1, 0, rows, :], 64, 1), acc_ref[2 * q, 0, rows, :])
 
     def pack_right(q, rows):
-        return jnp.where(low_half, acc_ref[2 * q, rows, side_at:], pltpu.roll(acc_ref[2 * q + 1, rows, side_at:], 64, 1))
+        return jnp.where(low_half, acc_ref[2 * q, 3, rows, :], pltpu.roll(acc_ref[2 * q + 1, 3, rows, :], 64, 1))
 
     middle, lower, upper = slice(EDGE, top), slice(0, EDGE), slice(top, top + EDGE)
     for q in range(3):
@@ -631,8 +589,8 @@
     copies = [
         copy(4, to_left.at[:, inner, :], from_right.at[:, inner, :], (ra, left)),
         copy(5, to_right.at[:, inner, :], from_left.at[:, inner, :], (ra, right)),
-        copy(6, acc_ref.at[:, lower, SIDE:side_at], from_up, (down, dec)),
-        copy(7, acc_ref.at[:, upper, SIDE:side_at], from_down, (up, dec)),
+        copy(6, acc_ref.at[:, 1:3, lower, :], from_up, (down, dec)),
+        copy(7, acc_ref.at[:, 1:3, upper, :], from_down, (up, dec)),
     ]
     for c in turns + copies:
         c.start()
@@ -655,13 +613,16 @@
     ]
     for c in more[2:]:
         c.start()
-    out_ref[...] = acc_ref[:, middle, SIDE:side_at]
+    for t in range(2):
+        out_ref[:, :, t * N : t * N + N] = acc_ref[:, 1 + t, middle, :]
     for c in turns:
         c.wait_send()
     for c in copies[2:]:
         c.wait()
-    out_ref[:, high_rows, :] += from_up[...] * in_high
-    out_ref[:, low_rows, :] += from_down[...] * in_low
+    for t in range(2):
+        cols = slice(t * N, t * N + N)
+        out_ref[:, high_rows, cols] += from_up[:, t] * in_high
+        out_ref[:, low_rows, cols] += from_down[:, t] * in_low
     for c in copies[:2] + more:
         c.wait()
     for q in range(3):
@@ -677,10 +638,10 @@
 
 
 def fold(acc, n_ra, n_dec):
-    bands, tra, tdec = acc.shape[0], acc.shape[1] - 2 * EDGE, acc.shape[2] - 2 * SIDE
+    bands, tra, tdec = acc.shape[0], acc.shape[2] - 2 * EDGE, acc.shape[1] * N - 2 * SIDE
     strip = pltpu.VMEM((3, tra, N), F32)
     corner = pltpu.VMEM((4, 3, EDGE, N), F32)
-    band = pltpu.VMEM((bands, EDGE, tdec), F32)
+    band = pltpu.VMEM((bands, 2, EDGE, N), F32)
     return pl.pallas_call(
         functools.partial(fold_kernel, n_ra, n_dec),
         out_shape=jax.ShapeDtypeStruct((bands, tra, tdec), F32),
@@ -699,9 +660,7 @@
     e_dev = observed.shape[0]
     packed = (((target_dec[:, 0] * 8 + band) * 256 + offset_ra) * 256 + offset_dec).reshape(n_dec, e_dev)
     meta = tile_meta(packed)
-    psfs, ext = exchange(packed, psf, model, n_ra, n_dec)
-    patches = cut(meta, ext)
-    back, slots = photometry(packed, observed, inv_var, psfs, patches, n_ra, n_dec)
+    back, slots = photometry(meta, packed, psf, observed, inv_var, model, n_ra, n_dec)
     residual, acc = scatter(meta, packed, slots, back, model.shape, n_dec)
     return residual, fold(acc, n_ra, n_dec)
 

time: 125 us -> 114 us (0.912)
  Pallas kernels: 119 us -> 108 us
    pallas_call x2 -> x0, Pallas kernels: 39.8 us -> none  [the longest x1 32.8 us: exchange(): pl.pallas_call(functools.partial(exchange_kernel, n_ra, n_dec), out_shape...]
    pallas_call x1, Pallas kernels: 46.8 us -> 76.9 us  [photometry(): pl.pallas_call(functools.partial(photometry_kernel, n_ra, n_dec), out_sha...]
where the time goes in v5:
time: 114 us
  Pallas kernels  108 us (95%)
  local copies, waits for them, and re-layouts  3.41 us (3%)
  other arithmetic  1.41 us (1%)
    pallas_call x1, Pallas kernels, photometry(): pl.pallas_call(functools.partial(photometry_kernel, n_ra, n_dec), out_sha...  76.9 us
    pallas_call x1, Pallas kernels, fold(): pl.pallas_call(functools.partial(fold_kernel, n_ra, n_dec), out_shape=jax...  21.5 us
    pallas_call x1, Pallas kernels, scatter(): pl.pallas_call(functools.partial(scatter_kernel, n_dec), grid_spec=pltpu....  8.2 us
    unnamed x1, local copies, waits for them, and re-layouts  2.74 us

profile of v5, /device:TPU:1, one launch (start us, length us, event | category | flops | bytes accessed | tf_op | source)
XLA Modules:
  0.0 113.6 jit_solution(3358227092353338987)
XLA Ops:
  0.6 0.7 broadcast_multiply_fusion
  1.3 0.7 multiply_add_fusion
  2.0 0.7 reshape.9.packed_ref
  2.7 1.5 %shard_map.185.meta_ref = s32[16,4]{1,0:T(8,128)} custom-call(s32[16,32]{1,0:T(8,128)} %reshape.9.packed_ref), custom_call_target="tpu_custom_call" | custom-call | tf_op jit(solution)/shard_map/pallas_call | solution.py:506
  4.2 76.9 %shard_map.186 = (f32[64,128,128]{2,1,0:T(8,128)}, f32[2560,128]{1,0:T(8,128)}) custom-call(s32[16,4]{1,0:T(8,128)} %shard_map.185.meta_ref, s32[16,32]{1,0:T(8,128)} %reshape.9.packed_ref, f32[32,3969]{1,0:T(8,128)} %psf_ref.1, f32[32,4356]{1,0:T(8,128)} %obs_ref.1, f32[32,4356]{1,0:T(8,128)} %var_ref.1, f32[6,256,256]{2,1,0:T(8,128)} %model_ref.1, ...), custom_call_target="tpu_custom_call" | custom-call | bytes 40000000 | tf_op jit(solution)/shard_map/pallas_call | solution.py:483
  81.1 8.2 %shard_map.187 = (f32[32,4356]{1,0:T(8,128)}, f32[6,4,384,128]{3,2,1,0:T(8,128)}) custom-call(s32[16,4]{1,0:T(8,128)} %shard_map.185.meta_ref, s32[16,32]{1,0:T(8,128)} %reshape.9.packed_ref, f32[2560,128]{1,0:T(8,128)} %get-tuple-element.6.slots_ref, f32[64,128,128]{2,1,0:T(8,128)} %get-tuple-element.7.back_ref), custom_call_target="tpu_custom_call" | custom-call | tf_op jit(solution)/shard_map/pallas_call | solution.py:549
  89.3 21.5 %shard_map.188 = f32[6,256,256]{2,1,0:T(8,128)} custom-call(f32[6,4,384,128]{3,2,1,0:T(8,128)} %get-tuple-element.9.acc_ref), custom_call_target="tpu_custom_call" | custom-call | bytes 40000000 | tf_op jit(solution)/shard_map/pallas_call | solution.py:645
  110.8 2.7 %copy.21 = f32[6,256,256]{2,1,0:T(8,128)} copy(f32[6,256,256]{2,1,0:T(8,128)} %shard_map.188) | data formatting | bytes 3145728

commit v6 on v5

--- a/solution.py
+++ b/solution.py
@@ -16,18 +16,22 @@
 GROUP = 16
 RING = 4
 PEERS = (
+    ((2, 0), (0, 2), (2, 2), (0, 0)),
     ((2, 1), (2, 3), (1, 2), (3, 2)),
     ((1, 1), (3, 3), (1, 3), (3, 1)),
-    ((2, 0), (0, 2), (2, 2), (0, 0)),
     ((1, 0), (3, 0), (0, 1), (0, 3)),
 )
+SLOT = 36
+B_LAG = 3
 N = 128
 PAIRS = 33
 PAD = 40
 PSF_ROWS = 32
 EDGE = 64
 SIDE = 128
-LIMIT = 60 * 1024 * 1024
+MAIN_LIMIT = 60 * 1024 * 1024
+SMALL_LIMIT = 18 * 1024 * 1024
+SCATTER_LIMIT = 18 * 1024 * 1024
 MESH = pl.DeviceIdType.MESH
 F32 = jnp.float32
 BF16 = jnp.bfloat16
@@ -96,8 +100,16 @@
     back_cols = wide(scale * to_freq(full).T)
     psf_rows = np.concatenate([np.concatenate([psf_rows[:N], psf_rows[:N]], axis=1),
                                np.concatenate([psf_rows[N:], np.zeros_like(psf_rows[N:])], axis=1)], axis=0)
-    return (patch_cols, patch_rows, psf_cols, psf_rows, pred_rows, pred_cols, res_cols, res_rows,
-            back_rows, back_cols)
+    tables = (patch_cols, patch_rows, psf_cols, psf_rows, pred_rows, pred_cols, res_cols, res_rows,
+              back_rows, back_cols)
+    places, at = [], 0
+    for table in tables:
+        places.append((at, table.shape[0]))
+        at += table.shape[0]
+    joined = np.zeros((at, 2 * N), ml_dtypes.bfloat16)
+    for (start, rows), table in zip(places, tables):
+        joined[start : start + rows, : table.shape[1]] = table
+    return joined, places
 
 
 def split(x):
@@ -125,8 +137,9 @@
 def left_three(table_ref, x):
     rows = table_ref.shape[0] // 2
     high, low = split(x)
-    both = dot(table_ref[...], high)
-    return both[:rows] + both[rows:] + dot(table_ref[:rows, :], low)
+    depth = x.shape[0]
+    both = dot(table_ref[:, :depth], high)
+    return both[:rows] + both[rows:] + dot(table_ref[:rows, :depth], low)
 
 
 def turned(y, sign):
@@ -309,6 +322,10 @@
     return pl.ds(pl.multiple_of(index * size, 8), size)
 
 
+def slot_rows(index, s):
+    return pl.ds(pl.multiple_of(index * (CAP * SLOT), 8) + s * SLOT, SLOT)
+
+
 def slot_chooser(packed_ref, dec, n_dec):
     row, column, first, second = own_places(packed_ref, dec)
     count = row.shape[1]
@@ -333,14 +350,20 @@
             out_ref[pl.ds(start + t, slots, stride=rows), :] = y[:, t * N : t * N + N]
 
 
-def photometry_kernel(n_ra, n_dec, meta_ref, packed_ref, psf_ref, obs_ref, var_ref, model_ref, *refs):
-    tables, refs = refs[:10], refs[10:]
+def photometry_kernel(n_ra, n_dec, places, meta_ref, packed_ref, *refs):
+    inputs, refs = refs[:5], refs[5:]
     (back_ref, residual_ref, ext_ref, to_right, to_left, from_left, from_right, corners, psf_out, psf_in,
      obs_slots, var_slots, pred_out, pred_in, resid_in, khat_ref, send, recv, send_psf, recv_psf,
-     send_pred, recv_pred, send_res, recv_res) = refs
+     send_pred, recv_pred, send_res, recv_res, psf_ref, obs_ref, var_ref, model_ref, joined, load) = refs
+    tables = [joined.at[pl.ds(start, rows), :] for start, rows in places]
+    loads = [pltpu.make_async_copy(src, dst, load.at[i]) for i, (src, dst) in enumerate(
+        zip(inputs, (psf_ref, obs_ref, var_ref, model_ref, joined)))]
+    for i in (3, 0, 1, 2, 4):
+        loads[i].start()
     ra, dec, up, down, right, left = neighbours(n_ra, n_dec)
     peers = [(ra, moved(dec, shift, n_dec, 1)) for _, shift in shifts()] + [(up, dec), (down, dec)]
     signal_all(peers)
+    loads[3].wait()
     tra, tdec = model_ref.shape[1], model_ref.shape[2]
     top = EDGE + tra
     low_half = lax.broadcasted_iota(jnp.int32, (1, N), 1) < 64
@@ -351,17 +374,22 @@
         to_left[q] = jnp.where(
             low_half, model_ref[2 * q, :, :N], pltpu.roll(model_ref[2 * q + 1, :, :N], 64, 1))
     wait_all(peers)
-    sides = [copy(0, to_right, from_left, (ra, right)), copy(1, to_left, from_right, (ra, left))]
+    ends = (slice(tra - EDGE, tra), slice(0, EDGE), slice(EDGE, tra - EDGE))
+    sides = []
+    for i, rows in enumerate(ends):
+        sides += [copy(2 * i, to_right.at[:, rows, :], from_left.at[:, rows, :], (ra, right)),
+                  copy(2 * i + 1, to_left.at[:, rows, :], from_right.at[:, rows, :], (ra, left))]
     for c in sides:
         c.start()
     copies = []
     for t in range(2):
         cols = slice(t * N, t * N + N)
-        copies += [copy(2 + t, model_ref.at[:, tra - EDGE :, cols], ext_ref.at[:, 1 + t, :EDGE, :], (up, dec)),
-                   copy(4 + t, model_ref.at[:, :EDGE, cols], ext_ref.at[:, 1 + t, top:, :], (down, dec))]
+        copies += [copy(6 + t, model_ref.at[:, tra - EDGE :, cols], ext_ref.at[:, 1 + t, :EDGE, :], (up, dec)),
+                   copy(8 + t, model_ref.at[:, :EDGE, cols], ext_ref.at[:, 1 + t, top:, :], (down, dec))]
     for c in copies:
         c.start()
     chosen = slot_chooser(packed_ref, dec, n_dec)
+    loads[0].wait()
     to_slots(chosen, psf_ref, psf_out, PSF_ROWS)
     moves = {}
     here = rows_of(dec, CAP * PSF_ROWS)
@@ -369,22 +397,34 @@
         tile = moved(dec, shift, n_dec, 1)
         moves[shift] = sender(send_psf, recv_psf)(
             d, psf_out.at[rows_of(tile, CAP * PSF_ROWS), :], psf_in.at[here, :], (ra, tile))
-        moves[shift].start()
+
+    def send_psfs(group):
+        for shift in group:
+            if shift in moves:
+                moves[shift].start()
+
+    send_psfs(PEERS[0])
     psf_in[here, :] = psf_out[here, :]
-    to_slots(chosen, obs_ref, obs_slots, PAD)
-    to_slots(chosen, var_ref, var_slots, PAD)
     for t in range(2):
         ext_ref[:, 1 + t, EDGE:top, :] = model_ref[:, :, t * N : t * N + N]
-    for c in sides:
+    loads[1].wait()
+    to_slots(chosen, obs_ref, obs_slots, SLOT)
+    more = []
+    for i in range(2):
+        for c in sides[2 * i : 2 * i + 2]:
+            c.wait_recv()
+        other = (up, dec) if i == 0 else (down, dec)
+        now = [copy(10 + i, from_left.at[:, ends[i], :], corners.at[i], other),
+               copy(12 + i, from_right.at[:, ends[i], :], corners.at[2 + i], other)]
+        for c in now:
+            c.start()
+        more += now
+    loads[2].wait()
+    to_slots(chosen, var_ref, var_slots, SLOT)
+    for c in sides[4:]:
         c.wait_recv()
-    more = [
-        copy(6, from_left.at[:, tra - EDGE :, :], corners.at[0], (up, dec)),
-        copy(7, from_left.at[:, :EDGE, :], corners.at[1], (down, dec)),
-        copy(8, from_right.at[:, tra - EDGE :, :], corners.at[2], (up, dec)),
-        copy(9, from_right.at[:, :EDGE, :], corners.at[3], (down, dec)),
-    ]
-    for c in more:
-        c.start()
+    for group in PEERS[1:]:
+        send_psfs(group)
     in_low, in_high, in_left, in_right = edges(n_ra, n_dec, ra, dec)
 
     def place(pieces):
@@ -413,20 +453,21 @@
     for c in sides:
         c.wait_send()
 
-    own = rows_of(dec, CAP * PAD)
+    own = rows_of(dec, CAP * SLOT)
     steps = len(PEERS)
     pred_moves, res_moves = {}, {}
     for d, shift in shifts():
         owner, tile = moved(dec, shift, n_dec, -1), moved(dec, shift, n_dec, 1)
         pred_moves[shift] = sender(send_pred, recv_pred)(
-            d, pred_out.at[rows_of(owner, CAP * PAD), :], pred_in.at[own, :], (ra, owner))
+            d, pred_out.at[rows_of(owner, CAP * SLOT), :], pred_in.at[own, :], (ra, owner))
         res_moves[shift] = sender(send_res, recv_res)(
-            d, residual_ref.at[rows_of(tile, CAP * PAD), :], resid_in.at[own, :], (ra, tile))
+            d, residual_ref.at[rows_of(tile, CAP * SLOT), :], resid_in.at[own, :], (ra, tile))
 
     def owned(j):
         return [(moved(dec, PEERS[j][e // CAP], n_dec, -1), e % CAP) for e in range(GROUP)]
 
-    for j in range(steps + 2):
+    loads[4].wait()
+    for j in range(steps + B_LAG):
         if j < steps:
             for shift in PEERS[j]:
                 if shift in moves:
@@ -438,13 +479,13 @@
                 tables[:6])
             for (o, s), k, f in zip(which, khat, flat):
                 khat_ref[o * CAP + s] = k
-                pred_out[rows_of(o * CAP + s, PAD), :] = f
+                pred_out[slot_rows(o, s), :] = f[:SLOT]
             for shift in PEERS[j]:
                 if shift in pred_moves:
                     pred_moves[shift].start()
         if 1 <= j <= steps:
             for shift in PEERS[j - 1]:
-                tile = rows_of(moved(dec, shift, n_dec, 1), CAP * PAD)
+                tile = rows_of(moved(dec, shift, n_dec, 1), CAP * SLOT)
                 if shift in pred_moves:
                     pred_moves[shift].wait_recv()
                     residual_ref[tile, :] = var_slots[tile, :] * (pred_in[tile, :] - obs_slots[tile, :])
@@ -453,13 +494,14 @@
                     resid = var_slots[own, :] * (pred_out[own, :] - obs_slots[own, :])
                     residual_ref[own, :] = resid
                     resid_in[own, :] = resid
-        if j >= 2:
-            for shift in PEERS[j - 2]:
+        if j >= B_LAG:
+            for shift in PEERS[j - B_LAG]:
                 if shift in res_moves:
                     res_moves[shift].wait_recv()
-            which = owned(j - 2)
+            which = owned(j - B_LAG)
             back = adjoint(
-                [resid_in[rows_of(o * CAP + s, PAD), :] for o, s in which],
+                [jnp.concatenate([resid_in[slot_rows(o, s), :], jnp.zeros((PAD - SLOT, N), F32)], axis=0)
+                 for o, s in which],
                 [khat_ref[o * CAP + s] for o, s in which], tables[6:])
             for (o, s), image in zip(which, back):
                 back_ref[o * CAP + s] = image
@@ -477,25 +519,27 @@
     bands, tra, tdec = model.shape
     strip = pltpu.VMEM((3, tra, N), F32)
     slots = n_dec * CAP
-    image, small = pltpu.VMEM((slots * PAD, N), F32), pltpu.VMEM((slots * PSF_ROWS, N), F32)
-    several, many = pltpu.SemaphoreType.DMA((10,)), pltpu.SemaphoreType.DMA((n_dec,))
-    tables = [jnp.asarray(t) for t in make_tables()]
+    image, small = pltpu.VMEM((slots * SLOT, N), F32), pltpu.VMEM((slots * PSF_ROWS, N), F32)
+    several, many = pltpu.SemaphoreType.DMA((14,)), pltpu.SemaphoreType.DMA((n_dec,))
+    joined, places = make_tables()
     return pl.pallas_call(
-        functools.partial(photometry_kernel, n_ra, n_dec),
+        functools.partial(photometry_kernel, n_ra, n_dec, places),
         out_shape=[
             jax.ShapeDtypeStruct((slots, N, N), F32),
-            jax.ShapeDtypeStruct((slots * PAD, N), F32),
+            jax.ShapeDtypeStruct((slots * SLOT, N), F32),
         ],
-        in_specs=[pl.BlockSpec(memory_space=pltpu.SMEM)] + vmem(5 + len(tables)),
+        in_specs=[pl.BlockSpec(memory_space=pltpu.SMEM)] + vmem(1) + [pl.BlockSpec(memory_space=pltpu.HBM)] * 5,
         out_specs=vmem(2),
         scratch_shapes=[pltpu.VMEM((bands, (tdec + 2 * SIDE) // N, tra + 2 * EDGE, N), F32),
                         strip, strip, strip, strip, pltpu.VMEM((4, 3, EDGE, N), F32), small, small,
                         image, image, image, image, image, pltpu.VMEM((slots, N, N), F32),
-                        several, several, many, many, many, many, many, many],
+                        several, several, many, many, many, many, many, many]
+        + [pltpu.VMEM(o.shape, o.dtype) for o in (psf, obs, var, model, joined)]
+        + [pltpu.SemaphoreType.DMA((5,))],
         compiler_params=pltpu.CompilerParams(
-            collective_id=0, has_side_effects=True, vmem_limit_bytes=LIMIT),
+            collective_id=0, has_side_effects=True, vmem_limit_bytes=MAIN_LIMIT),
         cost_estimate=pl.CostEstimate(flops=0, bytes_accessed=40_000_000, transcendentals=0),
-    )(meta, packed, psf, obs, var, model, *tables)
+    )(meta, packed, psf, obs, var, model, jnp.asarray(joined))
 
 
 def meta_kernel(packed_ref, meta_ref):
@@ -521,11 +565,11 @@
         chosen = (lax.broadcasted_iota(jnp.int32, (count, slots), 1) == place).astype(F32).astype(BF16)
         chosen = jnp.concatenate([chosen] * 3, axis=1)
         width = residual_ref.shape[1]
-        for start in range(0, PAD, 4):
+        for start in range(0, SLOT, 4):
             if start * N >= width:
                 break
             x = jnp.concatenate(
-                [slots_ref[pl.ds(start + t, slots, stride=PAD), :] for t in range(4)], axis=1)
+                [slots_ref[pl.ds(start + t, slots, stride=SLOT), :] for t in range(4)], axis=1)
             y = dot(chosen, three(x))
             end = min((start + 4) * N, width)
             residual_ref[:, start * N : end] = y[:, : end - start * N]
@@ -555,7 +599,7 @@
             out_specs=[whole(out), whole(wide)],
         ),
         out_shape=[jax.ShapeDtypeStruct(out, F32), jax.ShapeDtypeStruct(wide, F32)],
-        compiler_params=pltpu.CompilerParams(vmem_limit_bytes=LIMIT),
+        compiler_params=pltpu.CompilerParams(vmem_limit_bytes=SCATTER_LIMIT),
     )(meta, packed, residual, back)
 
 
@@ -650,7 +694,7 @@
         scratch_shapes=[strip, strip, strip, strip, corner, corner, band, band,
                         pltpu.SemaphoreType.DMA((12,)), pltpu.SemaphoreType.DMA((12,))],
         compiler_params=pltpu.CompilerParams(
-            collective_id=1, has_side_effects=True, vmem_limit_bytes=LIMIT),
+            collective_id=1, has_side_effects=True, vmem_limit_bytes=SMALL_LIMIT),
         cost_estimate=pl.CostEstimate(flops=0, bytes_accessed=40_000_000, transcendentals=0),
     )(acc)
 

time: 114 us -> 104 us (0.912); the launches traced: 114 us -> 102 us
  Pallas kernels: 108 us -> 94.8 us
  local copies, waits for them, and re-layouts: 3.41 us -> 5.28 us
    pallas_call x1, Pallas kernels: 76.9 us -> 67.2 us  [photometry(): pl.pallas_call(functools.partial(photometry_kernel, n_ra, n_dec, places),...]
    pallas_call x1, Pallas kernels: 8.2 us -> 3.89 us  [scatter(): pl.pallas_call(functools.partial(scatter_kernel, n_dec), grid_spec=pltpu....]
    unnamed x1 -> x9, local copies, waits for them, and re-layouts: 2.74 us -> 4.6 us
where the time goes in v6:
time: 104 us; the launch traced here: 102 us
  Pallas kernels  94.8 us (91%)
  local copies, waits for them, and re-layouts  5.28 us (5%)
  other arithmetic  1.41 us (1%)
    pallas_call x1, Pallas kernels, photometry(): pl.pallas_call(functools.partial(photometry_kernel, n_ra, n_dec, places),...  67.2 us
    pallas_call x1, Pallas kernels, fold(): pl.pallas_call(functools.partial(fold_kernel, n_ra, n_dec), out_shape=jax...  22.3 us
    unnamed x9, local copies, waits for them, and re-layouts  4.6 us
    pallas_call x1, Pallas kernels, scatter(): pl.pallas_call(functools.partial(scatter_kernel, n_dec), grid_spec=pltpu....  3.89 us

profile of v6, /device:TPU:1, one launch (start us, length us, event | category | flops | bytes accessed | tf_op | source)
XLA Modules:
  0.0 102.2 jit_solution(2905903736310825077)
XLA Ops:
  0.6 0.7 broadcast_multiply_fusion
  1.3 0.7 multiply_add_fusion
  2.0 0.7 reshape.9.packed_ref
  2.7 1.5 %shard_map.104.meta_ref = s32[16,4]{1,0:T(8,128)} custom-call(s32[16,32]{1,0:T(8,128)} %reshape.9.packed_ref), custom_call_target="tpu_custom_call" | custom-call | tf_op jit(solution)/shard_map/pallas_call | solution.py:550
  4.2 0.0 copy-start.2
  4.2 0.0 copy-start.3
  4.2 67.2 %shard_map.105 = (f32[64,128,128]{2,1,0:T(8,128)}, f32[2304,128]{1,0:T(8,128)}) custom-call(s32[16,4]{1,0:T(8,128)} %shard_map.104.meta_ref, s32[16,32]{1,0:T(8,128)} %reshape.9.packed_ref, f32[32,3969]{1,0:T(8,128)} %refs_0_.1, f32[32,4356]{1,0:T(8,128)} %refs_1_.1, f32[32,4356]{1,0:T(8,128)} %refs_2_.1, f32[6,256,256]{2,1,0:T(8,128)} %refs_3_.1, ...), custom_call_target="tpu_custom_call" | custom-call | bytes 40000000 | tf_op jit(solution)/shard_map/pallas_call | solution.py:525
  71.4 0.0 copy-done.2
  71.4 0.0 copy-done.3
  71.4 0.0 copy-start
  71.4 2.2 %copy-done = f32[64,128,128]{2,1,0:T(8,128)S(1)} copy-done((f32[64,128,128]{2,1,0:T(8,128)S(1)}, f32[64,128,128]{2,1,0:T(8,128)}, u32[]{:S(2)}) %copy-start) | copy-done | bytes 4194328
  73.6 0.0 copy-start.1
  73.6 1.3 %copy-done.1 = f32[2304,128]{1,0:T(8,128)S(1)} copy-done((f32[2304,128]{1,0:T(8,128)S(1)}, f32[2304,128]{1,0:T(8,128)}, u32[]{:S(2)}) %copy-start.1) | copy-done | bytes 1179672
  74.9 3.9 %shard_map.106 = (f32[32,4356]{1,0:T(8,128)}, f32[6,4,384,128]{3,2,1,0:T(8,128)S(1)}) custom-call(s32[16,4]{1,0:T(8,128)S(1)} %copy-done.3, s32[16,32]{1,0:T(8,128)S(1)} %copy-done.2, f32[2304,128]{1,0:T(8,128)S(1)} %copy-done.1, f32[64,128,128]{2,1,0:T(8,128)S(1)} %copy-done), custom_call_target="tpu_custom_call" | custom-call | tf_op jit(solution)/shard_map/pallas_call | solution.py:593
  78.8 22.3 %shard_map.107 = f32[6,256,256]{2,1,0:T(8,128)S(1)} custom-call(f32[6,4,384,128]{3,2,1,0:T(8,128)S(1)} %get-tuple-element.9.acc_ref), custom_call_target="tpu_custom_call" | custom-call | bytes 40000000 | tf_op jit(solution)/shard_map/pallas_call | solution.py:689
  101.0 1.1 %copy.12 = f32[6,256,256]{2,1,0:T(8,128)} copy(f32[6,256,256]{2,1,0:T(8,128)S(1)} %shard_map.107) | data formatting | bytes 3145728
Async XLA Ops:
  4.2 67.2 %copy-start.2 = (s32[16,32]{1,0:T(8,128)S(1)}, s32[16,32]{1,0:T(8,128)}, u32[]{:S(2)}) copy-start(s32[16,32]{1,0:T(8,128)} %reshape.9.packed_ref) | copy-start | bytes 6148
  4.2 67.2 %copy-start.3 = (s32[16,4]{1,0:T(8,128)S(1)}, s32[16,4]{1,0:T(8,128)}, u32[]{:S(2)}) copy-start(s32[16,4]{1,0:T(8,128)} %shard_map.104.meta_ref) | copy-start | bytes 772
  71.4 2.2 %copy-start = (f32[64,128,128]{2,1,0:T(8,128)S(1)}, f32[64,128,128]{2,1,0:T(8,128)}, u32[]{:S(2)}) copy-start(f32[64,128,128]{2,1,0:T(8,128)} %get-tuple-element.7.back_ref) | copy-start | bytes 12582916
  73.6 1.3 %copy-start.1 = (f32[2304,128]{1,0:T(8,128)S(1)}, f32[2304,128]{1,0:T(8,128)}, u32[]{:S(2)}) copy-start(f32[2304,128]{1,0:T(8,128)} %get-tuple-element.6.slots_ref) | copy-start | bytes 3538948

commit v7 on v6

--- a/solution.py
+++ b/solution.py
@@ -419,11 +419,12 @@
         for c in now:
             c.start()
         more += now
+    send_psfs(PEERS[1])
     loads[2].wait()
     to_slots(chosen, var_ref, var_slots, SLOT)
     for c in sides[4:]:
         c.wait_recv()
-    for group in PEERS[1:]:
+    for group in PEERS[2:]:
         send_psfs(group)
     in_low, in_high, in_left, in_right = edges(n_ra, n_dec, ra, dec)
 

time: 104 us -> 100 us (0.962); the launches traced: 102 us -> 99.7 us
  Pallas kernels: 94.8 us -> 92.3 us
    pallas_call x1, Pallas kernels: 22.3 us -> 16.9 us  [fold(): pl.pallas_call(functools.partial(fold_kernel, n_ra, n_dec), out_shape=jax...]
    pallas_call x1, Pallas kernels: 67.2 us -> 70 us  [photometry(): pl.pallas_call(functools.partial(photometry_kernel, n_ra, n_dec, places),...]
where the time goes in v7:
time: 100 us; the launch traced here: 99.7 us
  Pallas kernels  92.3 us (92%)
  local copies, waits for them, and re-layouts  5.28 us (5%)
  other arithmetic  1.41 us (1%)
    pallas_call x1, Pallas kernels, photometry(): pl.pallas_call(functools.partial(photometry_kernel, n_ra, n_dec, places),...  70 us
    pallas_call x1, Pallas kernels, fold(): pl.pallas_call(functools.partial(fold_kernel, n_ra, n_dec), out_shape=jax...  16.9 us
    unnamed x9, local copies, waits for them, and re-layouts  4.6 us
    pallas_call x1, Pallas kernels, scatter(): pl.pallas_call(functools.partial(scatter_kernel, n_dec), grid_spec=pltpu....  3.89 us

profile of v7, /device:TPU:1, one launch (start us, length us, event | category | flops | bytes accessed | tf_op | source)
XLA Modules:
  0.0 99.7 jit_solution(3251940209656739567)
XLA Ops:
  0.6 0.7 broadcast_multiply_fusion
  1.3 0.7 multiply_add_fusion
  2.0 0.7 reshape.9.packed_ref
  2.7 1.5 %shard_map.104.meta_ref = s32[16,4]{1,0:T(8,128)} custom-call(s32[16,32]{1,0:T(8,128)} %reshape.9.packed_ref), custom_call_target="tpu_custom_call" | custom-call | tf_op jit(solution)/shard_map/pallas_call | solution.py:551
  4.2 0.0 copy-start.2
  4.2 0.0 copy-start.3
  4.2 70.0 %shard_map.105 = (f32[64,128,128]{2,1,0:T(8,128)}, f32[2304,128]{1,0:T(8,128)}) custom-call(s32[16,4]{1,0:T(8,128)} %shard_map.104.meta_ref, s32[16,32]{1,0:T(8,128)} %reshape.9.packed_ref, f32[32,3969]{1,0:T(8,128)} %refs_0_.1, f32[32,4356]{1,0:T(8,128)} %refs_1_.1, f32[32,4356]{1,0:T(8,128)} %refs_2_.1, f32[6,256,256]{2,1,0:T(8,128)} %refs_3_.1, ...), custom_call_target="tpu_custom_call" | custom-call | bytes 40000000 | tf_op jit(solution)/shard_map/pallas_call | solution.py:526
  74.2 0.0 copy-done.2
  74.2 0.0 copy-done.3
  74.3 0.0 copy-start
  74.3 2.2 %copy-done = f32[64,128,128]{2,1,0:T(8,128)S(1)} copy-done((f32[64,128,128]{2,1,0:T(8,128)S(1)}, f32[64,128,128]{2,1,0:T(8,128)}, u32[]{:S(2)}) %copy-start) | copy-done | bytes 4194328
  76.4 0.0 copy-start.1
  76.4 1.3 %copy-done.1 = f32[2304,128]{1,0:T(8,128)S(1)} copy-done((f32[2304,128]{1,0:T(8,128)S(1)}, f32[2304,128]{1,0:T(8,128)}, u32[]{:S(2)}) %copy-start.1) | copy-done | bytes 1179672
  77.7 3.9 %shard_map.106 = (f32[32,4356]{1,0:T(8,128)}, f32[6,4,384,128]{3,2,1,0:T(8,128)S(1)}) custom-call(s32[16,4]{1,0:T(8,128)S(1)} %copy-done.3, s32[16,32]{1,0:T(8,128)S(1)} %copy-done.2, f32[2304,128]{1,0:T(8,128)S(1)} %copy-done.1, f32[64,128,128]{2,1,0:T(8,128)S(1)} %copy-done), custom_call_target="tpu_custom_call" | custom-call | tf_op jit(solution)/shard_map/pallas_call | solution.py:594
  81.6 16.9 %shard_map.107 = f32[6,256,256]{2,1,0:T(8,128)S(1)} custom-call(f32[6,4,384,128]{3,2,1,0:T(8,128)S(1)} %get-tuple-element.9.acc_ref), custom_call_target="tpu_custom_call" | custom-call | bytes 40000000 | tf_op jit(solution)/shard_map/pallas_call | solution.py:690
  98.5 1.1 %copy.12 = f32[6,256,256]{2,1,0:T(8,128)} copy(f32[6,256,256]{2,1,0:T(8,128)S(1)} %shard_map.107) | data formatting | bytes 3145728
Async XLA Ops:
  4.2 70.0 %copy-start.2 = (s32[16,32]{1,0:T(8,128)S(1)}, s32[16,32]{1,0:T(8,128)}, u32[]{:S(2)}) copy-start(s32[16,32]{1,0:T(8,128)} %reshape.9.packed_ref) | copy-start | bytes 6148
  4.2 70.0 %copy-start.3 = (s32[16,4]{1,0:T(8,128)S(1)}, s32[16,4]{1,0:T(8,128)}, u32[]{:S(2)}) copy-start(s32[16,4]{1,0:T(8,128)} %shard_map.104.meta_ref) | copy-start | bytes 772
  74.3 2.2 %copy-start = (f32[64,128,128]{2,1,0:T(8,128)S(1)}, f32[64,128,128]{2,1,0:T(8,128)}, u32[]{:S(2)}) copy-start(f32[64,128,128]{2,1,0:T(8,128)} %get-tuple-element.7.back_ref) | copy-start | bytes 12582916
  76.4 1.3 %copy-start.1 = (f32[2304,128]{1,0:T(8,128)S(1)}, f32[2304,128]{1,0:T(8,128)}, u32[]{:S(2)}) copy-start(f32[2304,128]{1,0:T(8,128)} %get-tuple-element.6.slots_ref) | copy-start | bytes 3538948
